TPU v7x, 512 devices: a whole 4x8x8 slice. The times are simulated.
512 devices in a mesh: bank: 64 (over z, y_lo, core), dp: 8 (over y_hi, x).
Axes of the slice: x: 4, y: 8 (y_hi: 2, y_lo: 4; y = y_hi * 4 + y_lo), z: 8, core: 2. Of those that a mesh axis runs over, the one named last changes fastest.
Arguments:
- queries: bfloat16 [131072, 1024], P(('bank', 'dp')), may hold values from -6 to 6
- w_input: bfloat16 [1024, 1024], P('dp'), may hold values from -0.1875 to 0.1875
- w_output: bfloat16 [1024, 256], P('dp'), may hold values from -0.1875 to 0.1875
- item_bank: bfloat16 [8192, 256], P('bank'), may hold values from -6 to 6
- positives: int32 [131072], P(('bank', 'dp')), may hold values from 0 to 8191
- fresh_rows: bfloat16 [4096, 256], P('bank'), may hold values from -6 to 6
- owners: int32 [4096, 1], P('bank'), may hold values from 0 to 63; in each aligned block of 64 rows (0 to 63, 64 to 127, ...) at most 2 rows name the same one
- slots: int32 [4096], P('bank'), may hold values from 0 to 127
Outputs:
- contrast_loss: float32 [131072], P(('bank', 'dp'))
- next_bank: bfloat16 [8192, 256], P('bank')
Inputs may be any that keep to these rules, and one draw needn't show every extreme that they name: `owners`: among the 64 rows of one index of bank, at most 2 name the same owner; some owner is named by exactly 2 of them.
All inputs are finite; a program needn't handle non-finite values.
Results may differ from a plain program's by a relative error of at most 0.0022.
Values may be sent and summed in bfloat16 or wider, within the bound.
No kernel may reach another device: no remote copies, remote signals or barrier semaphores. Data moves between devices by JAX's collectives and lax.ppermute only.
A program may use at most 64 MiB of HBM per device.

v0:
```python
import jax
import jax.numpy as jnp
from jax import lax
from jax.sharding import PartitionSpec as P


def body(queries, w_input, w_output, item_bank, positives, fresh_rows, owners, slots):
    query_count = queries.shape[0]
    columns = queries
    preact = jnp.dot(
        columns,
        lax.all_gather(w_input, "dp", axis=0, tiled=True),
        preferred_element_type=jnp.float32,
    )
    hidden = jax.nn.silu(preact).astype(jnp.bfloat16)
    columns = hidden
    embedding = jnp.dot(
        columns,
        lax.all_gather(w_output, "dp", axis=0, tiled=True),
        preferred_element_type=jnp.float32,
    )
    unit_query = (
        embedding * lax.rsqrt(jnp.sum(embedding * embedding, axis=1, keepdims=True) + 1e-06)
    ).astype(jnp.bfloat16)
    bank_count = lax.axis_size("bank")
    block_rows = lax.all_gather(item_bank, "bank", axis=0, tiled=True)
    running_max = jnp.full((query_count,), -1e30, jnp.float32)
    logits = 16.0 * lax.dot_general(
        unit_query, block_rows, (((1,), (1,)), ((), ())), preferred_element_type=jnp.float32
    )
    columns = jnp.arange(block_rows.shape[0], dtype=jnp.int32)
    new_max = jnp.maximum(running_max, jnp.max(logits, axis=1))
    new_sum = jnp.sum(jnp.exp(logits - new_max[:, None]), axis=1)
    hits = columns[None, :] == positives[:, None]
    new_picked = jnp.sum(jnp.where(hits, logits, 0.0), axis=1)
    contrast_loss = jnp.log(new_sum) + new_max - new_picked
    myself = lax.axis_index("bank")
    fresh_count = fresh_rows.shape[0]
    capacity = max(2, 2 * fresh_count // bank_count)
    global_index = myself * fresh_count + jnp.arange(fresh_count, dtype=jnp.int32)
    owner_dev = owners[:, 0]
    onehot = (owner_dev[:, None] == jnp.arange(bank_count, dtype=jnp.int32)[None, :]).astype(
        jnp.int32
    )
    before = jnp.cumsum(onehot, axis=0) - onehot
    placed = jnp.sum(before * onehot, axis=1)
    target = owner_dev * capacity + placed
    outbox_rows = (
        jnp.zeros((bank_count * capacity, fresh_rows.shape[1]), jnp.bfloat16)
        .at[target]
        .set(fresh_rows)
    )
    outbox_index = jnp.full((bank_count * capacity,), -1, jnp.int32).at[target].set(global_index)
    outbox_slot = jnp.zeros((bank_count * capacity,), jnp.int32).at[target].set(slots)
    got_rows, got_index, got_slot = (
        lax.all_to_all(outbox_rows, "bank", split_axis=0, concat_axis=0, tiled=True),
        lax.all_to_all(outbox_index, "bank", split_axis=0, concat_axis=0, tiled=True),
        lax.all_to_all(outbox_slot, "bank", split_axis=0, concat_axis=0, tiled=True),
    )
    bank_rows = item_bank.shape[0]
    winner = jnp.full((bank_rows,), -1, jnp.int32).at[got_slot].max(got_index)
    selector = ((got_index[None, :] == winner[:, None]) & (winner[:, None] >= 0)).astype(
        jnp.bfloat16
    )
    written = jnp.dot(selector, got_rows, preferred_element_type=jnp.float32)
    next_bank = jnp.where(winner[:, None] >= 0, written, item_bank.astype(jnp.float32)).astype(
        jnp.bfloat16
    )
    return (contrast_loss, next_bank)


def solution(mesh):
    return jax.shard_map(
        body,
        mesh=mesh,
        in_specs=(
            P(("bank", "dp"), None),
            P("dp", None),
            P("dp", None),
            P("bank", None),
            P(("bank", "dp")),
            P("bank", None),
            P("bank", None),
            P("bank"),
        ),
        out_specs=(P(("bank", "dp")), P("bank", None)),
        check_vma=False,
    )
```

profile of v0, /device:TPU:1, one launch (start us, length us, event | category | flops | bytes accessed | tf_op | source)
XLA Modules:
  0.0 235.1 jit_solution(16751140565871064266)
XLA Ops:
  7.2 0.7 all-gather.3.cloned.1.call-update
  8.0 0.7 all-gather.5.cloned.1.call-update
  8.7 0.7 fusion.8
  9.5 0.8 select_reduce_fusion.1
  10.3 0.7 fusion.11
  11.0 0.9 scatter_custom_fusion
  11.9 0.8 all_to_all.24
  12.7 15.4 %all-to-all-start = ((s32[64,2,1]{1,2,0:T(1,128)}), s32[64,2,1]{1,2,0:T(1,128)S(1)}, u32[]{:S(2)}, u32[]{:S(2)}) async-start(s32[64,2,1]{1,2,0:T(1,128)} %bitcast.3), calls=%async_computation | async-start | bytes 65536 | tf_op jit(solution)/shard_map/all_to_all | solution.py:58
  28.1 0.8 scatter_custom_fusion.1
  28.9 0.7 all_to_all.27
  29.6 8.0 %all-to-all-done = s32[64,2,1]{1,2,0:T(1,128)S(1)} async-done(((s32[64,2,1]{1,2,0:T(1,128)}), s32[64,2,1]{1,2,0:T(1,128)S(1)}, u32[]{:S(2)}, u32[]{:S(2)}) %all-to-all-start) | async-done | bytes 544 | tf_op jit(solution)/shard_map/all_to_all | solution.py:58
  37.6 4.6 %all-to-all-start.1 = ((s32[64,2,1]{1,2,0:T(1,128)}), s32[64,2,1]{1,2,0:T(1,128)S(1)}, u32[]{:S(2)}, u32[]{:S(2)}) async-start(s32[64,2,1]{1,2,0:T(1,128)} %bitcast.5), calls=%async_computation.1 | async-start | bytes 65536 | tf_op jit(solution)/shard_map/all_to_all | solution.py:57
  42.3 42.6 %all_gather.10 = bf16[1024,256]{1,0:T(8,128)(2,1)S(1)} all-gather(bf16[128,256]{1,0:T(8,128)(2,1)} %param.10), channel_id=1, replica_groups=mesh['bank'=64,'dp'=8] {'dp'}, dimensions={0}, use_global_device_ids=true | all-gather | bytes 589824 | tf_op jit(solution)/shard_map/all_gather | solution.py:19
  84.9 1.1 scatter_custom_fusion.3
  87.1 0.7 reduce.6
  88.0 19.4 %all-to-all-start.2 = ((bf16[64,2,256]{2,1,0:T(2,128)(2,1)}), bf16[64,2,256]{2,1,0:T(2,128)(2,1)S(1)}, u32[]{:S(2)}, u32[]{:S(2)}) async-start(bf16[64,2,256]{2,1,0:T(2,128)(2,1)} %all_to_all.30), calls=%async_computation.2 | async-start | bytes 131072 | tf_op jit(solution)/shard_map/all_to_all | solution.py:56
  107.4 0.7 reduce.7
  108.3 1.4 scatter_custom_fusion.2
  109.7 7.7 %all-to-all-done.2 = bf16[64,2,256]{2,1,0:T(2,128)(2,1)S(1)} async-done(((bf16[64,2,256]{2,1,0:T(2,128)(2,1)}), bf16[64,2,256]{2,1,0:T(2,128)(2,1)S(1)}, u32[]{:S(2)}, u32[]{:S(2)}) %all-to-all-start.2) | async-done | bytes 65568 | tf_op jit(solution)/shard_map/all_to_all | solution.py:56
  117.5 1.7 fusion
  119.2 2.7 %multiply_reduce_fusion = (f32[256]{0:T(256)S(1)}, f32[256,256]{0,1:T(8,128)S(1)}) fusion(bf16[1024,256]{1,0:T(8,128)(2,1)S(1)} %all_gather.10, bf16[256,1024]{1,0:T(8,128)(2,1)S(1)} %copy-done, bf16[1024,1024]{1,0:T(8,128)(2,1)} %all-gather.3.cloned.1.call-done), kind=kOutput, calls=%fused_computation.13 | convolution fusion | flops 672530176 | bytes 3408896 | tf_op jit(solution)/shard_map/dot_general | solution.py:17
  121.9 99.7 %all-gather.5.cloned.1.call-done = bf16[8192,256]{1,0:T(8,128)(2,1)} async-done(((bf16[128,256]{1,0:T(8,128)(2,1)}), bf16[8192,256]{1,0:T(8,128)(2,1)}) %all-gather.5.cloned.1.call-update) | async-done | bytes 4194320 | tf_op jit(solution)/shard_map/all_gather | solution.py:26
  221.6 3.6 %fusion.20 = (f32[256]{0:T(256)S(1)}, f32[256,8192]{1,0:T(8,128)S(1)}) fusion(bf16[8192,256]{1,0:T(8,128)(2,1)} %all-gather.5.cloned.1.call-done, f32[256,256]{0,1:T(8,128)S(1)} %get-tuple-element.5, f32[256]{0:T(256)S(1)} %add_rsqrt_fusion), kind=kOutput, calls=%fused_computation.42 | convolution fusion | flops 1078066944 | bytes 12847104 | tf_op jit(solution)/shard_map/dot_general | solution.py:28
  225.1 2.5 %exponential_reduce_fusion = (f32[256]{0:T(256)S(1)}, f32[256]{0:T(256)S(1)}) fusion(f32[256,8192]{1,0:T(8,128)S(1)} %get-tuple-element.7, f32[256]{0:T(256)S(1)} %broadcast_maximum_fusion, s32[256]{0:T(256)S(1)} %copy-done.1), kind=kLoop, calls=%fused_computation.7 | loop fusion | flops 10485248 | bytes 8392704 | tf_op jit(solution)/shard_map/reduce_sum | solution.py:33
  (20 shorter events, 2.3 us)
Async XLA Ops:
  7.2 112.0 %copy-start = (bf16[256,1024]{1,0:T(8,128)(2,1)S(1)}, bf16[256,1024]{1,0:T(8,128)(2,1)}, u32[]{:S(2)}) copy-start(bf16[256,1024]{1,0:T(8,128)(2,1)} %param.8) | copy-start | bytes 1572868
  7.2 112.0 %all-gather.3.cloned.1.call-start = ((), (), s32[]{:S(2)}) async-start(), calls=%async_computation.3 | async-start | bytes 2359296 | tf_op jit(solution)/shard_map/all_gather | solution.py:12
  7.9 213.6 %all-gather.5.cloned.1.call-start = ((), (), s32[]{:S(2)}) async-start(), calls=%async_computation.4 | async-start | bytes 4259840 | tf_op jit(solution)/shard_map/all_gather | solution.py:26
  12.7 24.9 %all-to-all-start = ((s32[64,2,1]{1,2,0:T(1,128)}), s32[64,2,1]{1,2,0:T(1,128)S(1)}, u32[]{:S(2)}, u32[]{:S(2)}) async-start(s32[64,2,1]{1,2,0:T(1,128)} %bitcast.3), calls=%async_computation | async-start | bytes 65536 | tf_op jit(solution)/shard_map/all_to_all | solution.py:58
  37.6 50.4 %all-to-all-start.1 = ((s32[64,2,1]{1,2,0:T(1,128)}), s32[64,2,1]{1,2,0:T(1,128)S(1)}, u32[]{:S(2)}, u32[]{:S(2)}) async-start(s32[64,2,1]{1,2,0:T(1,128)} %bitcast.5), calls=%async_computation.1 | async-start | bytes 65536 | tf_op jit(solution)/shard_map/all_to_all | solution.py:57
  88.0 29.4 %all-to-all-start.2 = ((bf16[64,2,256]{2,1,0:T(2,128)(2,1)}), bf16[64,2,256]{2,1,0:T(2,128)(2,1)S(1)}, u32[]{:S(2)}, u32[]{:S(2)}) async-start(bf16[64,2,256]{2,1,0:T(2,128)(2,1)} %all_to_all.30), calls=%async_computation.2 | async-start | bytes 131072 | tf_op jit(solution)/shard_map/all_to_all | solution.py:56
  121.9 103.3 %copy-start.1 = (s32[256]{0:T(256)S(1)}, s32[256]{0:T(256)}, u32[]{:S(2)}) copy-start(s32[256]{0:T(256)} %param.12) | copy-start | bytes 3076
Sparse Core Ops, SparseCore 0:
  11.2 84.3 all-gather.2
  97.7 123.7 all-gather.4
where the time goes:
time: 236 us; the launch traced here: 235 us
  waiting for transfers between devices  117 us (50%)
  blocking collectives  42.6 us (18%)
  starting transfers between devices  39.5 us (17%)
  between operations  14.2 us (6%)
  other arithmetic  8.34 us (4%)
  matrix products  7.95 us (3%)
  local copies, waits for them, and re-layouts  5.72 us (2%)
    all_gather x1, waiting for transfers between devices, body(): block_rows = lax.all_gather(item_bank, 'bank', axis=0, tiled=True)  99.7 us
    all_gather x1, blocking collectives, body(): lax.all_gather(w_output, 'dp', axis=0, tiled=True)  42.6 us
    all_to_all x1, starting transfers between devices, body(): lax.all_to_all(outbox_rows, 'bank', split_axis=0, concat_axis=0, tiled=True)  19.4 us
    all_to_all x1, starting transfers between devices, body(): lax.all_to_all(outbox_slot, 'bank', split_axis=0, concat_axis=0, tiled=True)  15.4 us
    all_to_all x1, waiting for transfers between devices, body(): lax.all_to_all(outbox_slot, 'bank', split_axis=0, concat_axis=0, tiled=True)  7.99 us
    all_to_all x1, waiting for transfers between devices, body(): lax.all_to_all(outbox_rows, 'bank', split_axis=0, concat_axis=0, tiled=True)  7.71 us
  transfers between devices with their start and end apart: 5, of which 3 were waited for; matrix products, arithmetic and copies ran while one was open for 6% of the time, Pallas kernels for 0%

commit v1 on v0

v1 whole, which is shorter than its diff:
```python
import functools
import math

import jax
import jax.numpy as jnp
from jax import lax
from jax.experimental import pallas as pl
from jax.experimental.pallas import tpu as pltpu
from jax.sharding import PartitionSpec as P

BF16 = jnp.bfloat16
F32 = jnp.float32
I32 = jnp.int32

CORES = 2
X = 4

VMEM = pltpu.VMEM
LIMIT = 48 * 1024 * 1024


def core_index():
    return lax.rem(lax.axis_index("bank"), CORES)


def x_index():
    return lax.rem(lax.axis_index("dp"), X)


def call(kernel, outs, args, scratch=()):
    return pl.pallas_call(
        kernel,
        out_shape=outs,
        in_specs=[pl.BlockSpec(memory_space=VMEM)] * len(args),
        out_specs=jax.tree.map(lambda _: pl.BlockSpec(memory_space=VMEM), outs),
        scratch_shapes=list(scratch),
        compiler_params=pltpu.CompilerParams(vmem_limit_bytes=LIMIT),
    )(*args)


def weights_kernel(w_input, w_output, out):
    half = w_input.shape[1] // CORES
    out_half = w_output.shape[1] // CORES
    rows = w_input.shape[0]
    core = core_index()
    first = w_input[:, pl.ds(pl.multiple_of(core * half, half), half)]
    second = w_output[:, pl.ds(pl.multiple_of(core * out_half, out_half), out_half)]
    pieces = half // out_half
    tall = rows // pieces
    for d in range(out.shape[0]):
        out[d, :rows, :] = first
        for i in range(pieces):
            out[d, rows:, i * out_half : (i + 1) * out_half] = second[i * tall : (i + 1) * tall, :]


def outbox_kernel(owners, slots, fresh, bank, out):
    part = bank.shape[0] // X
    x = x_index()
    own = bank[pl.ds(pl.multiple_of(x * part, part), part), :]
    chips = out.shape[0]
    for k in range(chips):
        out[k, :part, :] = own
    count = fresh.shape[0]
    owner = owners[...].astype(F32)
    across = jnp.broadcast_to(owner, (count, count))
    earlier = lax.broadcasted_iota(I32, (count, count), 0) < lax.broadcasted_iota(I32, (count, count), 1)
    same = across == across.T
    placed = jnp.sum(jnp.where(same & earlier, 1.0, 0.0), axis=0, keepdims=True)
    key = (owner * 2.0 + placed).astype(I32)
    row = lax.broadcasted_iota(I32, (chips * 8, count), 0)
    wanted = (row // 8) * 4 + (row % 4)
    chosen = wanted == key
    data = jnp.dot(chosen.astype(BF16), fresh[...], preferred_element_type=F32)
    slot = jnp.sum(jnp.where(chosen, slots[...].astype(F32) + 1.0, 0.0), axis=1, keepdims=True) - 1.0
    kind = lax.broadcasted_iota(I32, data.shape, 0) % 8
    both = jnp.where(kind < 4, data, slot).astype(BF16)
    out[:, part:, :] = both.reshape(chips, 8, both.shape[1])


def tower_kernel(queries, w_own, w_other, positives, out, hidden, w_last, unit):
    core = core_index()
    members, tall, half = w_own.shape
    rows = queries.shape[1] // members
    out_half = w_last.shape[1] // CORES
    pieces = half // out_half
    step = tall - rows
    q = queries[...]
    for which, w in ((core, w_own), (1 - core, w_other)):
        first = w[:, :rows, :].reshape(members * rows, half)
        v = jnp.dot(q, first, preferred_element_type=F32)
        v = (0.5 * v) * (1.0 + jnp.tanh(0.5 * v))
        hidden[:, pl.ds(pl.multiple_of(which * half, half), half)] = v.astype(BF16)
        at = pl.ds(pl.multiple_of(which * out_half, out_half), out_half)
        for d in range(members):
            for i in range(pieces):
                w_last[pl.ds(d * rows + i * step, step), at] = w[
                    d, rows:, i * out_half : (i + 1) * out_half
                ]
    embedding = jnp.dot(hidden[...], w_last[...], preferred_element_type=F32)
    norm = lax.rsqrt(jnp.sum(embedding * embedding, axis=1, keepdims=True) + 1e-06)
    unit[...] = (embedding * norm).astype(BF16)
    count = queries.shape[0]
    high = (positives[...] // 128).astype(F32)
    low = (positives[...] % 128).astype(F32)
    line = lax.broadcasted_iota(I32, (out.shape[1] - count, count), 0)
    tail = jnp.where(line == 0, high, jnp.where(line == 1, low, 0.0)).astype(BF16)
    for k in range(out.shape[0]):
        out[k, :count, :] = unit[...]
        out[k, count:, :] = tail


def scores_kernel(shared, box_own, box_other, out):
    core = core_index()
    x = x_index()
    chips = box_own.shape[0]
    part = box_own.shape[1] - 8
    local = chips * part
    count = out.shape[2]
    scale = 16.0 * math.log2(math.e)
    number = lax.broadcasted_iota(I32, (local, count), 0)
    banks = [b[:, :part, :].reshape(local, b.shape[2]) for b in (box_own, box_other)]
    for k in range(shared.shape[0]):
        query = shared[k, :count, :]
        tail = shared[k, count : count + 16, :].astype(F32)
        high, low = tail[0:1, :].astype(I32), tail[1:2, :].astype(I32)
        dots = [
            lax.dot_general(b, query, (((1,), (1,)), ((), ())), preferred_element_type=F32) for b in banks
        ]
        top = jnp.maximum(*[jnp.max(d, axis=0, keepdims=True) for d in dots])
        total = jnp.zeros_like(top)
        picked = jnp.zeros_like(top)
        for d, which in zip(dots, (core, 1 - core)):
            total += jnp.sum(jnp.exp2((d - top) * scale), axis=0, keepdims=True)
            mine = (high % CORES == which) & (low // part == x)
            at = jnp.where(mine, (high // CORES) * part + low % part, -1)
            picked += jnp.sum(jnp.where(number == at, d, 0.0), axis=0, keepdims=True)
        line = lax.broadcasted_iota(I32, (out.shape[1], count), 0)
        out[k, :, :] = jnp.where(
            line == 0, 16.0 * top, jnp.where(line == 1, total, jnp.where(line == 2, 16.0 * picked, 0.0))
        )


def loss_kernel(parts, out):
    top = jnp.max(parts[:, 0, :], axis=0, keepdims=True)
    total = jnp.sum(parts[:, 1, :] * jnp.exp(parts[:, 0, :] - top), axis=0, keepdims=True)
    out[...] = jnp.log(total) + top - jnp.sum(parts[:, 2, :], axis=0, keepdims=True)


def bank_kernel(box_own, box_other, bank, out):
    core = core_index()
    chips = box_own.shape[0]
    part = box_own.shape[1] - 8
    count = bank.shape[0]
    line = lax.broadcasted_iota(I32, (chips * 8, count), 0)
    kind = line % 8
    mine = (kind < 4) & ((kind // 2) == core)
    place = lax.broadcasted_iota(I32, (chips * 8, count), 1).astype(F32)
    keys, rows = [], []
    for box, source in ((box_own, core), (box_other, 1 - core)):
        block = box[:, part:, :].astype(F32)
        moved = jnp.concatenate([block[:, 4:, :], block[:, :4, :]], axis=1)
        slot = moved.reshape(chips * 8, block.shape[2])[:, :count]
        order = (line // 8) * 4 + source * 2 + kind % 2
        keys.append(jnp.where(mine & (slot == place), order, -1))
        rows.append(box[:, part:, :].reshape(chips * 8, block.shape[2]))
    winner = jnp.maximum(*[jnp.max(k, axis=0, keepdims=True) for k in keys])
    written = jnp.zeros(bank.shape, F32)
    found = jnp.zeros((count, 128), F32)
    for key, row in zip(keys, rows):
        chosen = jnp.where((key == winner) & (key >= 0), 1.0, 0.0).astype(BF16)
        contract = (((0,), (0,)), ((), ()))
        written += lax.dot_general(chosen, row, contract, preferred_element_type=F32)
        ones = jnp.ones((chips * 8, 128), BF16)
        found += lax.dot_general(chosen, ones, contract, preferred_element_type=F32)
    out[...] = jnp.where(found[:, :1] > 0.5, written, bank[...].astype(F32)).astype(BF16)


def body(queries, w_input, w_output, item_bank, positives, fresh_rows, owners, slots):
    sds = jax.ShapeDtypeStruct
    count = queries.shape[0]
    members = lax.axis_size("dp")
    chips = lax.axis_size("bank") // CORES
    part = item_bank.shape[0] // X
    width = item_bank.shape[1]
    half = w_input.shape[1] // CORES
    extra = w_output.size // CORES // half

    planes = [[k * CORES + c for k in range(chips)] for c in range(CORES)]
    rings = [[r * X + i for i in range(X)] for r in range(members // X)]
    swap = [(i, i ^ 1) for i in range(chips * CORES)]

    def exchange(a, axis, groups=None):
        return lax.all_to_all(a, axis, 0, 0, axis_index_groups=groups, tiled=True)

    w_send = call(
        weights_kernel, sds((members, w_input.shape[0] + extra, half), BF16), (w_input, w_output)
    )
    w_own = exchange(w_send, "dp")
    box_send = call(
        outbox_kernel,
        sds((chips, part + 8, width), BF16),
        (owners.reshape(1, -1), slots.reshape(1, -1), fresh_rows, item_bank),
    )
    box_send, w_own = lax.optimization_barrier((box_send, w_own))
    w_other = lax.ppermute(w_own, "bank", swap)
    box_own = exchange(box_send, "bank", planes)
    shared = call(
        tower_kernel,
        sds((X, count + 16, width), BF16),
        (queries, w_own, w_other, positives.reshape(1, -1)),
        [
            VMEM((count, w_input.shape[1]), BF16),
            VMEM((members * w_output.shape[0], width), BF16),
            VMEM((count, width), BF16),
        ],
    )
    box_own, shared = lax.optimization_barrier((box_own, shared))
    box_other = lax.ppermute(box_own, "bank", swap)
    shared = exchange(shared, "dp", rings)
    parts = call(scores_kernel, sds((X, 8, count), F32), (shared, box_own, box_other))
    parts = exchange(parts, "dp", rings)
    contrast_loss = call(loss_kernel, sds((1, count), F32), (parts,)).reshape(count)
    next_bank = call(bank_kernel, sds(item_bank.shape, BF16), (box_own, box_other, item_bank))
    return contrast_loss, next_bank


def solution(mesh):
    return jax.shard_map(
        body,
        mesh=mesh,
        in_specs=(
            P(("bank", "dp"), None),
            P("dp", None),
            P("dp", None),
            P("bank", None),
            P(("bank", "dp")),
            P("bank", None),
            P("bank", None),
            P("bank"),
        ),
        out_specs=(P(("bank", "dp")), P("bank", None)),
        check_vma=False,
    )
```

time: 236 us -> 111 us (0.47)
  waiting for transfers between devices: 117 us -> 41.1 us
  blocking collectives: 42.6 us -> 13.1 us
  between operations: 14.2 us -> 0.74 us
  Pallas kernels: 0 us -> 9.31 us
  other arithmetic: 8.34 us -> 0 us
  matrix products: 7.95 us -> 0 us
    all_gather x2 -> x0, waiting for transfers between devices: 99.7 us -> none  [the longest x1 99.7 us: body(): block_rows = lax.all_gather(item_bank, 'bank', axis=0, tiled=True)]
    all_gather x1 -> x0, blocking collectives: 42.6 us -> none  [body(): lax.all_gather(w_output, 'dp', axis=0, tiled=True)]
    all_to_all x3, waiting for transfers between devices: 15.7 us -> 41.1 us  [exchange(): return lax.all_to_all(a, axis, 0, 0, axis_index_groups=groups, tiled=True)]
    ppermute x0 -> x2, starting transfers between devices: none -> 14.1 us  [the longest x1 10 us: body(): w_other = lax.ppermute(w_own, 'bank', swap)]
    all_to_all x3, starting transfers between devices: 39.4 us -> 25.7 us  [exchange(): return lax.all_to_all(a, axis, 0, 0, axis_index_groups=groups, tiled=True)]
    all_to_all x0 -> x1, blocking collectives: none -> 13.1 us  [exchange(): return lax.all_to_all(a, axis, 0, 0, axis_index_groups=groups, tiled=True)]
    pallas_call x0 -> x6, Pallas kernels: none -> 9.31 us  [call(): pl.pallas_call(kernel, out_shape=outs, in_specs=[pl.BlockSpec(memory_spac...]
    dot_general x3 -> x0, matrix products: 7.95 us -> none  [the longest x1 3.57 us: body(): lax.dot_general(unit_query, block_rows, (((1,), (1,)), ((), ())), preferr...]
  transfers between devices with their start and end apart: 5 -> 5, of which waited for: 3 -> 3; matrix products, arithmetic and copies ran while one was open for 6% -> 0% of each run, Pallas kernels for 0% -> 3%
where the time goes in v1:
time: 111 us; the launch traced here: 109 us
  waiting for transfers between devices  41.1 us (37%)
  starting transfers between devices  39.9 us (36%)
  blocking collectives  13.1 us (12%)
  Pallas kernels  9.31 us (8%)
  local copies, waits for them, and re-layouts  5.23 us (5%)
    all_to_all x3, waiting for transfers between devices, exchange(): return lax.all_to_all(a, axis, 0, 0, axis_index_groups=groups, tiled=True)  41.1 us
    all_to_all x3, starting transfers between devices, exchange(): return lax.all_to_all(a, axis, 0, 0, axis_index_groups=groups, tiled=True)  25.7 us
    all_to_all x1, blocking collectives, exchange(): return lax.all_to_all(a, axis, 0, 0, axis_index_groups=groups, tiled=True)  13.1 us
    ppermute x1, starting transfers between devices, body(): w_other = lax.ppermute(w_own, 'bank', swap)  10 us
    pallas_call x6, Pallas kernels, call(): pl.pallas_call(kernel, out_shape=outs, in_specs=[pl.BlockSpec(memory_spac...  9.31 us
    unnamed x20, local copies, waits for them, and re-layouts  5.23 us
    ppermute x1, starting transfers between devices, body(): box_other = lax.ppermute(box_own, 'bank', swap)  4.12 us
  transfers between devices with their start and end apart: 5, of which 3 were waited for; matrix products, arithmetic and copies ran while one was open for 0% of the time, Pallas kernels for 3%

profile of v1, /device:TPU:1, one launch (start us, length us, event | category | flops | bytes accessed | tf_op | source)
XLA Modules:
  0.0 109.3 jit_solution(18425920733907932356)
XLA Ops:
  0.6 0.0 copy-start.3
  0.6 0.9 copy-done.3
  1.6 0.8 copy-done.5
  2.4 1.2 %shard_map.96 = bf16[8,160,512]{2,1,0:T(8,128)(2,1)} custom-call(bf16[128,1024]{1,0:T(8,128)(2,1)S(1)} %copy-done.3, bf16[128,256]{1,0:T(8,128)(2,1)S(1)} %copy-done.5), custom_call_target="tpu_custom_call" | custom-call | tf_op jit(solution)/shard_map/pallas_call | solution.py:31
  3.6 10.3 %all-to-all-start = ((bf16[8,160,512]{2,1,0:T(8,128)(2,1)}), bf16[8,160,512]{2,1,0:T(8,128)(2,1)S(1)}, u32[]{:S(2)}, u32[]{:S(2)}) async-start(bf16[8,160,512]{2,1,0:T(8,128)(2,1)} %shard_map.96), calls=%async_computation | async-start | bytes 2621440 | tf_op jit(solution)/shard_map/all_to_all | solution.py:193
  13.9 0.0 copy-done.4
  13.9 1.1 %shard_map.95 = bf16[32,40,256]{2,1,0:T(8,128)(2,1)} custom-call(s32[1,64]{1,0:T(1,128)S(1)} %bitcast.5, s32[1,64]{1,0:T(1,128)S(1)} %bitcast.6, bf16[64,256]{1,0:T(8,128)(2,1)S(1)} %copy-done.6, bf16[128,256]{1,0:T(8,128)(2,1)S(1)} %copy-done.4), custom_call_target="tpu_custom_call" | custom-call | tf_op jit(solution)/shard_map/pallas_call | solution.py:31
  15.0 24.6 %all-to-all-done.w_own = bf16[8,160,512]{2,1,0:T(8,128)(2,1)S(1)} async-done(((bf16[8,160,512]{2,1,0:T(8,128)(2,1)}), bf16[8,160,512]{2,1,0:T(8,128)(2,1)S(1)}, u32[]{:S(2)}, u32[]{:S(2)}) %all-to-all-start) | async-done | bytes 1310752 | tf_op jit(solution)/shard_map/all_to_all | solution.py:193
  39.6 10.0 %collective-permute-start = (bf16[8,160,512]{2,1,0:T(8,128)(2,1)S(1)}, bf16[8,160,512]{2,1,0:T(8,128)(2,1)S(1)}, u32[]{:S(2)}, u32[]{:S(2)}) collective-permute-start(bf16[8,160,512]{2,1,0:T(8,128)(2,1)S(1)} %all-to-all-done.w_own), channel_id=1, source_target_pairs={{0,8},{8,0},{16,24},{24,16},{32,40},{40,32},{48,56},{56,48},{64,72... | collective-permute-start | bytes 3932168 | tf_op jit(solution)/shard_map/ppermute | solution.py:205
  49.6 12.2 %all-to-all-start.1 = ((bf16[32,40,256]{2,1,0:T(8,128)(2,1)}), bf16[32,40,256]{2,1,0:T(8,128)(2,1)S(1)}, u32[]{:S(2)}, u32[]{:S(2)}) async-start(bf16[32,40,256]{2,1,0:T(8,128)(2,1)} %shard_map.95), calls=%async_computation.1 | async-start | bytes 1310720 | tf_op jit(solution)/shard_map/all_to_all | solution.py:193
  61.8 0.0 collective-permute-done.w_other
  61.8 1.1 copy-done
  62.9 1.3 %copy-done.1 = bf16[8,160,512]{2,1,0:T(8,128)(2,1)S(1)} copy-done((bf16[8,160,512]{2,1,0:T(8,128)(2,1)S(1)}, bf16[8,160,512]{2,1,0:T(8,128)(2,1)}, u32[]{:S(2)}) %copy-start.1) | copy-done | bytes 1310744
  64.2 1.0 copy-done.2
  65.3 1.3 %shard_map.97 = bf16[4,272,256]{2,1,0:T(8,128)(2,1)S(1)} custom-call(bf16[256,1024]{1,0:T(8,128)(2,1)S(1)} %copy-done.2, bf16[8,160,512]{2,1,0:T(8,128)(2,1)S(1)} %all-to-all-done.w_own, bf16[8,160,512]{2,1,0:T(8,128)(2,1)S(1)} %copy-done.1, s32[1,256]{1,0:T(1,128)S(1)} %bitcast.4), custom_call_target="tpu_custom_call" | custom-call | tf_op jit(solution)/shard_map/pallas_call | solution.py:31
  66.6 13.4 %all-to-all-done.1.box_own = bf16[32,40,256]{2,1,0:T(8,128)(2,1)S(1)} async-done(((bf16[32,40,256]{2,1,0:T(8,128)(2,1)}), bf16[32,40,256]{2,1,0:T(8,128)(2,1)S(1)}, u32[]{:S(2)}, u32[]{:S(2)}) %all-to-all-start.1) | async-done | bytes 655392 | tf_op jit(solution)/shard_map/all_to_all | solution.py:193
  80.0 4.1 %collective-permute-start.1 = (bf16[32,40,256]{2,1,0:T(8,128)(2,1)S(1)}, bf16[32,40,256]{2,1,0:T(8,128)(2,1)S(1)}, u32[]{:S(2)}, u32[]{:S(2)}) collective-permute-start(bf16[32,40,256]{2,1,0:T(8,128)(2,1)S(1)} %all-to-all-done.1.box_own), channel_id=1, source_target_pairs={{0,8},{8,0},{16,24},{24,16},{32,40},{40,32},{48,56},{56,48},{64,72... | collective-permute-start | bytes 1966088 | tf_op jit(solution)/shard_map/ppermute | solution.py:218
  84.1 13.1 %all_to_all.20.shared = bf16[4,272,256]{2,1,0:T(8,128)(2,1)S(1)} all-to-all(bf16[4,272,256]{2,1,0:T(8,128)(2,1)S(1)} %shard_map.97), channel_id=1, replica_groups={{0,1,2,3},{4,5,6,7},{8,9,10,11},{12,13,14,15},{16,17,18,19},{20,21,22,2..., dimensions={0} | all-to-all | bytes 1114112 | tf_op jit(solution)/shard_map/all_to_all | solution.py:193
  97.2 0.0 collective-permute-done.1.box_other
  97.2 4.0 %shard_map.98 = f32[4,8,256]{2,1,0:T(8,128)} custom-call(bf16[4,272,256]{2,1,0:T(8,128)(2,1)S(1)} %all_to_all.20.shared, bf16[32,40,256]{2,1,0:T(8,128)(2,1)S(1)} %all-to-all-done.1.box_own, bf16[32,40,256]{2,1,0:T(8,128)(2,1)S(1)} %collective-permute-done.1.box_other), custom_call_target="tpu_custom_call" | custom-call | tf_op jit(solution)/shard_map/pallas_call | solution.py:31
  101.2 3.3 %all-to-all-start.3 = ((f32[4,8,256]{2,1,0:T(8,128)}), f32[4,8,256]{2,1,0:T(8,128)S(1)}, u32[]{:S(2)}, u32[]{:S(2)}) async-start(f32[4,8,256]{2,1,0:T(8,128)} %shard_map.98), calls=%async_computation.3 | async-start | bytes 65536 | tf_op jit(solution)/shard_map/all_to_all | solution.py:193
  104.4 1.1 %shard_map.100 = bf16[128,256]{1,0:T(8,128)(2,1)} custom-call(bf16[32,40,256]{2,1,0:T(8,128)(2,1)S(1)} %all-to-all-done.1.box_own, bf16[32,40,256]{2,1,0:T(8,128)(2,1)S(1)} %collective-permute-done.1.box_other, bf16[128,256]{1,0:T(8,128)(2,1)S(1)} %copy-done.4), custom_call_target="tpu_custom_call" | custom-call | tf_op jit(solution)/shard_map/pallas_call | solution.py:31
  105.6 3.1 %all-to-all-done.3.parts = f32[4,8,256]{2,1,0:T(8,128)S(1)} async-done(((f32[4,8,256]{2,1,0:T(8,128)}), f32[4,8,256]{2,1,0:T(8,128)S(1)}, u32[]{:S(2)}, u32[]{:S(2)}) %all-to-all-start.3) | async-done | bytes 32800 | tf_op jit(solution)/shard_map/all_to_all | solution.py:193
  108.7 0.6 shard_map.99
  (13 shorter events, 0.0 us)
Async XLA Ops:
  0.6 1.0 copy-start.3
  1.6 0.8 copy-start.5
  3.6 10.3 %copy-start.4 = (bf16[128,256]{1,0:T(8,128)(2,1)S(1)}, bf16[128,256]{1,0:T(8,128)(2,1)}, u32[]{:S(2)}) copy-start(bf16[128,256]{1,0:T(8,128)(2,1)} %bank.3) | copy-start | bytes 196612
  3.6 10.3 %copy-start.6 = (bf16[64,256]{1,0:T(8,128)(2,1)S(1)}, bf16[64,256]{1,0:T(8,128)(2,1)}, u32[]{:S(2)}) copy-start(bf16[64,256]{1,0:T(8,128)(2,1)} %fresh.1) | copy-start | bytes 98308
  3.6 10.3 %copy-start.8 = (s32[64,1]{0,1:T(1,128)S(1)}, s32[64,1]{0,1:T(1,128)}, u32[]{:S(2)}) copy-start(s32[64,1]{0,1:T(1,128)} %param.14) | copy-start | bytes 772
  3.6 10.3 %copy-start.9 = (s32[64]{0:T(128)S(1)}, s32[64]{0:T(128)}, u32[]{:S(2)}) copy-start(s32[64]{0:T(128)} %param.15) | copy-start | bytes 772
  3.6 36.0 %all-to-all-start = ((bf16[8,160,512]{2,1,0:T(8,128)(2,1)}), bf16[8,160,512]{2,1,0:T(8,128)(2,1)S(1)}, u32[]{:S(2)}, u32[]{:S(2)}) async-start(bf16[8,160,512]{2,1,0:T(8,128)(2,1)} %shard_map.96), calls=%async_computation | async-start | bytes 2621440 | tf_op jit(solution)/shard_map/all_to_all | solution.py:193
  13.9 49.0 %copy-start.7 = (s32[256]{0:T(256)S(1)}, s32[256]{0:T(256)}, u32[]{:S(2)}) copy-start(s32[256]{0:T(256)} %param.12) | copy-start | bytes 3076
  39.6 22.3 %collective-permute-start = (bf16[8,160,512]{2,1,0:T(8,128)(2,1)S(1)}, bf16[8,160,512]{2,1,0:T(8,128)(2,1)S(1)}, u32[]{:S(2)}, u32[]{:S(2)}) collective-permute-start(bf16[8,160,512]{2,1,0:T(8,128)(2,1)S(1)} %all-to-all-done.w_own), channel_id=1, source_target_pairs={{0,8},{8,0},{16,24},{24,16},{32,40},{40,32},{48,56},{56,48},{64,72... | collective-permute-start | bytes 3932168 | tf_op jit(solution)/shard_map/ppermute | solution.py:205
  49.6 30.4 %all-to-all-start.1 = ((bf16[32,40,256]{2,1,0:T(8,128)(2,1)}), bf16[32,40,256]{2,1,0:T(8,128)(2,1)S(1)}, u32[]{:S(2)}, u32[]{:S(2)}) async-start(bf16[32,40,256]{2,1,0:T(8,128)(2,1)} %shard_map.95), calls=%async_computation.1 | async-start | bytes 1310720 | tf_op jit(solution)/shard_map/all_to_all | solution.py:193
  61.8 1.1 copy-start
  62.9 1.3 %copy-start.1 = (bf16[8,160,512]{2,1,0:T(8,128)(2,1)S(1)}, bf16[8,160,512]{2,1,0:T(8,128)(2,1)}, u32[]{:S(2)}) copy-start(bf16[8,160,512]{2,1,0:T(8,128)(2,1)} %copy-done) | copy-start | bytes 3932164
  64.2 1.0 copy-start.2
  80.0 17.2 %collective-permute-start.1 = (bf16[32,40,256]{2,1,0:T(8,128)(2,1)S(1)}, bf16[32,40,256]{2,1,0:T(8,128)(2,1)S(1)}, u32[]{:S(2)}, u32[]{:S(2)}) collective-permute-start(bf16[32,40,256]{2,1,0:T(8,128)(2,1)S(1)} %all-to-all-done.1.box_own), channel_id=1, source_target_pairs={{0,8},{8,0},{16,24},{24,16},{32,40},{40,32},{48,56},{56,48},{64,72... | collective-permute-start | bytes 1966088 | tf_op jit(solution)/shard_map/ppermute | solution.py:218
  101.2 7.5 %all-to-all-start.3 = ((f32[4,8,256]{2,1,0:T(8,128)}), f32[4,8,256]{2,1,0:T(8,128)S(1)}, u32[]{:S(2)}, u32[]{:S(2)}) async-start(f32[4,8,256]{2,1,0:T(8,128)} %shard_map.98), calls=%async_computation.3 | async-start | bytes 65536 | tf_op jit(solution)/shard_map/all_to_all | solution.py:193

commit v2 on v0

v2 whole, which is shorter than its diff:
```python
import functools
import math

import jax
import jax.numpy as jnp
from jax import lax
from jax.experimental import pallas as pl
from jax.experimental.pallas import tpu as pltpu
from jax.sharding import PartitionSpec as P

BF16 = jnp.bfloat16
F32 = jnp.float32
I32 = jnp.int32

CORES = 2
X = 4
Y_LO = 4
Y = 8

VMEM = pltpu.VMEM
LIMIT = 48 * 1024 * 1024


def core_index():
    return lax.rem(lax.axis_index("bank"), CORES)


def y_lo_index():
    return lax.rem(lax.div(lax.axis_index("bank"), CORES), Y_LO)


def along_y(devices, members, moves):
    pairs = []
    for b in range(devices):
        for d in range(members):
            z, lo, core = b // (Y_LO * CORES), b // CORES % Y_LO, b % CORES
            hi, x = d // X, d % X
            y = moves[core][hi * Y_LO + lo] % Y
            to = ((z * Y_LO + y % Y_LO) * CORES + core) * members + y // Y_LO * X + x
            pairs.append((b * members + d, to))
    return pairs


def call(kernel, outs, args, scratch=()):
    return pl.pallas_call(
        kernel,
        out_shape=outs,
        in_specs=[pl.BlockSpec(memory_space=VMEM)] * len(args),
        out_specs=jax.tree.map(lambda _: pl.BlockSpec(memory_space=VMEM), outs),
        scratch_shapes=list(scratch),
        compiler_params=pltpu.CompilerParams(vmem_limit_bytes=LIMIT),
    )(*args)


def weights_kernel(w_input, w_output, out):
    rows, width = w_input.shape
    unit = w_output.shape[0] // CORES
    tall = out.shape[0] - rows
    wide = w_output.shape[1]

    def write(core):
        picked = [w_input[:, j + core * unit : j + (core + 1) * unit] for j in range(0, width, CORES * unit)]
        out[:rows, :] = jnp.concatenate(picked, axis=1)
        for i in range(unit // tall):
            at = core * unit + i * tall
            out[rows:, i * wide : (i + 1) * wide] = w_output[at : at + tall, :]

    for core in range(CORES):
        pl.when(core_index() == core)(functools.partial(write, core))


def outbox_kernel(owners, slots, fresh, bank, out):
    part = bank.shape[0]
    ring = out.shape[0]
    chips = ring * Y_LO
    for z in range(ring):
        out[z, :part, :] = bank[...]
    count = fresh.shape[0]
    owner = owners[...].astype(F32)
    across = jnp.broadcast_to(owner, (count, count))
    earlier = lax.broadcasted_iota(I32, (count, count), 0) < lax.broadcasted_iota(I32, (count, count), 1)
    same = across == across.T
    placed = jnp.sum(jnp.where(same & earlier, 1.0, 0.0), axis=0, keepdims=True)
    key = (owner * 2.0 + placed).astype(I32)
    row = lax.broadcasted_iota(I32, (chips * 8, count), 0)
    wanted = (row // 8) * 4 + (row % 4)
    chosen = wanted == key
    data = jnp.dot(chosen.astype(BF16), fresh[...], preferred_element_type=F32)
    slot = jnp.sum(jnp.where(chosen, slots[...].astype(F32) + 1.0, 0.0), axis=1, keepdims=True) - 1.0
    kind = lax.broadcasted_iota(I32, data.shape, 0) % 8
    both = jnp.where(kind < 4, data, slot).astype(BF16)
    out[:, part:, :] = both.reshape(ring, Y_LO * 8, both.shape[1])


def join_kernel(own, other, out):
    rows = own.shape[0]
    out[:rows, :] = own[...]
    out[rows:, :] = other[...]


def tower_kernel(q_own, q_other, w0, w1, w2, w3, positives, out, first, last):
    d = lax.axis_index("dp")
    x, y_hi = lax.rem(d, X), lax.div(d, X)
    count, depth = q_own.shape
    wide = out.shape[1]
    members = lax.axis_size("dp")
    rows = depth // members
    both = w0.shape[0] // 2
    tall = both - rows
    unit = tall * (w0.shape[1] // wide)
    for delta, w in enumerate((w0, w1, w2, w3)):
        for swapped in range(2):
            hi = jnp.where(swapped == 1, 1 - y_hi, y_hi)
            source = hi * X + lax.rem(x - delta + X, X)
            base = swapped * both
            first[pl.ds(pl.multiple_of(source * rows, rows), rows), :] = w[base : base + rows, :]
            for i in range(unit // tall):
                at = pl.multiple_of(source * unit + i * tall, tall)
                last[pl.ds(at, tall), :] = w[base + rows : base + both, i * wide : (i + 1) * wide]
    for i, q in enumerate((q_own, q_other)):
        v = jnp.dot(q[...], first[...], preferred_element_type=F32)
        v = (0.5 * v) * (1.0 + jnp.tanh(0.5 * v))
        out[i * count : (i + 1) * count, :] = jnp.dot(
            v.astype(BF16), last[...], preferred_element_type=F32
        )
    out[CORES * count :, :] = jnp.broadcast_to(positives[...].astype(F32), (8, wide))


def pick(box, part, which):
    rows = [box[:, part + 8 * j : part + 8 * (j + 1), :] for j in range(Y_LO)]
    out = rows[0]
    for j in range(1, Y_LO):
        out = jnp.where(which == j, rows[j], out)
    return out


def spread_kernel(box, *outs):
    y_lo = y_lo_index()
    part = outs[0].shape[1] - 8
    for i, out in enumerate(outs):
        out[:, :part, :] = box[:, :part, :]
        out[:, part:, :] = pick(box, part, lax.rem(y_lo + i + 1, Y_LO))


def scores_kernel(mine, received, b0, b1, b2, b3, keep, send):
    core, y_lo = core_index(), y_lo_index()
    count = keep.shape[1]
    ring = b1.shape[0]
    part = b1.shape[1] - 8
    scale = 16.0 * math.log2(math.e)
    local = ring * part
    number = lax.broadcasted_iota(I32, (local, count), 0)
    line = lax.broadcasted_iota(I32, (8, count), 0)
    for i, (place, out) in enumerate(((mine, keep), (received, send))):
        j = 1 - i
        embedding = mine[i * count : (i + 1) * count, :] + received[j * count : (j + 1) * count, :]
        norm = lax.rsqrt(jnp.sum(embedding * embedding, axis=1, keepdims=True) + 1e-06)
        unit = (embedding * norm).astype(BF16)
        positive = place[CORES * count : CORES * count + 1, :].astype(I32)
        block = positive // part
        chip = block // CORES
        away = (y_lo - chip % Y_LO + Y_LO) % Y_LO
        at = (chip // Y_LO) * part + positive % part
        at = jnp.where(block % CORES == core, at, -1)
        top = total = picked = None
        for delta, box in enumerate((b0, b1, b2, b3)):
            bank = box[:, :part, :].reshape(local, box.shape[2])
            d = lax.dot_general(bank, unit, (((1,), (1,)), ((), ())), preferred_element_type=F32)
            high = jnp.max(d, axis=0, keepdims=True)
            hit = number == jnp.where(away == delta, at, -1)
            here = jnp.sum(jnp.where(hit, d, 0.0), axis=0, keepdims=True)
            if top is None:
                top, picked = high, here
                total = jnp.sum(jnp.exp2((d - top) * scale), axis=0, keepdims=True)
            else:
                old, top = top, jnp.maximum(top, high)
                total = total * jnp.exp2((old - top) * scale)
                total += jnp.sum(jnp.exp2((d - top) * scale), axis=0, keepdims=True)
                picked += here
        out[:8, :] = jnp.where(
            line == 0, 16.0 * top, jnp.where(line == 1, total, jnp.where(line == 2, 16.0 * picked, 0.0))
        )
    blocks = [pick(b0, part, y_lo)] + [b[:, part:, :] for b in (b1, b2, b3)]
    for i, block in enumerate(blocks):
        fresh = block.reshape(ring * 8, block.shape[2]).astype(F32)
        for out in (keep, send):
            out[8 + i * ring * 8 : 8 + (i + 1) * ring * 8, :] = fresh


def last_kernel(keep, got, bank, loss, next_bank):
    tops = [keep[0:1, :], got[0:1, :]]
    top = jnp.maximum(*tops)
    total = sum(s[1:2, :] * jnp.exp(t - top) for s, t in zip((keep, got), tops))
    loss[...] = jnp.log(total) + top - (keep[2:3, :] + got[2:3, :])

    core, y_lo = core_index(), y_lo_index()
    count, wide = bank.shape
    lines = keep.shape[0] - 8
    ring = lines // (8 * Y_LO)
    line = lax.broadcasted_iota(I32, (lines, count), 0)
    kind = line % 8
    mine = (kind < 4) & ((kind // 2) == core)
    chip = (line // 8 % ring) * Y_LO + (y_lo + Y_LO - line // (8 * ring)) % Y_LO
    place = lax.broadcasted_iota(I32, (lines, count), 1).astype(F32)
    keys, rows = [], []
    for source, ref in ((core, keep), (1 - core, got)):
        block = ref[8:, :].reshape(lines // 8, 8, wide)
        slot = jnp.concatenate([block[:, 4:, :count], block[:, :4, :count]], axis=1)
        slot = slot.reshape(lines, count)
        order = chip * 4 + source * 2 + kind % 2
        keys.append(jnp.where(mine & (slot == place), order, -1))
        rows.append(ref[8:, :].astype(BF16))
    winner = jnp.maximum(*[jnp.max(k, axis=0, keepdims=True) for k in keys])
    written = jnp.zeros(bank.shape, F32)
    found = jnp.zeros((count, 128), F32)
    for key, row in zip(keys, rows):
        chosen = jnp.where((key == winner) & (key >= 0), 1.0, 0.0).astype(BF16)
        contract = (((0,), (0,)), ((), ()))
        written += lax.dot_general(chosen, row, contract, preferred_element_type=F32)
        ones = jnp.ones((lines, 128), BF16)
        found += lax.dot_general(chosen, ones, contract, preferred_element_type=F32)
    next_bank[...] = jnp.where(found[:, :1] > 0.5, written, bank[...].astype(F32)).astype(BF16)


def body(queries, w_input, w_output, item_bank, positives, fresh_rows, owners, slots):
    sds = jax.ShapeDtypeStruct
    count = queries.shape[0]
    members = lax.axis_size("dp")
    devices = lax.axis_size("bank")
    chips = devices // CORES
    ring = chips // Y_LO
    part, width = item_bank.shape
    half = w_input.shape[1] // CORES
    tall = w_input.shape[0] + w_output.size // CORES // half

    columns = [[z * Y_LO * CORES + i for z in range(ring)] for i in range(Y_LO * CORES)]
    swap = [(i, i ^ 1) for i in range(devices)]

    def around(a, delta):
        return lax.ppermute(
            a, "dp", [(i, i // X * X + (i % X + delta) % X) for i in range(members)]
        )

    def move_y(a, to):
        return lax.ppermute(a, ("bank", "dp"), along_y(devices, members, to))

    box_send = call(
        outbox_kernel,
        sds((ring, part + Y_LO * 8, width), BF16),
        (owners.reshape(1, -1), slots.reshape(1, -1), fresh_rows, item_bank),
    )
    box = lax.all_to_all(box_send, "bank", 0, 0, axis_index_groups=columns, tiled=True)
    w_mine = call(weights_kernel, sds((tall, half), BF16), (w_input, w_output))
    w_swapped = move_y(w_mine, [[6, 7, 4, 5, 2, 3, 0, 1]] * CORES)
    q_other = lax.ppermute(queries, "bank", swap)
    boxes = call(spread_kernel, (sds((ring, part + 8, width), BF16),) * 3, (box,))
    boxes = [
        move_y(b, [[y + step for y in range(Y)] for step in steps])
        for b, steps in zip(boxes, ((1, 1), (2, -2), (-1, -1)))
    ]
    w_both = call(join_kernel, sds((2 * tall, half), BF16), (w_mine, w_swapped))
    weights = [w_both] + [around(w_both, delta) for delta in range(1, X)]
    mine = call(
        tower_kernel,
        sds((CORES * count + 8, width), F32),
        (queries, q_other, *weights, positives.reshape(1, -1)),
        [VMEM((w_input.shape[1], half), BF16), VMEM((half, width), BF16)],
    )
    received = lax.ppermute(mine, "bank", swap)
    keep, send = call(
        scores_kernel, (sds((8 + chips * 8, width), F32),) * 2, (mine, received, box, *boxes)
    )
    got = lax.ppermute(send, "bank", swap)
    loss, next_bank = call(
        last_kernel,
        (sds((1, count), F32), sds(item_bank.shape, BF16)),
        (keep, got, item_bank),
    )
    return loss.reshape(count), next_bank


def solution(mesh):
    return jax.shard_map(
        body,
        mesh=mesh,
        in_specs=(
            P(("bank", "dp"), None),
            P("dp", None),
            P("dp", None),
            P("bank", None),
            P(("bank", "dp")),
            P("bank", None),
            P("bank", None),
            P("bank"),
        ),
        out_specs=(P(("bank", "dp")), P("bank", None)),
        check_vma=False,
    )
```

time: 236 us -> 83.1 us (0.35)
  waiting for transfers between devices: 117 us -> 23 us
  blocking collectives: 42.6 us -> 0 us
  between operations: 14.2 us -> 0.82 us
  starting transfers between devices: 39.5 us -> 48.4 us
  other arithmetic: 8.34 us -> 0 us
  matrix products: 7.95 us -> 0 us
  Pallas kernels: 0 us -> 7.34 us
  local copies, waits for them, and re-layouts: 5.72 us -> 2.28 us
    all_gather x2 -> x0, waiting for transfers between devices: 99.7 us -> none  [the longest x1 99.7 us: body(): block_rows = lax.all_gather(item_bank, 'bank', axis=0, tiled=True)]
    all_gather x1 -> x0, blocking collectives: 42.6 us -> none  [body(): lax.all_gather(w_output, 'dp', axis=0, tiled=True)]
    ppermute x0 -> x10, starting transfers between devices: none -> 37.4 us  [the longest x4 17.4 us: move_y(): return lax.ppermute(a, ('bank', 'dp'), along_y(devices, members, to))]
    all_to_all x3 -> x1, starting transfers between devices: 39.4 us -> 11 us  [body(): lax.all_to_all(box_send, 'bank', 0, 0, axis_index_groups=columns, tiled=T...]
    ppermute x0 -> x10, waiting for transfers between devices: none -> 23 us  [the longest x4 17 us: move_y(): return lax.ppermute(a, ('bank', 'dp'), along_y(devices, members, to))]
    all_to_all x3 -> x1, waiting for transfers between devices: 15.7 us -> 0.01 us  [body(): lax.all_to_all(box_send, 'bank', 0, 0, axis_index_groups=columns, tiled=T...]
    dot_general x3 -> x0, matrix products: 7.95 us -> none  [the longest x1 3.57 us: body(): lax.dot_general(unit_query, block_rows, (((1,), (1,)), ((), ())), preferr...]
    pallas_call x0 -> x7, Pallas kernels: none -> 7.34 us  [call(): pl.pallas_call(kernel, out_shape=outs, in_specs=[pl.BlockSpec(memory_spac...]
  transfers between devices with their start and end apart: 5 -> 11, of which waited for: 3 -> 5; matrix products, arithmetic and copies ran while one was open for 6% -> 0% of each run, Pallas kernels for 0% -> 2%
where the time goes in v2:
time: 83.1 us; the launch traced here: 81.9 us
  starting transfers between devices  48.4 us (58%)
  waiting for transfers between devices  23 us (28%)
  Pallas kernels  7.34 us (9%)
  local copies, waits for them, and re-layouts  2.28 us (3%)
    ppermute x4, starting transfers between devices, move_y(): return lax.ppermute(a, ('bank', 'dp'), along_y(devices, members, to))  17.4 us
    ppermute x4, waiting for transfers between devices, move_y(): return lax.ppermute(a, ('bank', 'dp'), along_y(devices, members, to))  17 us
    all_to_all x1, starting transfers between devices, body(): lax.all_to_all(box_send, 'bank', 0, 0, axis_index_groups=columns, tiled=T...  11 us
    ppermute x3, starting transfers between devices, around(): lax.ppermute(a, 'dp', [(i, i // X * X + (i % X + delta) % X) for i in ran...  9.33 us
    pallas_call x7, Pallas kernels, call(): pl.pallas_call(kernel, out_shape=outs, in_specs=[pl.BlockSpec(memory_spac...  7.34 us
    ppermute x1, starting transfers between devices, body(): received = lax.ppermute(mine, 'bank', swap)  5.29 us
    ppermute x3, waiting for transfers between devices, around(): lax.ppermute(a, 'dp', [(i, i // X * X + (i % X + delta) % X) for i in ran...  3.41 us
    ppermute x1, starting transfers between devices, body(): q_other = lax.ppermute(queries, 'bank', swap)  2.86 us
  transfers between devices with their start and end apart: 11, of which 5 were waited for; matrix products, arithmetic and copies ran while one was open for 0% of the time, Pallas kernels for 2%

profile of v2, /device:TPU:1, one launch (start us, length us, event | category | flops | bytes accessed | tf_op | source)
XLA Modules:
  0.0 81.9 jit_solution(5234733661160208568)
XLA Ops:
  0.7 0.6 copy-done.7
  1.3 0.8 %copy-done.1 = bf16[128,256]{1,0:T(8,128)(2,1)S(1)} copy-done((bf16[128,256]{1,0:T(8,128)(2,1)S(1)}, bf16[128,256]{1,0:T(8,128)(2,1)}, u32[]{:S(2)}) %copy-start.1) | copy-done | bytes 65560
  2.1 0.8 copy-done.5
  2.9 1.1 %shard_map.98 = bf16[8,160,256]{2,1,0:T(8,128)(2,1)} custom-call(s32[1,64]{1,0:T(1,128)S(1)} %bitcast.5, s32[1,64]{1,0:T(1,128)S(1)} %bitcast.6, bf16[64,256]{1,0:T(8,128)(2,1)S(1)} %copy-done.5, bf16[128,256]{1,0:T(8,128)(2,1)S(1)} %copy-done.1), custom_call_target="tpu_custom_call" | custom-call | tf_op jit(solution)/shard_map/pallas_call | solution.py:45
  4.0 11.0 %all-to-all-start = ((bf16[8,160,256]{2,1,0:T(8,128)(2,1)}), bf16[8,160,256]{2,1,0:T(8,128)(2,1)S(1)}, u32[]{:S(2)}, u32[]{:S(2)}) async-start(bf16[8,160,256]{2,1,0:T(8,128)(2,1)} %shard_map.98), calls=%async_computation | async-start | bytes 1310720 | tf_op jit(solution)/shard_map/all_to_all | solution.py:252
  15.0 2.9 %collective-permute-start = (bf16[256,1024]{1,0:T(8,128)(2,1)S(1)}, bf16[256,1024]{1,0:T(8,128)(2,1)S(1)}, u32[]{:S(2)}, u32[]{:S(2)}) collective-permute-start(bf16[256,1024]{1,0:T(8,128)(2,1)S(1)} %copy-done), channel_id=1, source_target_pairs={{0,8},{8,0},{16,24},{24,16},{32,40},{40,32},{48,56},{56,48},{64,72... | collective-permute-start | bytes 1572872 | tf_op jit(solution)/shard_map/ppermute | solution.py:255
  17.9 0.1 shard_map.95.own
  18.1 5.9 %collective-permute-start.1 = (bf16[160,512]{1,0:T(8,128)(2,1)S(1)}, bf16[160,512]{1,0:T(8,128)(2,1)S(1)}, u32[]{:S(2)}, u32[]{:S(2)}) collective-permute-start(bf16[160,512]{1,0:T(8,128)(2,1)S(1)} %shard_map.95.own), channel_id=1, source_target_pairs={{0,36},{1,37},{2,38},{3,39},{4,32},{5,33},{6,34},{7,35},{8,44},{9,... | collective-permute-start | bytes 491528 | tf_op jit(solution)/shard_map/ppermute | solution.py:245
  24.0 7.3 %collective-permute-done.1.other = bf16[160,512]{1,0:T(8,128)(2,1)S(1)} collective-permute-done((bf16[160,512]{1,0:T(8,128)(2,1)S(1)}, bf16[160,512]{1,0:T(8,128)(2,1)S(1)}, u32[]{:S(2)}, u32[]{:S(2)}) %collective-permute-start.1) | collective-permute-done | bytes 163872 | tf_op jit(solution)/shard_map/ppermute | solution.py:245
  31.3 4.4 %collective-permute-start.4 = (bf16[320,512]{1,0:T(8,128)(2,1)S(1)}, bf16[320,512]{1,0:T(8,128)(2,1)S(1)}, u32[]{:S(2)}, u32[]{:S(2)}) collective-permute-start(bf16[320,512]{1,0:T(8,128)(2,1)S(1)} %shard_map.96.w0), channel_id=1, source_target_pairs={{0,3},{1,0},{2,1},{3,2},{4,7},{5,4},{6,5},{7,6},{8,11},{9,8},{10,9... | collective-permute-start | bytes 983048 | tf_op jit(solution)/shard_map/ppermute | solution.py:240
  35.7 2.4 %collective-permute-start.3 = (bf16[320,512]{1,0:T(8,128)(2,1)S(1)}, bf16[320,512]{1,0:T(8,128)(2,1)S(1)}, u32[]{:S(2)}, u32[]{:S(2)}) collective-permute-start(bf16[320,512]{1,0:T(8,128)(2,1)S(1)} %shard_map.96.w0), channel_id=1, source_target_pairs={{0,2},{1,3},{2,0},{3,1},{4,6},{5,7},{6,4},{7,5},{8,10},{9,11},{10,... | collective-permute-start | bytes 983048 | tf_op jit(solution)/shard_map/ppermute | solution.py:240
  38.1 2.5 %collective-permute-start.2 = (bf16[320,512]{1,0:T(8,128)(2,1)S(1)}, bf16[320,512]{1,0:T(8,128)(2,1)S(1)}, u32[]{:S(2)}, u32[]{:S(2)}) collective-permute-start(bf16[320,512]{1,0:T(8,128)(2,1)S(1)} %shard_map.96.w0), channel_id=1, source_target_pairs={{0,1},{1,2},{2,3},{3,0},{4,5},{5,6},{6,7},{7,4},{8,9},{9,10},{10,1... | collective-permute-start | bytes 983048 | tf_op jit(solution)/shard_map/ppermute | solution.py:240
  40.8 3.4 %collective-permute-start.6 = (bf16[8,136,256]{2,1,0:T(8,128)(2,1)S(1)}, bf16[8,136,256]{2,1,0:T(8,128)(2,1)S(1)}, u32[]{:S(2)}, u32[]{:S(2)}) collective-permute-start(bf16[8,136,256]{2,1,0:T(8,128)(2,1)S(1)} %get-tuple-element.9), channel_id=1, source_target_pairs={{0,16},{1,17},{2,18},{3,19},{4,20},{5,21},{6,22},{7,23},{8,24},{9,... | collective-permute-start | bytes 1671176 | tf_op jit(solution)/shard_map/ppermute | solution.py:245
  44.2 4.9 %collective-permute-start.7 = (bf16[8,136,256]{2,1,0:T(8,128)(2,1)S(1)}, bf16[8,136,256]{2,1,0:T(8,128)(2,1)S(1)}, u32[]{:S(2)}, u32[]{:S(2)}) collective-permute-start(bf16[8,136,256]{2,1,0:T(8,128)(2,1)S(1)} %get-tuple-element.10), channel_id=1, source_target_pairs={{0,32},{1,33},{2,34},{3,35},{4,36},{5,37},{6,38},{7,39},{8,44},{9,... | collective-permute-start | bytes 1671176 | tf_op jit(solution)/shard_map/ppermute | solution.py:245
  49.1 3.2 %collective-permute-start.8 = (bf16[8,136,256]{2,1,0:T(8,128)(2,1)S(1)}, bf16[8,136,256]{2,1,0:T(8,128)(2,1)S(1)}, u32[]{:S(2)}, u32[]{:S(2)}) collective-permute-start(bf16[8,136,256]{2,1,0:T(8,128)(2,1)S(1)} %get-tuple-element.11), channel_id=1, source_target_pairs={{0,52},{1,53},{2,54},{3,55},{4,48},{5,49},{6,50},{7,51},{8,60},{9,... | collective-permute-start | bytes 1671176 | tf_op jit(solution)/shard_map/ppermute | solution.py:245
  52.3 3.4 %collective-permute-done.2.w1 = bf16[320,512]{1,0:T(8,128)(2,1)S(1)} collective-permute-done((bf16[320,512]{1,0:T(8,128)(2,1)S(1)}, bf16[320,512]{1,0:T(8,128)(2,1)S(1)}, u32[]{:S(2)}, u32[]{:S(2)}) %collective-permute-start.2) | collective-permute-done | bytes 327712 | tf_op jit(solution)/shard_map/ppermute | solution.py:240
  55.7 1.1 %shard_map.97.mine = f32[520,256]{1,0:T(8,128)S(1)} custom-call(bf16[256,1024]{1,0:T(8,128)(2,1)S(1)} %copy-done, bf16[256,1024]{1,0:T(8,128)(2,1)S(1)} %collective-permute-done.q_other, bf16[320,512]{1,0:T(8,128)(2,1)S(1)} %shard_map.96.w0, bf16[320,512]{1,0:T(8,128)(2,1)S(1)} %collective-permute-done.2.w1, bf16[320,512]{1,0:T(8,128)(2,1)S(1)} %collective-permute-done.3.w2, ...), custom_call_target="tpu_custom_call" | custom-call | tf_op jit(solution)/shard_map/pallas_call | solution.py:45
  56.9 5.3 %collective-permute-start.5 = (f32[520,256]{1,0:T(8,128)S(1)}, f32[520,256]{1,0:T(8,128)S(1)}, u32[]{:S(2)}, u32[]{:S(2)}) collective-permute-start(f32[520,256]{1,0:T(8,128)S(1)} %shard_map.97.mine), channel_id=1, source_target_pairs={{0,8},{8,0},{16,24},{24,16},{32,40},{40,32},{48,56},{56,48},{64,72... | collective-permute-start | bytes 1597448 | tf_op jit(solution)/shard_map/ppermute | solution.py:269
  62.2 1.5 %collective-permute-done.5.received = f32[520,256]{1,0:T(8,128)S(1)} collective-permute-done((f32[520,256]{1,0:T(8,128)S(1)}, f32[520,256]{1,0:T(8,128)S(1)}, u32[]{:S(2)}, u32[]{:S(2)}) %collective-permute-start.5) | collective-permute-done | bytes 532512 | tf_op jit(solution)/shard_map/ppermute | solution.py:269
  63.7 9.7 %collective-permute-done.8.b3 = bf16[8,136,256]{2,1,0:T(8,128)(2,1)S(1)} collective-permute-done((bf16[8,136,256]{2,1,0:T(8,128)(2,1)S(1)}, bf16[8,136,256]{2,1,0:T(8,128)(2,1)S(1)}, u32[]{:S(2)}, u32[]{:S(2)}) %collective-permute-start.8) | collective-permute-done | bytes 557088 | tf_op jit(solution)/shard_map/ppermute | solution.py:245
  73.4 3.6 %shard_map.100 = (f32[264,256]{1,0:T(8,128)S(1)}, f32[264,256]{1,0:T(8,128)S(1)}) custom-call(f32[520,256]{1,0:T(8,128)S(1)} %shard_map.97.mine, f32[520,256]{1,0:T(8,128)S(1)} %collective-permute-done.5.received, bf16[8,160,256]{2,1,0:T(8,128)(2,1)S(1)} %all-to-all-done.box.b0, bf16[8,136,256]{2,1,0:T(8,128)(2,1)S(1)} %collective-permute-done.6.b1, ...), custom_call_target="tpu_custom_call" | custom-call | tf_op jit(solution)/shard_map/pallas_call | solution.py:45
  77.0 2.5 %collective-permute-start.9 = (f32[264,256]{1,0:T(8,128)S(1)}, f32[264,256]{1,0:T(8,128)S(1)}, u32[]{:S(2)}, u32[]{:S(2)}) collective-permute-start(f32[264,256]{1,0:T(8,128)S(1)} %get-tuple-element.13), channel_id=1, source_target_pairs={{0,8},{8,0},{16,24},{24,16},{32,40},{40,32},{48,56},{56,48},{64,72... | collective-permute-start | bytes 811016 | tf_op jit(solution)/shard_map/ppermute | solution.py:273
  79.5 1.2 %collective-permute-done.9.got = f32[264,256]{1,0:T(8,128)S(1)} collective-permute-done((f32[264,256]{1,0:T(8,128)S(1)}, f32[264,256]{1,0:T(8,128)S(1)}, u32[]{:S(2)}, u32[]{:S(2)}) %collective-permute-start.9) | collective-permute-done | bytes 270368 | tf_op jit(solution)/shard_map/ppermute | solution.py:273
  80.7 1.2 %shard_map.101 = (f32[1,256]{1,0:T(1,128)}, bf16[128,256]{1,0:T(8,128)(2,1)}) custom-call(f32[264,256]{1,0:T(8,128)S(1)} %get-tuple-element.12.keep, f32[264,256]{1,0:T(8,128)S(1)} %collective-permute-done.9.got, bf16[128,256]{1,0:T(8,128)(2,1)S(1)} %copy-done.2), custom_call_target="tpu_custom_call" | custom-call | tf_op jit(solution)/shard_map/pallas_call | solution.py:45
  (23 shorter events, 0.2 us)
Async XLA Ops:
  0.6 0.7 copy-start.7
  0.6 0.7 copy-start.8
  1.3 0.8 %copy-start.1 = (bf16[128,256]{1,0:T(8,128)(2,1)S(1)}, bf16[128,256]{1,0:T(8,128)(2,1)}, u32[]{:S(2)}) copy-start(bf16[128,256]{1,0:T(8,128)(2,1)} %bank.3) | copy-start | bytes 196612
  2.1 0.8 copy-start.5
  4.0 11.0 %copy-start = (bf16[256,1024]{1,0:T(8,128)(2,1)S(1)}, bf16[256,1024]{1,0:T(8,128)(2,1)}, u32[]{:S(2)}) copy-start(bf16[256,1024]{1,0:T(8,128)(2,1)} %q_own.1) | copy-start | bytes 1572868
  4.0 13.9 %copy-start.3 = (bf16[128,1024]{1,0:T(8,128)(2,1)S(1)}, bf16[128,1024]{1,0:T(8,128)(2,1)}, u32[]{:S(2)}) copy-start(bf16[128,1024]{1,0:T(8,128)(2,1)} %w_input.1) | copy-start | bytes 786436
  4.0 13.9 %copy-start.4 = (bf16[128,256]{1,0:T(8,128)(2,1)S(1)}, bf16[128,256]{1,0:T(8,128)(2,1)}, u32[]{:S(2)}) copy-start(bf16[128,256]{1,0:T(8,128)(2,1)} %w_output.1) | copy-start | bytes 196612
  4.0 36.6 %all-to-all-start = ((bf16[8,160,256]{2,1,0:T(8,128)(2,1)}), bf16[8,160,256]{2,1,0:T(8,128)(2,1)S(1)}, u32[]{:S(2)}, u32[]{:S(2)}) async-start(bf16[8,160,256]{2,1,0:T(8,128)(2,1)} %shard_map.98), calls=%async_computation | async-start | bytes 1310720 | tf_op jit(solution)/shard_map/all_to_all | solution.py:252
  15.0 40.7 %collective-permute-start = (bf16[256,1024]{1,0:T(8,128)(2,1)S(1)}, bf16[256,1024]{1,0:T(8,128)(2,1)S(1)}, u32[]{:S(2)}, u32[]{:S(2)}) collective-permute-start(bf16[256,1024]{1,0:T(8,128)(2,1)S(1)} %copy-done), channel_id=1, source_target_pairs={{0,8},{8,0},{16,24},{24,16},{32,40},{40,32},{48,56},{56,48},{64,72... | collective-permute-start | bytes 1572872 | tf_op jit(solution)/shard_map/ppermute | solution.py:255
  18.1 13.2 %collective-permute-start.1 = (bf16[160,512]{1,0:T(8,128)(2,1)S(1)}, bf16[160,512]{1,0:T(8,128)(2,1)S(1)}, u32[]{:S(2)}, u32[]{:S(2)}) collective-permute-start(bf16[160,512]{1,0:T(8,128)(2,1)S(1)} %shard_map.95.own), channel_id=1, source_target_pairs={{0,36},{1,37},{2,38},{3,39},{4,32},{5,33},{6,34},{7,35},{8,44},{9,... | collective-permute-start | bytes 491528 | tf_op jit(solution)/shard_map/ppermute | solution.py:245
  31.3 12.9 %collective-permute-start.4 = (bf16[320,512]{1,0:T(8,128)(2,1)S(1)}, bf16[320,512]{1,0:T(8,128)(2,1)S(1)}, u32[]{:S(2)}, u32[]{:S(2)}) collective-permute-start(bf16[320,512]{1,0:T(8,128)(2,1)S(1)} %shard_map.96.w0), channel_id=1, source_target_pairs={{0,3},{1,0},{2,1},{3,2},{4,7},{5,4},{6,5},{7,6},{8,11},{9,8},{10,9... | collective-permute-start | bytes 983048 | tf_op jit(solution)/shard_map/ppermute | solution.py:240
  35.7 13.4 %collective-permute-start.3 = (bf16[320,512]{1,0:T(8,128)(2,1)S(1)}, bf16[320,512]{1,0:T(8,128)(2,1)S(1)}, u32[]{:S(2)}, u32[]{:S(2)}) collective-permute-start(bf16[320,512]{1,0:T(8,128)(2,1)S(1)} %shard_map.96.w0), channel_id=1, source_target_pairs={{0,2},{1,3},{2,0},{3,1},{4,6},{5,7},{6,4},{7,5},{8,10},{9,11},{10,... | collective-permute-start | bytes 983048 | tf_op jit(solution)/shard_map/ppermute | solution.py:240
  38.1 17.6 %collective-permute-start.2 = (bf16[320,512]{1,0:T(8,128)(2,1)S(1)}, bf16[320,512]{1,0:T(8,128)(2,1)S(1)}, u32[]{:S(2)}, u32[]{:S(2)}) collective-permute-start(bf16[320,512]{1,0:T(8,128)(2,1)S(1)} %shard_map.96.w0), channel_id=1, source_target_pairs={{0,1},{1,2},{2,3},{3,0},{4,5},{5,6},{6,7},{7,4},{8,9},{9,10},{10,1... | collective-permute-start | bytes 983048 | tf_op jit(solution)/shard_map/ppermute | solution.py:240
  40.8 23.0 %collective-permute-start.6 = (bf16[8,136,256]{2,1,0:T(8,128)(2,1)S(1)}, bf16[8,136,256]{2,1,0:T(8,128)(2,1)S(1)}, u32[]{:S(2)}, u32[]{:S(2)}) collective-permute-start(bf16[8,136,256]{2,1,0:T(8,128)(2,1)S(1)} %get-tuple-element.9), channel_id=1, source_target_pairs={{0,16},{1,17},{2,18},{3,19},{4,20},{5,21},{6,22},{7,23},{8,24},{9,... | collective-permute-start | bytes 1671176 | tf_op jit(solution)/shard_map/ppermute | solution.py:245
  44.2 19.5 %collective-permute-start.7 = (bf16[8,136,256]{2,1,0:T(8,128)(2,1)S(1)}, bf16[8,136,256]{2,1,0:T(8,128)(2,1)S(1)}, u32[]{:S(2)}, u32[]{:S(2)}) collective-permute-start(bf16[8,136,256]{2,1,0:T(8,128)(2,1)S(1)} %get-tuple-element.10), channel_id=1, source_target_pairs={{0,32},{1,33},{2,34},{3,35},{4,36},{5,37},{6,38},{7,39},{8,44},{9,... | collective-permute-start | bytes 1671176 | tf_op jit(solution)/shard_map/ppermute | solution.py:245
  49.1 6.6 %copy-start.6 = (s32[256]{0:T(256)S(1)}, s32[256]{0:T(256)}, u32[]{:S(2)}) copy-start(s32[256]{0:T(256)} %param.12) | copy-start | bytes 3076
  49.1 24.2 %collective-permute-start.8 = (bf16[8,136,256]{2,1,0:T(8,128)(2,1)S(1)}, bf16[8,136,256]{2,1,0:T(8,128)(2,1)S(1)}, u32[]{:S(2)}, u32[]{:S(2)}) collective-permute-start(bf16[8,136,256]{2,1,0:T(8,128)(2,1)S(1)} %get-tuple-element.11), channel_id=1, source_target_pairs={{0,52},{1,53},{2,54},{3,55},{4,48},{5,49},{6,50},{7,51},{8,60},{9,... | collective-permute-start | bytes 1671176 | tf_op jit(solution)/shard_map/ppermute | solution.py:245
  56.9 23.8 %copy-start.2 = (bf16[128,256]{1,0:T(8,128)(2,1)S(1)}, bf16[128,256]{1,0:T(8,128)(2,1)}, u32[]{:S(2)}) copy-start(bf16[128,256]{1,0:T(8,128)(2,1)} %bank.3) | copy-start | bytes 196612
  56.9 6.8 %collective-permute-start.5 = (f32[520,256]{1,0:T(8,128)S(1)}, f32[520,256]{1,0:T(8,128)S(1)}, u32[]{:S(2)}, u32[]{:S(2)}) collective-permute-start(f32[520,256]{1,0:T(8,128)S(1)} %shard_map.97.mine), channel_id=1, source_target_pairs={{0,8},{8,0},{16,24},{24,16},{32,40},{40,32},{48,56},{56,48},{64,72... | collective-permute-start | bytes 1597448 | tf_op jit(solution)/shard_map/ppermute | solution.py:269
  77.0 3.7 %collective-permute-start.9 = (f32[264,256]{1,0:T(8,128)S(1)}, f32[264,256]{1,0:T(8,128)S(1)}, u32[]{:S(2)}, u32[]{:S(2)}) collective-permute-start(f32[264,256]{1,0:T(8,128)S(1)} %get-tuple-element.13), channel_id=1, source_target_pairs={{0,8},{8,0},{16,24},{24,16},{32,40},{40,32},{48,56},{56,48},{64,72... | collective-permute-start | bytes 811016 | tf_op jit(solution)/shard_map/ppermute | solution.py:273

commit v3 on v2

v3 whole, which is shorter than its diff:
```python
import functools
import math

import jax
import jax.numpy as jnp
from jax import lax
from jax.experimental import pallas as pl
from jax.experimental.pallas import tpu as pltpu
from jax.sharding import PartitionSpec as P

BF16 = jnp.bfloat16
F32 = jnp.float32
I32 = jnp.int32

CORES = 2
X = 4
Y_LO = 4
Y = 8

VMEM = pltpu.VMEM
LIMIT = 48 * 1024 * 1024
MOST = 60 * 1024 * 1024
SMALL = pl.CostEstimate(flops=1 << 10, bytes_accessed=1 << 10, transcendentals=0)
LARGE = pl.CostEstimate(flops=1 << 36, bytes_accessed=1 << 10, transcendentals=0)


def core_index():
    return lax.rem(lax.axis_index("bank"), CORES)


def y_lo_index():
    return lax.rem(lax.div(lax.axis_index("bank"), CORES), Y_LO)


def half_index():
    return lax.rem(lax.rem(lax.axis_index("dp"), X) + core_index(), 2)


def to_partner(devices, members):
    pairs = []
    for b in range(devices):
        for d in range(members):
            x = d % X
            other = (x + 1 if (x + b) % 2 == 0 else x - 1) % X
            pairs.append((b * members + d, b * members + d - x + other))
    return pairs


def along_y(devices, members, moves):
    pairs = []
    for b in range(devices):
        for d in range(members):
            z, lo, core = b // (Y_LO * CORES), b // CORES % Y_LO, b % CORES
            hi, x = d // X, d % X
            y = moves[core][hi * Y_LO + lo] % Y
            to = ((z * Y_LO + y % Y_LO) * CORES + core) * members + y // Y_LO * X + x
            pairs.append((b * members + d, to))
    return pairs


def call(kernel, outs, args, scratch=(), ins=VMEM, space=None, limit=LIMIT, cost=SMALL):
    space = space or jax.tree.map(lambda _: VMEM, outs)
    return pl.pallas_call(
        kernel,
        out_shape=outs,
        in_specs=[pl.BlockSpec(memory_space=ins)] * len(args),
        out_specs=jax.tree.map(lambda _, s: pl.BlockSpec(memory_space=s), outs, space),
        scratch_shapes=list(scratch),
        cost_estimate=cost,
        compiler_params=pltpu.CompilerParams(vmem_limit_bytes=limit),
    )(*args)


def weights_kernel(w_input_in, w_output_in, half, w_input, w_output, sems):
    loads = [
        pltpu.make_async_copy(a, b, sems.at[i])
        for i, (a, b) in enumerate(((w_input_in, w_input), (w_output_in, w_output)))
    ]
    for copy in loads:
        copy.start()
    for copy in loads:
        copy.wait()
    tall, width = w_input.shape
    unit = w_output.shape[0] // CORES
    step = half.shape[0] - tall
    wide = w_output.shape[1]

    def write(core):
        picked = [w_input[:, j + core * unit : j + (core + 1) * unit] for j in range(0, width, CORES * unit)]
        half[:tall, :] = jnp.concatenate(picked, axis=1)
        for i in range(unit // step):
            at = core * unit + i * step
            half[tall:, i * wide : (i + 1) * wide] = w_output[at : at + step, :]

    for core in range(CORES):
        pl.when(core_index() == core)(functools.partial(write, core))


def outbox_kernel(owners_in, slots_in, fresh_in, bank_in, out, owners, slots, fresh, bank, rows, sems):
    part = bank.shape[0]
    ring = out.shape[0]
    at = pl.multiple_of(half_index() * part, part)
    loads = [
        pltpu.make_async_copy(a, b, sems.at[i])
        for i, (a, b) in enumerate(
            (
                (bank_in.at[pl.ds(at, part)], bank),
                (owners_in, owners),
                (slots_in, slots),
                (fresh_in, fresh),
            )
        )
    ]
    blocks = [pltpu.make_async_copy(bank, out.at[z, pl.ds(0, part)], sems.at[5 + z]) for z in range(ring)]
    for copy in loads:
        copy.start()
    loads[0].wait()
    for copy in blocks:
        copy.start()
    for copy in loads[1:]:
        copy.wait()
    count = fresh.shape[0]
    owner = owners[...].astype(F32)
    across = jnp.broadcast_to(owner, (count, count))
    earlier = lax.broadcasted_iota(I32, (count, count), 0) < lax.broadcasted_iota(I32, (count, count), 1)
    same = across == across.T
    placed = jnp.sum(jnp.where(same & earlier, 1.0, 0.0), axis=0, keepdims=True)
    key = (owner * 2.0 + placed).astype(I32)
    row = lax.broadcasted_iota(I32, (ring * Y_LO * 8, count), 0)
    wanted = (row // 8) * 4 + (row % 4)
    chosen = wanted == key
    data = jnp.dot(chosen.astype(BF16), fresh[...], preferred_element_type=F32)
    slot = jnp.sum(jnp.where(chosen, slots[...].astype(F32) + 1.0, 0.0), axis=1, keepdims=True) - 1.0
    kind = lax.broadcasted_iota(I32, data.shape, 0) % 8
    both = jnp.where(kind < 4, data, slot).astype(BF16)
    rows[...] = both.reshape(rows.shape)
    store = pltpu.make_async_copy(rows, out.at[:, pl.ds(part, rows.shape[1])], sems.at[4])
    store.start()
    for copy in (*blocks, store):
        copy.wait()


def join_kernel(own, other, out):
    rows = own.shape[0]
    out[:rows, :] = own[...]
    out[rows:, :] = other[...]


def tower_kernel(q_own, q_other, w0, w1, w2, w3, positives, out, first, last):
    d = lax.axis_index("dp")
    x, y_hi = lax.rem(d, X), lax.div(d, X)
    count, depth = q_own.shape
    wide = out.shape[1]
    members = lax.axis_size("dp")
    rows = depth // members
    both = w0.shape[0] // 2
    tall = both - rows
    unit = tall * (w0.shape[1] // wide)
    for delta, w in enumerate((w0, w1, w2, w3)):
        for swapped in range(2):
            hi = jnp.where(swapped == 1, 1 - y_hi, y_hi)
            source = hi * X + lax.rem(x + X - away_of(delta), X)
            base = swapped * both
            first[pl.ds(pl.multiple_of(source * rows, rows), rows), :] = w[base : base + rows, :]
            for i in range(unit // tall):
                at = pl.multiple_of(source * unit + i * tall, tall)
                last[pl.ds(at, tall), :] = w[base + rows : base + both, i * wide : (i + 1) * wide]
    for i, q in enumerate((q_own, q_other)):
        v = jnp.dot(q[...], first[...], preferred_element_type=F32)
        v = (0.5 * v) * (1.0 + jnp.tanh(0.5 * v))
        out[i * count : (i + 1) * count, :] = jnp.dot(
            v.astype(BF16), last[...], preferred_element_type=F32
        )
    out[CORES * count :, :] = jnp.broadcast_to(positives[...].astype(F32), (8, wide))


def away_of(i):
    return jnp.where(core_index() == 0, i, (4 - i) % 4)


def pick(box, part, which):
    rows = [box[:, part + 8 * j : part + 8 * (j + 1), :] for j in range(Y_LO)]
    out = rows[0]
    for j in range(1, Y_LO):
        out = jnp.where(which == j, rows[j], out)
    return out


def two_kernel(box, out):
    y_lo = y_lo_index()
    part = out.shape[1] - 16
    out[:, :part, :] = box[:, :part, :]
    fresh = [pick(box, part, lax.rem(y_lo + away_of(i), Y_LO)) for i in (2, 3)]
    out[:, part:, :] = jnp.concatenate(fresh, axis=1)


def one_kernel(box, two, out):
    part = two.shape[1] - 16
    out[:, :part, :] = box[:, :part, :]
    out[:, part : 2 * part, :] = two[:, :part, :]
    own = pick(box, part, lax.rem(y_lo_index() + away_of(1), Y_LO))
    out[:, 2 * part :, :] = jnp.concatenate([own, two[:, part + 8 :, :]], axis=1)


def unit_kernel(mine, received, out):
    count = (mine.shape[0] - 8) // CORES
    line = lax.broadcasted_iota(I32, (16, mine.shape[1]), 0)
    tail = jnp.zeros(line.shape, F32)
    for i, place in enumerate((mine, received)):
        j = 1 - i
        embedding = mine[i * count : (i + 1) * count, :] + received[j * count : (j + 1) * count, :]
        norm = lax.rsqrt(jnp.sum(embedding * embedding, axis=1, keepdims=True) + 1e-06)
        out[i * count : (i + 1) * count, :] = (embedding * norm).astype(BF16)
        positive = place[CORES * count : CORES * count + 1, :].astype(I32)
        tail = jnp.where(line == 2 * i, (positive // 128).astype(F32), tail)
        tail = jnp.where(line == 2 * i + 1, (positive % 128).astype(F32), tail)
    out[CORES * count :, :] = tail.astype(BF16)


def score_kernel(far, units, *refs):
    out = refs[-1]
    old = refs[0] if far else None
    core, y_lo, half = core_index(), y_lo_index(), half_index()
    ring, count = refs[1].shape[0], out.shape[1]
    part = (refs[1].shape[1] - 16) // (2 if far else 1)
    boxes = ((1, refs[1], 0), (3, refs[1], part)) if far else ((0, refs[0], 0), (2, refs[1], 0))
    scale = 16.0 * math.log2(math.e)
    local = ring * part
    number = lax.broadcasted_iota(I32, (local, count), 0)
    line = lax.broadcasted_iota(I32, (8, count), 0)
    tail = units[CORES * count :, :].astype(F32)
    for i in range(CORES):
        unit = units[i * count : (i + 1) * count, :]
        block = tail[2 * i : 2 * i + 1, :].astype(I32)
        row = tail[2 * i + 1 : 2 * i + 2, :].astype(I32)
        chip = block // CORES
        away = (y_lo - chip % Y_LO + Y_LO) % Y_LO
        at = (chip // Y_LO) * part + row % part
        at = jnp.where((block % CORES == core) & (row // part == half), at, -1)
        top = total = picked = None
        if old is not None:
            top, total, picked = (old[8 * i + k : 8 * i + k + 1, :] for k in range(3))
        for delta, box, base in boxes:
            bank = box[:, base : base + part, :].reshape(local, box.shape[2])
            d = lax.dot_general(bank, unit, (((1,), (1,)), ((), ())), preferred_element_type=F32)
            high = jnp.max(d, axis=0, keepdims=True)
            hit = number == jnp.where(away == away_of(delta), at, -1)
            here = jnp.sum(jnp.where(hit, d, 0.0), axis=0, keepdims=True)
            if top is None:
                top, picked = high, here
                total = jnp.sum(jnp.exp2((d - top) * scale), axis=0, keepdims=True)
            else:
                before, top = top, jnp.maximum(top, high)
                total = total * jnp.exp2((before - top) * scale)
                total += jnp.sum(jnp.exp2((d - top) * scale), axis=0, keepdims=True)
                picked += here
        out[8 * i : 8 * i + 8, :] = jnp.where(
            line == 0, top, jnp.where(line == 1, total, jnp.where(line == 2, picked, 0.0))
        )


def merge_kernel(state, back, b0, b2, b1, keep, send):
    line = lax.broadcasted_iota(I32, (8, state.shape[1]), 0)
    scale = 16.0 * math.log2(math.e)
    for i, out in enumerate((keep, send)):
        a, b = state[8 * i : 8 * i + 8, :], back[8 * i : 8 * i + 8, :]
        top = jnp.maximum(a[0:1, :], b[0:1, :])
        total = sum(s[1:2, :] * jnp.exp2((s[0:1, :] - top) * scale) for s in (a, b))
        out[:8, :] = jnp.where(line == 0, top, jnp.where(line == 1, total, a + b))
    ring, width = b2.shape[0], b2.shape[2]
    part = b2.shape[1] - 16
    blocks = [
        pick(b0, part, y_lo_index()),
        b1[:, 2 * part : 2 * part + 8, :],
        b2[:, part : part + 8, :],
        b1[:, 2 * part + 8 :, :],
    ]
    for i, block in enumerate(blocks):
        fresh = block.reshape(ring * 8, width).astype(F32)
        for out in (keep, send):
            out[8 + i * ring * 8 : 8 + (i + 1) * ring * 8, :] = fresh


def last_kernel(keep, got, bank, loss, next_bank):
    tops = [keep[0:1, :], got[0:1, :]]
    top = jnp.maximum(*tops)
    total = sum(s[1:2, :] * jnp.exp(16.0 * (t - top)) for s, t in zip((keep, got), tops))
    loss[...] = jnp.log(total) + 16.0 * (top - (keep[2:3, :] + got[2:3, :]))

    core, y_lo = core_index(), y_lo_index()
    count, wide = bank.shape
    lines = keep.shape[0] - 8
    ring = lines // (8 * Y_LO)
    line = lax.broadcasted_iota(I32, (lines, count), 0)
    kind = line % 8
    mine = (kind < 4) & ((kind // 2) == core)
    group = line // (8 * ring)
    place = lax.broadcasted_iota(I32, (lines, count), 1).astype(F32)
    keys, rows = [], []
    for source, ref in ((core, keep), (1 - core, got)):
        block = ref[8:, :].reshape(lines // 8, 8, wide)
        slot = jnp.concatenate([block[:, 4:, :count], block[:, :4, :count]], axis=1)
        slot = slot.reshape(lines, count)
        away = jnp.where(source == 0, group, (Y_LO - group) % Y_LO)
        chip = (line // 8 % ring) * Y_LO + (y_lo + Y_LO - away) % Y_LO
        order = chip * 4 + source * 2 + kind % 2
        keys.append(jnp.where(mine & (slot == place), order, -1))
        rows.append(ref[8:, :].astype(BF16))
    winner = jnp.maximum(*[jnp.max(k, axis=0, keepdims=True) for k in keys])
    written = jnp.zeros(bank.shape, F32)
    found = jnp.zeros((count, 128), F32)
    for key, row in zip(keys, rows):
        chosen = jnp.where((key == winner) & (key >= 0), 1.0, 0.0).astype(BF16)
        contract = (((0,), (0,)), ((), ()))
        written += lax.dot_general(chosen, row, contract, preferred_element_type=F32)
        ones = jnp.ones((lines, 128), BF16)
        found += lax.dot_general(chosen, ones, contract, preferred_element_type=F32)
    next_bank[...] = jnp.where(found[:, :1] > 0.5, written, bank[...].astype(F32)).astype(BF16)


def body(queries, w_input, w_output, item_bank, positives, fresh_rows, owners, slots):
    sds = jax.ShapeDtypeStruct
    count = queries.shape[0]
    members = lax.axis_size("dp")
    devices = lax.axis_size("bank")
    chips = devices // CORES
    ring = chips // Y_LO
    part, width = item_bank.shape[0] // 2, item_bank.shape[1]
    half = w_input.shape[1] // CORES
    tall = w_input.shape[0] + w_output.size // CORES // half

    columns = [[z * Y_LO * CORES + i for z in range(ring)] for i in range(Y_LO * CORES)]
    swap = [(i, i ^ 1) for i in range(devices)]

    def around(a, delta):
        pairs = []
        for i in range(devices * members):
            x, up = i % X, i // members % CORES == 0
            pairs.append((i, i - x + (x + (delta if up else -delta)) % X))
        return lax.ppermute(a, ("bank", "dp"), pairs)

    def move_y(a, to):
        return lax.ppermute(a, ("bank", "dp"), along_y(devices, members, to))

    w_mine = call(
        weights_kernel,
        sds((tall, half), BF16),
        (w_input, w_output),
        [VMEM(w_input.shape, BF16), VMEM(w_output.shape, BF16), pltpu.SemaphoreType.DMA((2,))],
        ins=pl.ANY,
        limit=MOST,
    )
    box_send = call(
        outbox_kernel,
        sds((ring, part + Y_LO * 8, width), BF16),
        (owners.reshape(1, -1), slots.reshape(1, -1), fresh_rows, item_bank),
        [
            VMEM((1, owners.shape[0]), I32),
            VMEM((1, slots.shape[0]), I32),
            VMEM(fresh_rows.shape, BF16),
            VMEM((part, width), BF16),
            VMEM((ring, Y_LO * 8, width), BF16),
            pltpu.SemaphoreType.DMA((5 + ring,)),
        ],
        ins=pl.ANY,
        space=pl.ANY,
        limit=MOST,
    )
    b0 = lax.all_to_all(box_send, "bank", 0, 0, axis_index_groups=columns, tiled=True)
    w_swapped = move_y(w_mine, [[6, 7, 4, 5, 2, 3, 0, 1]] * CORES)
    q_other = lax.ppermute(queries, "bank", swap)
    b2 = call(two_kernel, sds((ring, part + 16, width), BF16), (b0,))
    b2 = move_y(b2, [[y + step for y in range(Y)] for step in (2, -2)])
    b1 = call(one_kernel, sds((ring, 2 * part + 16, width), BF16), (b0, b2))
    b1 = move_y(b1, [[y + step for y in range(Y)] for step in (1, -1)])
    w_both = call(join_kernel, sds((2 * tall, half), BF16), (w_mine, w_swapped), cost=LARGE)
    weights = [w_both] + [around(w_both, delta) for delta in range(1, X)]
    b0, q_other = lax.optimization_barrier((b0, q_other))
    mine = call(
        tower_kernel,
        sds((CORES * count + 8, width), F32),
        (queries, q_other, *weights, positives.reshape(1, -1)),
        [VMEM((w_input.shape[1], half), BF16), VMEM((half, width), BF16)],
    )
    received = lax.ppermute(mine, "bank", swap)
    units = call(unit_kernel, sds((CORES * count + 16, width), BF16), (mine, received))
    partners = lax.ppermute(units, ("bank", "dp"), to_partner(devices, members))

    def score(far, units, *refs):
        return call(
            functools.partial(score_kernel, far), sds((8 * CORES, count), F32), (units, *refs)
        )

    state = score(False, units, b0, b2)
    theirs = score(False, partners, b0, b2)
    theirs = score(True, partners, theirs, b1)
    back = lax.ppermute(theirs, ("bank", "dp"), to_partner(devices, members))
    state = score(True, units, state, b1)
    keep, send = call(
        merge_kernel,
        (sds((8 + chips * 8, width), F32),) * 2,
        (state, back, b0, b2, b1),
    )
    got = lax.ppermute(send, "bank", swap)
    loss, next_bank = call(
        last_kernel,
        (sds((1, count), F32), sds(item_bank.shape, BF16)),
        (keep, got, item_bank),
    )
    return loss.reshape(count), next_bank


def solution(mesh):
    return jax.shard_map(
        body,
        mesh=mesh,
        in_specs=(
            P(("bank", "dp"), None),
            P("dp", None),
            P("dp", None),
            P("bank", None),
            P(("bank", "dp")),
            P("bank", None),
            P("bank", None),
            P("bank"),
        ),
        out_specs=(P(("bank", "dp")), P("bank", None)),
        check_vma=False,
    )
```

time: 83.1 us -> 75.7 us (0.911)
  waiting for transfers between devices: 23 us -> 16.2 us
  Pallas kernels: 7.34 us -> 10.2 us
  local copies, waits for them, and re-layouts: 2.28 us -> 0.02 us
    ppermute x4 -> x3, waiting for transfers between devices: 17 us -> 0.01 us  [move_y(): return lax.ppermute(a, ('bank', 'dp'), along_y(devices, members, to))]
    ppermute x3 -> x5, waiting for transfers between devices: 3.41 us -> 14.2 us  [the longest x3 8.34 us: around(): return lax.ppermute(a, ('bank', 'dp'), pairs)]
    ppermute x3 -> x5, starting transfers between devices: 9.33 us -> 15.9 us  [the longest x3 9.33 us: around(): return lax.ppermute(a, ('bank', 'dp'), pairs)]
    ppermute x4 -> x3, starting transfers between devices: 17.4 us -> 11.4 us  [move_y(): return lax.ppermute(a, ('bank', 'dp'), along_y(devices, members, to))]
    ppermute x1, starting transfers between devices: 5.29 us -> 1.92 us  [body(): received = lax.ppermute(mine, 'bank', swap)]
    pallas_call x7 -> x13, Pallas kernels: 7.34 us -> 10.2 us  [call(): pl.pallas_call(kernel, out_shape=outs, in_specs=[pl.BlockSpec(memory_spac...]
    ppermute x1, starting transfers between devices: 2.54 us -> 5.37 us  [body(): got = lax.ppermute(send, 'bank', swap)]
    unnamed x18 -> x8, local copies, waits for them, and re-layouts: 2.28 us -> 0.02 us
  transfers between devices with their start and end apart: 11 -> 12, of which waited for: 5 -> 7; matrix products, arithmetic and copies ran while one was open for 0% -> 0% of each run, Pallas kernels for 2% -> 8%
where the time goes in v3:
time: 75.7 us; the launch traced here: 75.2 us
  starting transfers between devices  47.9 us (63%)
  waiting for transfers between devices  16.2 us (21%)
  Pallas kernels  10.2 us (13%)
  between operations  0.86 us (1%)
    ppermute x3, starting transfers between devices, move_y(): return lax.ppermute(a, ('bank', 'dp'), along_y(devices, members, to))  11.4 us
    all_to_all x1, starting transfers between devices, body(): lax.all_to_all(box_send, 'bank', 0, 0, axis_index_groups=columns, tiled=T...  10.2 us
    pallas_call x13, Pallas kernels, call(): pl.pallas_call(kernel, out_shape=outs, in_specs=[pl.BlockSpec(memory_spac...  10.2 us
    ppermute x3, starting transfers between devices, around(): return lax.ppermute(a, ('bank', 'dp'), pairs)  9.33 us
    ppermute x3, waiting for transfers between devices, around(): return lax.ppermute(a, ('bank', 'dp'), pairs)  8.34 us
    ppermute x1, waiting for transfers between devices, body(): partners = lax.ppermute(units, ('bank', 'dp'), to_partner(devices, members))  5.39 us
    ppermute x1, starting transfers between devices, body(): got = lax.ppermute(send, 'bank', swap)  5.37 us
    ppermute x1, starting transfers between devices, body(): partners = lax.ppermute(units, ('bank', 'dp'), to_partner(devices, members))  3.31 us
  transfers between devices with their start and end apart: 12, of which 7 were waited for; matrix products, arithmetic and copies ran while one was open for 0% of the time, Pallas kernels for 8%

profile of v3, /device:TPU:1, one launch (start us, length us, event | category | flops | bytes accessed | tf_op | source)
XLA Modules:
  0.0 75.2 jit_solution(677030520211558932)
XLA Ops:
  0.6 1.7 %shard_map.96.own = bf16[160,512]{1,0:T(8,128)(2,1)} custom-call(bf16[128,1024]{1,0:T(8,128)(2,1)} %w_input_in.1, bf16[128,256]{1,0:T(8,128)(2,1)} %w_output_in.1), custom_call_target="tpu_custom_call" | custom-call | flops 1024 | bytes 1024 | tf_op jit(solution)/shard_map/pallas_call | solution.py:63
  2.4 6.7 %collective-permute-start.1 = (bf16[160,512]{1,0:T(8,128)(2,1)}, bf16[160,512]{1,0:T(8,128)(2,1)S(1)}, u32[]{:S(2)}, u32[]{:S(2)}) collective-permute-start(bf16[160,512]{1,0:T(8,128)(2,1)} %shard_map.96.own), channel_id=1, source_target_pairs={{0,36},{1,37},{2,38},{3,39},{4,32},{5,33},{6,34},{7,35},{8,44},{9,... | collective-permute-start | bytes 491528 | tf_op jit(solution)/shard_map/ppermute | solution.py:343
  9.1 1.9 %shard_map.95 = bf16[8,96,256]{2,1,0:T(8,128)(2,1)} custom-call(s32[1,64]{1,0:T(1,128)} %bitcast.5, s32[1,64]{1,0:T(1,128)} %bitcast.6, bf16[64,256]{1,0:T(8,128)(2,1)} %fresh_in.1, bf16[128,256]{1,0:T(8,128)(2,1)} %bank.1), custom_call_target="tpu_custom_call" | custom-call | flops 1024 | bytes 1024 | tf_op jit(solution)/shard_map/pallas_call | solution.py:63
  11.0 10.2 %all-to-all-start = ((bf16[8,96,256]{2,1,0:T(8,128)(2,1)}), bf16[8,96,256]{2,1,0:T(8,128)(2,1)S(1)}, u32[]{:S(2)}, u32[]{:S(2)}) async-start(bf16[8,96,256]{2,1,0:T(8,128)(2,1)} %shard_map.95), calls=%async_computation | async-start | bytes 786432 | tf_op jit(solution)/shard_map/all_to_all | solution.py:369
  21.2 3.1 %collective-permute-start = (bf16[256,1024]{1,0:T(8,128)(2,1)S(1)}, bf16[256,1024]{1,0:T(8,128)(2,1)S(1)}, u32[]{:S(2)}, u32[]{:S(2)}) collective-permute-start(bf16[256,1024]{1,0:T(8,128)(2,1)S(1)} %copy-done), channel_id=1, source_target_pairs={{0,8},{8,0},{16,24},{24,16},{32,40},{40,32},{48,56},{56,48},{64,72... | collective-permute-start | bytes 1572872 | tf_op jit(solution)/shard_map/ppermute | solution.py:371
  24.4 4.4 %collective-permute-start.2 = (bf16[320,512]{1,0:T(8,128)(2,1)S(1)}, bf16[320,512]{1,0:T(8,128)(2,1)S(1)}, u32[]{:S(2)}, u32[]{:S(2)}) collective-permute-start(bf16[320,512]{1,0:T(8,128)(2,1)S(1)} %shard_map.97.w0), channel_id=1, source_target_pairs={{0,1},{1,2},{2,3},{3,0},{4,5},{5,6},{6,7},{7,4},{8,11},{9,8},{10,9... | collective-permute-start | bytes 983048 | tf_op jit(solution)/shard_map/ppermute | solution.py:340
  28.8 2.4 %collective-permute-start.3 = (bf16[320,512]{1,0:T(8,128)(2,1)S(1)}, bf16[320,512]{1,0:T(8,128)(2,1)S(1)}, u32[]{:S(2)}, u32[]{:S(2)}) collective-permute-start(bf16[320,512]{1,0:T(8,128)(2,1)S(1)} %shard_map.97.w0), channel_id=1, source_target_pairs={{0,2},{1,3},{2,0},{3,1},{4,6},{5,7},{6,4},{7,5},{8,10},{9,11},{10,... | collective-permute-start | bytes 983048 | tf_op jit(solution)/shard_map/ppermute | solution.py:340
  31.3 2.5 %collective-permute-start.4 = (bf16[320,512]{1,0:T(8,128)(2,1)S(1)}, bf16[320,512]{1,0:T(8,128)(2,1)S(1)}, u32[]{:S(2)}, u32[]{:S(2)}) collective-permute-start(bf16[320,512]{1,0:T(8,128)(2,1)S(1)} %shard_map.97.w0), channel_id=1, source_target_pairs={{0,3},{1,0},{2,1},{3,2},{4,7},{5,4},{6,5},{7,6},{8,9},{9,10},{10,1... | collective-permute-start | bytes 983048 | tf_op jit(solution)/shard_map/ppermute | solution.py:340
  34.6 2.7 %collective-permute-start.6 = (bf16[8,80,256]{2,1,0:T(8,128)(2,1)S(1)}, bf16[8,80,256]{2,1,0:T(8,128)(2,1)S(1)}, u32[]{:S(2)}, u32[]{:S(2)}) collective-permute-start(bf16[8,80,256]{2,1,0:T(8,128)(2,1)S(1)} %shard_map.100), channel_id=1, source_target_pairs={{0,32},{1,33},{2,34},{3,35},{4,36},{5,37},{6,38},{7,39},{8,44},{9,... | collective-permute-start | bytes 983048 | tf_op jit(solution)/shard_map/ppermute | solution.py:343
  37.4 2.9 %collective-permute-done.2.w1 = bf16[320,512]{1,0:T(8,128)(2,1)S(1)} collective-permute-done((bf16[320,512]{1,0:T(8,128)(2,1)S(1)}, bf16[320,512]{1,0:T(8,128)(2,1)S(1)}, u32[]{:S(2)}, u32[]{:S(2)}) %collective-permute-start.2) | collective-permute-done | bytes 327712 | tf_op jit(solution)/shard_map/ppermute | solution.py:340
  40.3 1.8 %collective-permute-done.3.w2 = bf16[320,512]{1,0:T(8,128)(2,1)S(1)} collective-permute-done((bf16[320,512]{1,0:T(8,128)(2,1)S(1)}, bf16[320,512]{1,0:T(8,128)(2,1)S(1)}, u32[]{:S(2)}, u32[]{:S(2)}) %collective-permute-start.3) | collective-permute-done | bytes 327712 | tf_op jit(solution)/shard_map/ppermute | solution.py:340
  42.1 3.7 %collective-permute-done.4.w3 = bf16[320,512]{1,0:T(8,128)(2,1)S(1)} collective-permute-done((bf16[320,512]{1,0:T(8,128)(2,1)S(1)}, bf16[320,512]{1,0:T(8,128)(2,1)S(1)}, u32[]{:S(2)}, u32[]{:S(2)}) %collective-permute-start.4) | collective-permute-done | bytes 327712 | tf_op jit(solution)/shard_map/ppermute | solution.py:340
  45.7 1.1 %shard_map.98.mine = f32[520,256]{1,0:T(8,128)S(1)} custom-call(bf16[256,1024]{1,0:T(8,128)(2,1)S(1)} %copy-done, bf16[256,1024]{1,0:T(8,128)(2,1)S(1)} %collective-permute-done.q_other, bf16[320,512]{1,0:T(8,128)(2,1)S(1)} %shard_map.97.w0, bf16[320,512]{1,0:T(8,128)(2,1)S(1)} %collective-permute-done.2.w1, bf16[320,512]{1,0:T(8,128)(2,1)S(1)} %collective-permute-done.3.w2, ...), custom_call_target="tpu_custom_call" | custom-call | flops 1024 | bytes 1024 | tf_op jit(solution)/shard_map/pallas_call | solution.py:63
  46.9 1.9 %collective-permute-start.5 = (f32[520,256]{1,0:T(8,128)S(1)}, f32[520,256]{1,0:T(8,128)S(1)}, u32[]{:S(2)}, u32[]{:S(2)}) collective-permute-start(f32[520,256]{1,0:T(8,128)S(1)} %shard_map.98.mine), channel_id=1, source_target_pairs={{0,8},{8,0},{16,24},{24,16},{32,40},{40,32},{48,56},{56,48},{64,72... | collective-permute-start | bytes 1597448 | tf_op jit(solution)/shard_map/ppermute | solution.py:385
  48.9 1.9 %collective-permute-start.7 = (bf16[8,144,256]{2,1,0:T(8,128)(2,1)S(1)}, bf16[8,144,256]{2,1,0:T(8,128)(2,1)S(1)}, u32[]{:S(2)}, u32[]{:S(2)}) collective-permute-start(bf16[8,144,256]{2,1,0:T(8,128)(2,1)S(1)} %shard_map.102), channel_id=1, source_target_pairs={{0,16},{1,17},{2,18},{3,19},{4,20},{5,21},{6,22},{7,23},{8,60},{9,... | collective-permute-start | bytes 1769480 | tf_op jit(solution)/shard_map/ppermute | solution.py:343
  51.0 3.3 %collective-permute-start.8 = (bf16[528,256]{1,0:T(8,128)(2,1)S(1)}, bf16[528,256]{1,0:T(8,128)(2,1)S(1)}, u32[]{:S(2)}, u32[]{:S(2)}) collective-permute-start(bf16[528,256]{1,0:T(8,128)(2,1)S(1)} %shard_map.99.units), channel_id=1, source_target_pairs={{0,1},{1,0},{2,3},{3,2},{4,5},{5,4},{6,7},{7,6},{8,11},{9,10},{10,... | collective-permute-start | bytes 811016 | tf_op jit(solution)/shard_map/ppermute | solution.py:387
  54.3 5.4 %collective-permute-done.8.units = bf16[528,256]{1,0:T(8,128)(2,1)S(1)} collective-permute-done((bf16[528,256]{1,0:T(8,128)(2,1)S(1)}, bf16[528,256]{1,0:T(8,128)(2,1)S(1)}, u32[]{:S(2)}, u32[]{:S(2)}) %collective-permute-start.8) | collective-permute-done | bytes 270368 | tf_op jit(solution)/shard_map/ppermute | solution.py:387
  59.7 0.9 %shard_map.104.refs_0_ = f32[16,256]{1,0:T(8,128)S(1)} custom-call(bf16[528,256]{1,0:T(8,128)(2,1)S(1)} %collective-permute-done.8.units, bf16[8,96,256]{2,1,0:T(8,128)(2,1)S(1)} %all-to-all-done.box.refs_0_.b0, bf16[8,80,256]{2,1,0:T(8,128)(2,1)S(1)} %collective-permute-done.6.refs_1_.two.b2), custom_call_target="tpu_custom_call" | custom-call | flops 1024 | bytes 1024 | tf_op jit(solution)/shard_map/pallas_call | solution.py:63
  60.7 0.9 %shard_map.105 = f32[16,256]{1,0:T(8,128)S(1)} custom-call(bf16[528,256]{1,0:T(8,128)(2,1)S(1)} %collective-permute-done.8.units, f32[16,256]{1,0:T(8,128)S(1)} %shard_map.104.refs_0_, bf16[8,144,256]{2,1,0:T(8,128)(2,1)S(1)} %collective-permute-done.7.refs_1_.b1), custom_call_target="tpu_custom_call" | custom-call | flops 1024 | bytes 1024 | tf_op jit(solution)/shard_map/pallas_call | solution.py:63
  61.6 3.3 %collective-permute-start.9 = (f32[16,256]{1,0:T(8,128)S(1)}, f32[16,256]{1,0:T(8,128)S(1)}, u32[]{:S(2)}, u32[]{:S(2)}) collective-permute-start(f32[16,256]{1,0:T(8,128)S(1)} %shard_map.105), channel_id=1, source_target_pairs={{0,1},{1,0},{2,3},{3,2},{4,5},{5,4},{6,7},{7,6},{8,11},{9,10},{10,... | collective-permute-start | bytes 49160 | tf_op jit(solution)/shard_map/ppermute | solution.py:397
  64.9 0.9 %shard_map.101.refs_0_ = f32[16,256]{1,0:T(8,128)S(1)} custom-call(bf16[528,256]{1,0:T(8,128)(2,1)S(1)} %shard_map.99.units, bf16[8,96,256]{2,1,0:T(8,128)(2,1)S(1)} %all-to-all-done.box.refs_0_.b0, bf16[8,80,256]{2,1,0:T(8,128)(2,1)S(1)} %collective-permute-done.6.refs_1_.two.b2), custom_call_target="tpu_custom_call" | custom-call | flops 1024 | bytes 1024 | tf_op jit(solution)/shard_map/pallas_call | solution.py:63
  67.3 5.4 %collective-permute-start.10 = (f32[264,256]{1,0:T(8,128)S(1)}, f32[264,256]{1,0:T(8,128)S(1)}, u32[]{:S(2)}, u32[]{:S(2)}) collective-permute-start(f32[264,256]{1,0:T(8,128)S(1)} %get-tuple-element.11), channel_id=1, source_target_pairs={{0,8},{8,0},{16,24},{24,16},{32,40},{40,32},{48,56},{56,48},{64,72... | collective-permute-start | bytes 811016 | tf_op jit(solution)/shard_map/ppermute | solution.py:404
  72.7 1.2 %collective-permute-done.10.got = f32[264,256]{1,0:T(8,128)S(1)} collective-permute-done((f32[264,256]{1,0:T(8,128)S(1)}, f32[264,256]{1,0:T(8,128)S(1)}, u32[]{:S(2)}, u32[]{:S(2)}) %collective-permute-start.10) | collective-permute-done | bytes 270368 | tf_op jit(solution)/shard_map/ppermute | solution.py:404
  73.9 1.3 %shard_map.107 = (f32[1,256]{1,0:T(1,128)}, bf16[128,256]{1,0:T(8,128)(2,1)}) custom-call(f32[264,256]{1,0:T(8,128)S(1)} %get-tuple-element.10.keep, f32[264,256]{1,0:T(8,128)S(1)} %collective-permute-done.10.got, bf16[128,256]{1,0:T(8,128)(2,1)S(1)} %copy-done.1), custom_call_target="tpu_custom_call" | custom-call | flops 1024 | bytes 1024 | tf_op jit(solution)/shard_map/pallas_call | solution.py:63
  (21 shorter events, 2.6 us)
Async XLA Ops:
  2.4 22.0 %collective-permute-start.1 = (bf16[160,512]{1,0:T(8,128)(2,1)}, bf16[160,512]{1,0:T(8,128)(2,1)S(1)}, u32[]{:S(2)}, u32[]{:S(2)}) collective-permute-start(bf16[160,512]{1,0:T(8,128)(2,1)} %shard_map.96.own), channel_id=1, source_target_pairs={{0,36},{1,37},{2,38},{3,39},{4,32},{5,33},{6,34},{7,35},{8,44},{9,... | collective-permute-start | bytes 491528 | tf_op jit(solution)/shard_map/ppermute | solution.py:343
  9.1 12.1 %copy-start = (bf16[256,1024]{1,0:T(8,128)(2,1)S(1)}, bf16[256,1024]{1,0:T(8,128)(2,1)}, u32[]{:S(2)}) copy-start(bf16[256,1024]{1,0:T(8,128)(2,1)} %q_own.1) | copy-start | bytes 1572868
  11.0 13.4 %copy-start.2 = (bf16[160,512]{1,0:T(8,128)(2,1)S(1)}, bf16[160,512]{1,0:T(8,128)(2,1)}, u32[]{:S(2)}) copy-start(bf16[160,512]{1,0:T(8,128)(2,1)} %shard_map.96.own) | copy-start | bytes 491524
  11.0 23.6 %all-to-all-start = ((bf16[8,96,256]{2,1,0:T(8,128)(2,1)}), bf16[8,96,256]{2,1,0:T(8,128)(2,1)S(1)}, u32[]{:S(2)}, u32[]{:S(2)}) async-start(bf16[8,96,256]{2,1,0:T(8,128)(2,1)} %shard_map.95), calls=%async_computation | async-start | bytes 786432 | tf_op jit(solution)/shard_map/all_to_all | solution.py:369
  21.2 16.2 %collective-permute-start = (bf16[256,1024]{1,0:T(8,128)(2,1)S(1)}, bf16[256,1024]{1,0:T(8,128)(2,1)S(1)}, u32[]{:S(2)}, u32[]{:S(2)}) collective-permute-start(bf16[256,1024]{1,0:T(8,128)(2,1)S(1)} %copy-done), channel_id=1, source_target_pairs={{0,8},{8,0},{16,24},{24,16},{32,40},{40,32},{48,56},{56,48},{64,72... | collective-permute-start | bytes 1572872 | tf_op jit(solution)/shard_map/ppermute | solution.py:371
  24.4 15.9 %collective-permute-start.2 = (bf16[320,512]{1,0:T(8,128)(2,1)S(1)}, bf16[320,512]{1,0:T(8,128)(2,1)S(1)}, u32[]{:S(2)}, u32[]{:S(2)}) collective-permute-start(bf16[320,512]{1,0:T(8,128)(2,1)S(1)} %shard_map.97.w0), channel_id=1, source_target_pairs={{0,1},{1,2},{2,3},{3,0},{4,5},{5,6},{6,7},{7,4},{8,11},{9,8},{10,9... | collective-permute-start | bytes 983048 | tf_op jit(solution)/shard_map/ppermute | solution.py:340
  28.8 13.2 %collective-permute-start.3 = (bf16[320,512]{1,0:T(8,128)(2,1)S(1)}, bf16[320,512]{1,0:T(8,128)(2,1)S(1)}, u32[]{:S(2)}, u32[]{:S(2)}) collective-permute-start(bf16[320,512]{1,0:T(8,128)(2,1)S(1)} %shard_map.97.w0), channel_id=1, source_target_pairs={{0,2},{1,3},{2,0},{3,1},{4,6},{5,7},{6,4},{7,5},{8,10},{9,11},{10,... | collective-permute-start | bytes 983048 | tf_op jit(solution)/shard_map/ppermute | solution.py:340
  31.3 14.5 %collective-permute-start.4 = (bf16[320,512]{1,0:T(8,128)(2,1)S(1)}, bf16[320,512]{1,0:T(8,128)(2,1)S(1)}, u32[]{:S(2)}, u32[]{:S(2)}) collective-permute-start(bf16[320,512]{1,0:T(8,128)(2,1)S(1)} %shard_map.97.w0), channel_id=1, source_target_pairs={{0,3},{1,0},{2,1},{3,2},{4,7},{5,4},{6,5},{7,6},{8,9},{9,10},{10,1... | collective-permute-start | bytes 983048 | tf_op jit(solution)/shard_map/ppermute | solution.py:340
  34.6 11.1 %copy-start.3 = (s32[256]{0:T(256)S(1)}, s32[256]{0:T(256)}, u32[]{:S(2)}) copy-start(s32[256]{0:T(256)} %param.12) | copy-start | bytes 3076
  34.6 14.2 %collective-permute-start.6 = (bf16[8,80,256]{2,1,0:T(8,128)(2,1)S(1)}, bf16[8,80,256]{2,1,0:T(8,128)(2,1)S(1)}, u32[]{:S(2)}, u32[]{:S(2)}) collective-permute-start(bf16[8,80,256]{2,1,0:T(8,128)(2,1)S(1)} %shard_map.100), channel_id=1, source_target_pairs={{0,32},{1,33},{2,34},{3,35},{4,36},{5,37},{6,38},{7,39},{8,44},{9,... | collective-permute-start | bytes 983048 | tf_op jit(solution)/shard_map/ppermute | solution.py:343
  46.9 3.9 %collective-permute-start.5 = (f32[520,256]{1,0:T(8,128)S(1)}, f32[520,256]{1,0:T(8,128)S(1)}, u32[]{:S(2)}, u32[]{:S(2)}) collective-permute-start(f32[520,256]{1,0:T(8,128)S(1)} %shard_map.98.mine), channel_id=1, source_target_pairs={{0,8},{8,0},{16,24},{24,16},{32,40},{40,32},{48,56},{56,48},{64,72... | collective-permute-start | bytes 1597448 | tf_op jit(solution)/shard_map/ppermute | solution.py:385
  48.9 11.8 %collective-permute-start.7 = (bf16[8,144,256]{2,1,0:T(8,128)(2,1)S(1)}, bf16[8,144,256]{2,1,0:T(8,128)(2,1)S(1)}, u32[]{:S(2)}, u32[]{:S(2)}) collective-permute-start(bf16[8,144,256]{2,1,0:T(8,128)(2,1)S(1)} %shard_map.102), channel_id=1, source_target_pairs={{0,16},{1,17},{2,18},{3,19},{4,20},{5,21},{6,22},{7,23},{8,60},{9,... | collective-permute-start | bytes 1769480 | tf_op jit(solution)/shard_map/ppermute | solution.py:343
  51.0 8.7 %collective-permute-start.8 = (bf16[528,256]{1,0:T(8,128)(2,1)S(1)}, bf16[528,256]{1,0:T(8,128)(2,1)S(1)}, u32[]{:S(2)}, u32[]{:S(2)}) collective-permute-start(bf16[528,256]{1,0:T(8,128)(2,1)S(1)} %shard_map.99.units), channel_id=1, source_target_pairs={{0,1},{1,0},{2,3},{3,2},{4,5},{5,4},{6,7},{7,6},{8,11},{9,10},{10,... | collective-permute-start | bytes 811016 | tf_op jit(solution)/shard_map/ppermute | solution.py:387
  61.6 5.7 %collective-permute-start.9 = (f32[16,256]{1,0:T(8,128)S(1)}, f32[16,256]{1,0:T(8,128)S(1)}, u32[]{:S(2)}, u32[]{:S(2)}) collective-permute-start(f32[16,256]{1,0:T(8,128)S(1)} %shard_map.105), channel_id=1, source_target_pairs={{0,1},{1,0},{2,3},{3,2},{4,5},{5,4},{6,7},{7,6},{8,11},{9,10},{10,... | collective-permute-start | bytes 49160 | tf_op jit(solution)/shard_map/ppermute | solution.py:397
  66.8 7.1 %copy-start.1 = (bf16[128,256]{1,0:T(8,128)(2,1)S(1)}, bf16[128,256]{1,0:T(8,128)(2,1)}, u32[]{:S(2)}) copy-start(bf16[128,256]{1,0:T(8,128)(2,1)} %bank.1) | copy-start | bytes 196612
  67.3 6.5 %collective-permute-start.10 = (f32[264,256]{1,0:T(8,128)S(1)}, f32[264,256]{1,0:T(8,128)S(1)}, u32[]{:S(2)}, u32[]{:S(2)}) collective-permute-start(f32[264,256]{1,0:T(8,128)S(1)} %get-tuple-element.11), channel_id=1, source_target_pairs={{0,8},{8,0},{16,24},{24,16},{32,40},{40,32},{48,56},{56,48},{64,72... | collective-permute-start | bytes 811016 | tf_op jit(solution)/shard_map/ppermute | solution.py:404

commit v4 on v3

--- a/solution.py
+++ b/solution.py
@@ -71,32 +71,10 @@
     )(*args)
 
 
-def weights_kernel(w_input_in, w_output_in, half, w_input, w_output, sems):
-    loads = [
-        pltpu.make_async_copy(a, b, sems.at[i])
-        for i, (a, b) in enumerate(((w_input_in, w_input), (w_output_in, w_output)))
-    ]
-    for copy in loads:
-        copy.start()
-    for copy in loads:
-        copy.wait()
-    tall, width = w_input.shape
-    unit = w_output.shape[0] // CORES
-    step = half.shape[0] - tall
-    wide = w_output.shape[1]
-
-    def write(core):
-        picked = [w_input[:, j + core * unit : j + (core + 1) * unit] for j in range(0, width, CORES * unit)]
-        half[:tall, :] = jnp.concatenate(picked, axis=1)
-        for i in range(unit // step):
-            at = core * unit + i * step
-            half[tall:, i * wide : (i + 1) * wide] = w_output[at : at + step, :]
-
-    for core in range(CORES):
-        pl.when(core_index() == core)(functools.partial(write, core))
-
-
-def outbox_kernel(owners_in, slots_in, fresh_in, bank_in, out, owners, slots, fresh, bank, rows, sems):
+def first_kernel(
+    w_input_in, w_output_in, owners_in, slots_in, fresh_in, bank_in,
+    half, out, w_input, w_output, owners, slots, fresh, bank, rows, sems,
+):
     part = bank.shape[0]
     ring = out.shape[0]
     at = pl.multiple_of(half_index() * part, part)
@@ -108,16 +86,18 @@
                 (owners_in, owners),
                 (slots_in, slots),
                 (fresh_in, fresh),
+                (w_input_in, w_input),
+                (w_output_in, w_output),
             )
         )
     ]
-    blocks = [pltpu.make_async_copy(bank, out.at[z, pl.ds(0, part)], sems.at[5 + z]) for z in range(ring)]
+    blocks = [pltpu.make_async_copy(bank, out.at[z, pl.ds(0, part)], sems.at[7 + z]) for z in range(ring)]
     for copy in loads:
         copy.start()
     loads[0].wait()
     for copy in blocks:
         copy.start()
-    for copy in loads[1:]:
+    for copy in loads[1:4]:
         copy.wait()
     count = fresh.shape[0]
     owner = owners[...].astype(F32)
@@ -134,8 +114,24 @@
     kind = lax.broadcasted_iota(I32, data.shape, 0) % 8
     both = jnp.where(kind < 4, data, slot).astype(BF16)
     rows[...] = both.reshape(rows.shape)
-    store = pltpu.make_async_copy(rows, out.at[:, pl.ds(part, rows.shape[1])], sems.at[4])
+    store = pltpu.make_async_copy(rows, out.at[:, pl.ds(part, rows.shape[1])], sems.at[6])
     store.start()
+    for copy in loads[4:]:
+        copy.wait()
+    tall, width = w_input.shape
+    unit = w_output.shape[0] // CORES
+    step = half.shape[0] - tall
+    wide = w_output.shape[1]
+
+    def write(core):
+        picked = [w_input[:, j + core * unit : j + (core + 1) * unit] for j in range(0, width, CORES * unit)]
+        half[:tall, :] = jnp.concatenate(picked, axis=1)
+        for i in range(unit // step):
+            at = core * unit + i * step
+            half[tall:, i * wide : (i + 1) * wide] = w_output[at : at + step, :]
+
+    for core in range(CORES):
+        pl.when(core_index() == core)(functools.partial(write, core))
     for copy in (*blocks, store):
         copy.wait()
 
@@ -217,13 +213,17 @@
     out[CORES * count :, :] = tail.astype(BF16)
 
 
-def score_kernel(far, units, *refs):
+def score_kernel(near, far, units, *refs):
     out = refs[-1]
-    old = refs[0] if far else None
+    old = None if near else refs[0]
     core, y_lo, half = core_index(), y_lo_index(), half_index()
     ring, count = refs[1].shape[0], out.shape[1]
-    part = (refs[1].shape[1] - 16) // (2 if far else 1)
-    boxes = ((1, refs[1], 0), (3, refs[1], part)) if far else ((0, refs[0], 0), (2, refs[1], 0))
+    part = refs[1].shape[1] - 16 if near else (refs[1].shape[1] - 16) // 2
+    boxes = []
+    if near:
+        boxes += [(0, refs[0], 0), (2, refs[1], 0)]
+    if far:
+        boxes += [(1, refs[-2], 0), (3, refs[-2], part)]
     scale = 16.0 * math.log2(math.e)
     local = ring * part
     number = lax.broadcasted_iota(I32, (local, count), 0)
@@ -259,14 +259,8 @@
         )
 
 
-def merge_kernel(state, back, b0, b2, b1, keep, send):
-    line = lax.broadcasted_iota(I32, (8, state.shape[1]), 0)
-    scale = 16.0 * math.log2(math.e)
-    for i, out in enumerate((keep, send)):
-        a, b = state[8 * i : 8 * i + 8, :], back[8 * i : 8 * i + 8, :]
-        top = jnp.maximum(a[0:1, :], b[0:1, :])
-        total = sum(s[1:2, :] * jnp.exp2((s[0:1, :] - top) * scale) for s in (a, b))
-        out[:8, :] = jnp.where(line == 0, top, jnp.where(line == 1, total, a + b))
+def fresh_kernel(b0, b2, b1, mine, theirs):
+    core = core_index()
     ring, width = b2.shape[0], b2.shape[2]
     part = b2.shape[1] - 16
     blocks = [
@@ -275,37 +269,48 @@
         b2[:, part : part + 8, :],
         b1[:, 2 * part + 8 :, :],
     ]
+    count = ring * 2
     for i, block in enumerate(blocks):
-        fresh = block.reshape(ring * 8, width).astype(F32)
-        for out in (keep, send):
-            out[8 + i * ring * 8 : 8 + (i + 1) * ring * 8, :] = fresh
-
-
-def last_kernel(keep, got, bank, loss, next_bank):
+        block = block.astype(F32)
+        for j in range(2):
+            pair = [block[:, 4 * j + 2 * c : 4 * j + 2 * c + 2, :].reshape(count, width) for c in range(CORES)]
+            at = (4 * j + i) * count
+            mine[at : at + count, :] = jnp.where(core == 0, pair[0], pair[1])
+            theirs[at : at + count, :] = jnp.where(core == 0, pair[1], pair[0])
+
+
+def merge_kernel(state, back, theirs, keep, send):
+    line = lax.broadcasted_iota(I32, (8, state.shape[1]), 0)
+    scale = 16.0 * math.log2(math.e)
+    for i, out in enumerate((keep, send)):
+        a, b = state[8 * i : 8 * i + 8, :], back[8 * i : 8 * i + 8, :]
+        top = jnp.maximum(a[0:1, :], b[0:1, :])
+        total = sum(s[1:2, :] * jnp.exp2((s[0:1, :] - top) * scale) for s in (a, b))
+        out[:8, :] = jnp.where(line == 0, top, jnp.where(line == 1, total, a + b))
+    send[8:, :] = theirs[...]
+
+
+def last_kernel(keep, got, mine, bank, loss, next_bank):
     tops = [keep[0:1, :], got[0:1, :]]
     top = jnp.maximum(*tops)
     total = sum(s[1:2, :] * jnp.exp(16.0 * (t - top)) for s, t in zip((keep, got), tops))
     loss[...] = jnp.log(total) + 16.0 * (top - (keep[2:3, :] + got[2:3, :]))
 
     core, y_lo = core_index(), y_lo_index()
-    count, wide = bank.shape
-    lines = keep.shape[0] - 8
-    ring = lines // (8 * Y_LO)
+    count = bank.shape[0]
+    lines = mine.shape[0] // 2
+    ring = lines // (2 * Y_LO)
     line = lax.broadcasted_iota(I32, (lines, count), 0)
-    kind = line % 8
-    mine = (kind < 4) & ((kind // 2) == core)
-    group = line // (8 * ring)
+    group = line // (2 * ring)
     place = lax.broadcasted_iota(I32, (lines, count), 1).astype(F32)
     keys, rows = [], []
-    for source, ref in ((core, keep), (1 - core, got)):
-        block = ref[8:, :].reshape(lines // 8, 8, wide)
-        slot = jnp.concatenate([block[:, 4:, :count], block[:, :4, :count]], axis=1)
-        slot = slot.reshape(lines, count)
+    for source, ref, base in ((core, mine, 0), (1 - core, got, 8)):
         away = jnp.where(source == 0, group, (Y_LO - group) % Y_LO)
-        chip = (line // 8 % ring) * Y_LO + (y_lo + Y_LO - away) % Y_LO
-        order = chip * 4 + source * 2 + kind % 2
-        keys.append(jnp.where(mine & (slot == place), order, -1))
-        rows.append(ref[8:, :].astype(BF16))
+        chip = (line // 2 % ring) * Y_LO + (y_lo + Y_LO - away) % Y_LO
+        order = chip * 4 + source * 2 + line % 2
+        slot = ref[base + lines : base + 2 * lines, :count]
+        keys.append(jnp.where(slot == place, order, -1))
+        rows.append(ref[base : base + lines, :].astype(BF16))
     winner = jnp.maximum(*[jnp.max(k, axis=0, keepdims=True) for k in keys])
     written = jnp.zeros(bank.shape, F32)
     found = jnp.zeros((count, 128), F32)
@@ -342,28 +347,22 @@
     def move_y(a, to):
         return lax.ppermute(a, ("bank", "dp"), along_y(devices, members, to))
 
-    w_mine = call(
-        weights_kernel,
-        sds((tall, half), BF16),
-        (w_input, w_output),
-        [VMEM(w_input.shape, BF16), VMEM(w_output.shape, BF16), pltpu.SemaphoreType.DMA((2,))],
-        ins=pl.ANY,
-        limit=MOST,
-    )
-    box_send = call(
-        outbox_kernel,
-        sds((ring, part + Y_LO * 8, width), BF16),
-        (owners.reshape(1, -1), slots.reshape(1, -1), fresh_rows, item_bank),
+    w_mine, box_send = call(
+        first_kernel,
+        (sds((tall, half), BF16), sds((ring, part + Y_LO * 8, width), BF16)),
+        (w_input, w_output, owners.reshape(1, -1), slots.reshape(1, -1), fresh_rows, item_bank),
         [
+            VMEM(w_input.shape, BF16),
+            VMEM(w_output.shape, BF16),
             VMEM((1, owners.shape[0]), I32),
             VMEM((1, slots.shape[0]), I32),
             VMEM(fresh_rows.shape, BF16),
             VMEM((part, width), BF16),
             VMEM((ring, Y_LO * 8, width), BF16),
-            pltpu.SemaphoreType.DMA((5 + ring,)),
+            pltpu.SemaphoreType.DMA((7 + ring,)),
         ],
         ins=pl.ANY,
-        space=pl.ANY,
+        space=(VMEM, pl.ANY),
         limit=MOST,
     )
     b0 = lax.all_to_all(box_send, "bank", 0, 0, axis_index_groups=columns, tiled=True)
@@ -386,26 +385,28 @@
     units = call(unit_kernel, sds((CORES * count + 16, width), BF16), (mine, received))
     partners = lax.ppermute(units, ("bank", "dp"), to_partner(devices, members))
 
-    def score(far, units, *refs):
+    def score(near, far, units, *refs):
         return call(
-            functools.partial(score_kernel, far), sds((8 * CORES, count), F32), (units, *refs)
+            functools.partial(score_kernel, near, far), sds((8 * CORES, count), F32), (units, *refs)
         )
 
-    state = score(False, units, b0, b2)
-    theirs = score(False, partners, b0, b2)
-    theirs = score(True, partners, theirs, b1)
+    state = score(True, False, units, b0, b2)
+    theirs = score(True, False, partners, b0, b2)
+    theirs = score(False, True, partners, theirs, b1)
     back = lax.ppermute(theirs, ("bank", "dp"), to_partner(devices, members))
-    state = score(True, units, state, b1)
+    state = score(False, True, units, state, b1)
+    rows = (sds((4 * chips, width), F32),) * 2
+    fresh_mine, fresh_theirs = call(fresh_kernel, rows, (b0, b2, b1))
     keep, send = call(
         merge_kernel,
-        (sds((8 + chips * 8, width), F32),) * 2,
-        (state, back, b0, b2, b1),
+        (sds((8, count), F32), sds((8 + 4 * chips, width), F32)),
+        (state, back, fresh_theirs),
     )
     got = lax.ppermute(send, "bank", swap)
     loss, next_bank = call(
         last_kernel,
         (sds((1, count), F32), sds(item_bank.shape, BF16)),
-        (keep, got, item_bank),
+        (keep, got, fresh_mine, item_bank),
     )
     return loss.reshape(count), next_bank
 

time: 75.7 us -> 74.2 us (0.980)
  Pallas kernels: 10.2 us -> 8.89 us
    pallas_call x13, Pallas kernels: 10.2 us -> 8.89 us  [call(): pl.pallas_call(kernel, out_shape=outs, in_specs=[pl.BlockSpec(memory_spac...]
  transfers between devices with their start and end apart: 12 -> 12, of which waited for: 7 -> 7; matrix products, arithmetic and copies ran while one was open for 0% -> 0% of each run, Pallas kernels for 8% -> 6%
where the time goes in v4:
time: 74.2 us; the launch traced here: 73.6 us
  starting transfers between devices  48 us (65%)
  waiting for transfers between devices  15.9 us (21%)
  Pallas kernels  8.89 us (12%)
  between operations  0.85 us (1%)
    ppermute x3, starting transfers between devices, move_y(): return lax.ppermute(a, ('bank', 'dp'), along_y(devices, members, to))  11.4 us
    all_to_all x1, starting transfers between devices, body(): lax.all_to_all(box_send, 'bank', 0, 0, axis_index_groups=columns, tiled=T...  10.2 us
    ppermute x3, starting transfers between devices, around(): return lax.ppermute(a, ('bank', 'dp'), pairs)  9.33 us
    pallas_call x13, Pallas kernels, call(): pl.pallas_call(kernel, out_shape=outs, in_specs=[pl.BlockSpec(memory_spac...  8.89 us
    ppermute x3, waiting for transfers between devices, around(): return lax.ppermute(a, ('bank', 'dp'), pairs)  8.33 us
    ppermute x1, waiting for transfers between devices, body(): partners = lax.ppermute(units, ('bank', 'dp'), to_partner(devices, members))  5.39 us
    ppermute x1, starting transfers between devices, body(): got = lax.ppermute(send, 'bank', swap)  5.37 us
    ppermute x1, starting transfers between devices, body(): back = lax.ppermute(theirs, ('bank', 'dp'), to_partner(devices, members))  3.33 us
  transfers between devices with their start and end apart: 12, of which 7 were waited for; matrix products, arithmetic and copies ran while one was open for 0% of the time, Pallas kernels for 6%

profile of v4, /device:TPU:1, one launch (start us, length us, event | category | flops | bytes accessed | tf_op | source)
XLA Modules:
  0.0 73.6 jit_solution(6222620517856044954)
XLA Ops:
  0.6 2.6 %shard_map.95 = (bf16[160,512]{1,0:T(8,128)(2,1)}, bf16[8,96,256]{2,1,0:T(8,128)(2,1)}) custom-call(bf16[128,1024]{1,0:T(8,128)(2,1)} %w_input_in.1, bf16[128,256]{1,0:T(8,128)(2,1)} %w_output_in.1, s32[1,64]{1,0:T(1,128)} %bitcast.5, s32[1,64]{1,0:T(1,128)} %bitcast.6, bf16[64,256]{1,0:T(8,128)(2,1)} %fresh_in.1, bf16[128,256]{1,0:T(8,128)(2,1)} %bank.1), custom_call_target="tpu_custom_call" | custom-call | flops 1024 | bytes 1024 | tf_op jit(solution)/shard_map/pallas_call | solution.py:63
  3.2 6.7 %collective-permute-start.1 = (bf16[160,512]{1,0:T(8,128)(2,1)}, bf16[160,512]{1,0:T(8,128)(2,1)S(1)}, u32[]{:S(2)}, u32[]{:S(2)}) collective-permute-start(bf16[160,512]{1,0:T(8,128)(2,1)} %get-tuple-element.14.own), channel_id=1, source_target_pairs={{0,36},{1,37},{2,38},{3,39},{4,32},{5,33},{6,34},{7,35},{8,44},{9,... | collective-permute-start | bytes 491528 | tf_op jit(solution)/shard_map/ppermute | solution.py:348
  10.0 10.2 %all-to-all-start = ((bf16[8,96,256]{2,1,0:T(8,128)(2,1)}), bf16[8,96,256]{2,1,0:T(8,128)(2,1)S(1)}, u32[]{:S(2)}, u32[]{:S(2)}) async-start(bf16[8,96,256]{2,1,0:T(8,128)(2,1)} %get-tuple-element.12), calls=%async_computation | async-start | bytes 786432 | tf_op jit(solution)/shard_map/all_to_all | solution.py:368
  20.2 3.1 %collective-permute-start = (bf16[256,1024]{1,0:T(8,128)(2,1)S(1)}, bf16[256,1024]{1,0:T(8,128)(2,1)S(1)}, u32[]{:S(2)}, u32[]{:S(2)}) collective-permute-start(bf16[256,1024]{1,0:T(8,128)(2,1)S(1)} %copy-done), channel_id=1, source_target_pairs={{0,8},{8,0},{16,24},{24,16},{32,40},{40,32},{48,56},{56,48},{64,72... | collective-permute-start | bytes 1572872 | tf_op jit(solution)/shard_map/ppermute | solution.py:370
  23.4 4.4 %collective-permute-start.2 = (bf16[320,512]{1,0:T(8,128)(2,1)S(1)}, bf16[320,512]{1,0:T(8,128)(2,1)S(1)}, u32[]{:S(2)}, u32[]{:S(2)}) collective-permute-start(bf16[320,512]{1,0:T(8,128)(2,1)S(1)} %shard_map.96.w0), channel_id=1, source_target_pairs={{0,1},{1,2},{2,3},{3,0},{4,5},{5,6},{6,7},{7,4},{8,11},{9,8},{10,9... | collective-permute-start | bytes 983048 | tf_op jit(solution)/shard_map/ppermute | solution.py:345
  27.8 2.4 %collective-permute-start.3 = (bf16[320,512]{1,0:T(8,128)(2,1)S(1)}, bf16[320,512]{1,0:T(8,128)(2,1)S(1)}, u32[]{:S(2)}, u32[]{:S(2)}) collective-permute-start(bf16[320,512]{1,0:T(8,128)(2,1)S(1)} %shard_map.96.w0), channel_id=1, source_target_pairs={{0,2},{1,3},{2,0},{3,1},{4,6},{5,7},{6,4},{7,5},{8,10},{9,11},{10,... | collective-permute-start | bytes 983048 | tf_op jit(solution)/shard_map/ppermute | solution.py:345
  30.2 2.5 %collective-permute-start.4 = (bf16[320,512]{1,0:T(8,128)(2,1)S(1)}, bf16[320,512]{1,0:T(8,128)(2,1)S(1)}, u32[]{:S(2)}, u32[]{:S(2)}) collective-permute-start(bf16[320,512]{1,0:T(8,128)(2,1)S(1)} %shard_map.96.w0), channel_id=1, source_target_pairs={{0,3},{1,0},{2,1},{3,2},{4,7},{5,4},{6,5},{7,6},{8,9},{9,10},{10,1... | collective-permute-start | bytes 983048 | tf_op jit(solution)/shard_map/ppermute | solution.py:345
  33.6 2.7 %collective-permute-start.6 = (bf16[8,80,256]{2,1,0:T(8,128)(2,1)S(1)}, bf16[8,80,256]{2,1,0:T(8,128)(2,1)S(1)}, u32[]{:S(2)}, u32[]{:S(2)}) collective-permute-start(bf16[8,80,256]{2,1,0:T(8,128)(2,1)S(1)} %shard_map.99), channel_id=1, source_target_pairs={{0,32},{1,33},{2,34},{3,35},{4,36},{5,37},{6,38},{7,39},{8,44},{9,... | collective-permute-start | bytes 983048 | tf_op jit(solution)/shard_map/ppermute | solution.py:348
  36.3 2.9 %collective-permute-done.2.w1 = bf16[320,512]{1,0:T(8,128)(2,1)S(1)} collective-permute-done((bf16[320,512]{1,0:T(8,128)(2,1)S(1)}, bf16[320,512]{1,0:T(8,128)(2,1)S(1)}, u32[]{:S(2)}, u32[]{:S(2)}) %collective-permute-start.2) | collective-permute-done | bytes 327712 | tf_op jit(solution)/shard_map/ppermute | solution.py:345
  39.2 1.8 %collective-permute-done.3.w2 = bf16[320,512]{1,0:T(8,128)(2,1)S(1)} collective-permute-done((bf16[320,512]{1,0:T(8,128)(2,1)S(1)}, bf16[320,512]{1,0:T(8,128)(2,1)S(1)}, u32[]{:S(2)}, u32[]{:S(2)}) %collective-permute-start.3) | collective-permute-done | bytes 327712 | tf_op jit(solution)/shard_map/ppermute | solution.py:345
  41.0 3.7 %collective-permute-done.4.w3 = bf16[320,512]{1,0:T(8,128)(2,1)S(1)} collective-permute-done((bf16[320,512]{1,0:T(8,128)(2,1)S(1)}, bf16[320,512]{1,0:T(8,128)(2,1)S(1)}, u32[]{:S(2)}, u32[]{:S(2)}) %collective-permute-start.4) | collective-permute-done | bytes 327712 | tf_op jit(solution)/shard_map/ppermute | solution.py:345
  44.7 1.1 %shard_map.97.mine = f32[520,256]{1,0:T(8,128)S(1)} custom-call(bf16[256,1024]{1,0:T(8,128)(2,1)S(1)} %copy-done, bf16[256,1024]{1,0:T(8,128)(2,1)S(1)} %collective-permute-done.q_other, bf16[320,512]{1,0:T(8,128)(2,1)S(1)} %shard_map.96.w0, bf16[320,512]{1,0:T(8,128)(2,1)S(1)} %collective-permute-done.2.w1, bf16[320,512]{1,0:T(8,128)(2,1)S(1)} %collective-permute-done.3.w2, ...), custom_call_target="tpu_custom_call" | custom-call | flops 1024 | bytes 1024 | tf_op jit(solution)/shard_map/pallas_call | solution.py:63
  45.8 1.9 %collective-permute-start.5 = (f32[520,256]{1,0:T(8,128)S(1)}, f32[520,256]{1,0:T(8,128)S(1)}, u32[]{:S(2)}, u32[]{:S(2)}) collective-permute-start(f32[520,256]{1,0:T(8,128)S(1)} %shard_map.97.mine), channel_id=1, source_target_pairs={{0,8},{8,0},{16,24},{24,16},{32,40},{40,32},{48,56},{56,48},{64,72... | collective-permute-start | bytes 1597448 | tf_op jit(solution)/shard_map/ppermute | solution.py:384
  47.8 1.9 %collective-permute-start.7 = (bf16[8,144,256]{2,1,0:T(8,128)(2,1)S(1)}, bf16[8,144,256]{2,1,0:T(8,128)(2,1)S(1)}, u32[]{:S(2)}, u32[]{:S(2)}) collective-permute-start(bf16[8,144,256]{2,1,0:T(8,128)(2,1)S(1)} %shard_map.101), channel_id=1, source_target_pairs={{0,16},{1,17},{2,18},{3,19},{4,20},{5,21},{6,22},{7,23},{8,60},{9,... | collective-permute-start | bytes 1769480 | tf_op jit(solution)/shard_map/ppermute | solution.py:348
  49.9 3.3 %collective-permute-start.8 = (bf16[528,256]{1,0:T(8,128)(2,1)S(1)}, bf16[528,256]{1,0:T(8,128)(2,1)S(1)}, u32[]{:S(2)}, u32[]{:S(2)}) collective-permute-start(bf16[528,256]{1,0:T(8,128)(2,1)S(1)} %shard_map.98.units), channel_id=1, source_target_pairs={{0,1},{1,0},{2,3},{3,2},{4,5},{5,4},{6,7},{7,6},{8,11},{9,10},{10,... | collective-permute-start | bytes 811016 | tf_op jit(solution)/shard_map/ppermute | solution.py:386
  53.3 5.4 %collective-permute-done.8.units = bf16[528,256]{1,0:T(8,128)(2,1)S(1)} collective-permute-done((bf16[528,256]{1,0:T(8,128)(2,1)S(1)}, bf16[528,256]{1,0:T(8,128)(2,1)S(1)}, u32[]{:S(2)}, u32[]{:S(2)}) %collective-permute-start.8) | collective-permute-done | bytes 270368 | tf_op jit(solution)/shard_map/ppermute | solution.py:386
  58.6 0.9 %shard_map.103.refs_0_ = f32[16,256]{1,0:T(8,128)S(1)} custom-call(bf16[528,256]{1,0:T(8,128)(2,1)S(1)} %collective-permute-done.8.units, bf16[8,96,256]{2,1,0:T(8,128)(2,1)S(1)} %all-to-all-done.box.refs_0_.b0, bf16[8,80,256]{2,1,0:T(8,128)(2,1)S(1)} %collective-permute-done.6.refs_1_.two.b2), custom_call_target="tpu_custom_call" | custom-call | flops 1024 | bytes 1024 | tf_op jit(solution)/shard_map/pallas_call | solution.py:63
  59.6 0.9 %shard_map.104 = f32[16,256]{1,0:T(8,128)S(1)} custom-call(bf16[528,256]{1,0:T(8,128)(2,1)S(1)} %collective-permute-done.8.units, f32[16,256]{1,0:T(8,128)S(1)} %shard_map.103.refs_0_, bf16[8,144,256]{2,1,0:T(8,128)(2,1)S(1)} %collective-permute-done.7.refs_1_.b1), custom_call_target="tpu_custom_call" | custom-call | flops 1024 | bytes 1024 | tf_op jit(solution)/shard_map/pallas_call | solution.py:63
  60.5 3.3 %collective-permute-start.9 = (f32[16,256]{1,0:T(8,128)S(1)}, f32[16,256]{1,0:T(8,128)S(1)}, u32[]{:S(2)}, u32[]{:S(2)}) collective-permute-start(f32[16,256]{1,0:T(8,128)S(1)} %shard_map.104), channel_id=1, source_target_pairs={{0,1},{1,0},{2,3},{3,2},{4,5},{5,4},{6,7},{7,6},{8,11},{9,10},{10,... | collective-permute-start | bytes 49160 | tf_op jit(solution)/shard_map/ppermute | solution.py:396
  63.9 0.9 %shard_map.100.refs_0_ = f32[16,256]{1,0:T(8,128)S(1)} custom-call(bf16[528,256]{1,0:T(8,128)(2,1)S(1)} %shard_map.98.units, bf16[8,96,256]{2,1,0:T(8,128)(2,1)S(1)} %all-to-all-done.box.refs_0_.b0, bf16[8,80,256]{2,1,0:T(8,128)(2,1)S(1)} %collective-permute-done.6.refs_1_.two.b2), custom_call_target="tpu_custom_call" | custom-call | flops 1024 | bytes 1024 | tf_op jit(solution)/shard_map/pallas_call | solution.py:63
  64.9 0.9 %shard_map.102.state = f32[16,256]{1,0:T(8,128)S(1)} custom-call(bf16[528,256]{1,0:T(8,128)(2,1)S(1)} %shard_map.98.units, f32[16,256]{1,0:T(8,128)S(1)} %shard_map.100.refs_0_, bf16[8,144,256]{2,1,0:T(8,128)(2,1)S(1)} %collective-permute-done.7.refs_1_.b1), custom_call_target="tpu_custom_call" | custom-call | flops 1024 | bytes 1024 | tf_op jit(solution)/shard_map/pallas_call | solution.py:63
  66.3 5.4 %collective-permute-start.10 = (f32[136,256]{1,0:T(8,128)S(1)}, f32[136,256]{1,0:T(8,128)S(1)}, u32[]{:S(2)}, u32[]{:S(2)}) collective-permute-start(f32[136,256]{1,0:T(8,128)S(1)} %get-tuple-element.18), channel_id=1, source_target_pairs={{0,8},{8,0},{16,24},{24,16},{32,40},{40,32},{48,56},{56,48},{64,72... | collective-permute-start | bytes 417800 | tf_op jit(solution)/shard_map/ppermute | solution.py:405
  71.6 1.0 %collective-permute-done.10.got = f32[136,256]{1,0:T(8,128)S(1)} collective-permute-done((f32[136,256]{1,0:T(8,128)S(1)}, f32[136,256]{1,0:T(8,128)S(1)}, u32[]{:S(2)}, u32[]{:S(2)}) %collective-permute-start.10) | collective-permute-done | bytes 139296 | tf_op jit(solution)/shard_map/ppermute | solution.py:405
  72.6 1.0 %shard_map.107 = (f32[1,256]{1,0:T(1,128)}, bf16[128,256]{1,0:T(8,128)(2,1)}) custom-call(f32[8,256]{1,0:T(8,128)S(1)} %get-tuple-element.17.keep, f32[136,256]{1,0:T(8,128)S(1)} %collective-permute-done.10.got, f32[128,256]{1,0:T(8,128)S(1)} %get-tuple-element.19.mine, bf16[128,256]{1,0:T(8,128)(2,1)S(1)} %copy-done.1), custom_call_target="tpu_custom_call" | custom-call | flops 1024 | bytes 1024 | tf_op jit(solution)/shard_map/pallas_call | solution.py:63
  (21 shorter events, 1.7 us)
Async XLA Ops:
  0.6 19.5 %copy-start = (bf16[256,1024]{1,0:T(8,128)(2,1)S(1)}, bf16[256,1024]{1,0:T(8,128)(2,1)}, u32[]{:S(2)}) copy-start(bf16[256,1024]{1,0:T(8,128)(2,1)} %q_own.1) | copy-start | bytes 1572868
  3.2 20.1 %collective-permute-start.1 = (bf16[160,512]{1,0:T(8,128)(2,1)}, bf16[160,512]{1,0:T(8,128)(2,1)S(1)}, u32[]{:S(2)}, u32[]{:S(2)}) collective-permute-start(bf16[160,512]{1,0:T(8,128)(2,1)} %get-tuple-element.14.own), channel_id=1, source_target_pairs={{0,36},{1,37},{2,38},{3,39},{4,32},{5,33},{6,34},{7,35},{8,44},{9,... | collective-permute-start | bytes 491528 | tf_op jit(solution)/shard_map/ppermute | solution.py:348
  10.0 13.4 %copy-start.3 = (bf16[160,512]{1,0:T(8,128)(2,1)S(1)}, bf16[160,512]{1,0:T(8,128)(2,1)}, u32[]{:S(2)}) copy-start(bf16[160,512]{1,0:T(8,128)(2,1)} %get-tuple-element.14.own) | copy-start | bytes 491524
  10.0 23.6 %all-to-all-start = ((bf16[8,96,256]{2,1,0:T(8,128)(2,1)}), bf16[8,96,256]{2,1,0:T(8,128)(2,1)S(1)}, u32[]{:S(2)}, u32[]{:S(2)}) async-start(bf16[8,96,256]{2,1,0:T(8,128)(2,1)} %get-tuple-element.12), calls=%async_computation | async-start | bytes 786432 | tf_op jit(solution)/shard_map/all_to_all | solution.py:368
  20.2 16.2 %collective-permute-start = (bf16[256,1024]{1,0:T(8,128)(2,1)S(1)}, bf16[256,1024]{1,0:T(8,128)(2,1)S(1)}, u32[]{:S(2)}, u32[]{:S(2)}) collective-permute-start(bf16[256,1024]{1,0:T(8,128)(2,1)S(1)} %copy-done), channel_id=1, source_target_pairs={{0,8},{8,0},{16,24},{24,16},{32,40},{40,32},{48,56},{56,48},{64,72... | collective-permute-start | bytes 1572872 | tf_op jit(solution)/shard_map/ppermute | solution.py:370
  23.4 15.9 %collective-permute-start.2 = (bf16[320,512]{1,0:T(8,128)(2,1)S(1)}, bf16[320,512]{1,0:T(8,128)(2,1)S(1)}, u32[]{:S(2)}, u32[]{:S(2)}) collective-permute-start(bf16[320,512]{1,0:T(8,128)(2,1)S(1)} %shard_map.96.w0), channel_id=1, source_target_pairs={{0,1},{1,2},{2,3},{3,0},{4,5},{5,6},{6,7},{7,4},{8,11},{9,8},{10,9... | collective-permute-start | bytes 983048 | tf_op jit(solution)/shard_map/ppermute | solution.py:345
  27.8 13.2 %collective-permute-start.3 = (bf16[320,512]{1,0:T(8,128)(2,1)S(1)}, bf16[320,512]{1,0:T(8,128)(2,1)S(1)}, u32[]{:S(2)}, u32[]{:S(2)}) collective-permute-start(bf16[320,512]{1,0:T(8,128)(2,1)S(1)} %shard_map.96.w0), channel_id=1, source_target_pairs={{0,2},{1,3},{2,0},{3,1},{4,6},{5,7},{6,4},{7,5},{8,10},{9,11},{10,... | collective-permute-start | bytes 983048 | tf_op jit(solution)/shard_map/ppermute | solution.py:345
  30.2 14.5 %collective-permute-start.4 = (bf16[320,512]{1,0:T(8,128)(2,1)S(1)}, bf16[320,512]{1,0:T(8,128)(2,1)S(1)}, u32[]{:S(2)}, u32[]{:S(2)}) collective-permute-start(bf16[320,512]{1,0:T(8,128)(2,1)S(1)} %shard_map.96.w0), channel_id=1, source_target_pairs={{0,3},{1,0},{2,1},{3,2},{4,7},{5,4},{6,5},{7,6},{8,9},{9,10},{10,1... | collective-permute-start | bytes 983048 | tf_op jit(solution)/shard_map/ppermute | solution.py:345
  33.6 11.1 %copy-start.2 = (s32[256]{0:T(256)S(1)}, s32[256]{0:T(256)}, u32[]{:S(2)}) copy-start(s32[256]{0:T(256)} %param.12) | copy-start | bytes 3076
  33.6 14.2 %collective-permute-start.6 = (bf16[8,80,256]{2,1,0:T(8,128)(2,1)S(1)}, bf16[8,80,256]{2,1,0:T(8,128)(2,1)S(1)}, u32[]{:S(2)}, u32[]{:S(2)}) collective-permute-start(bf16[8,80,256]{2,1,0:T(8,128)(2,1)S(1)} %shard_map.99), channel_id=1, source_target_pairs={{0,32},{1,33},{2,34},{3,35},{4,36},{5,37},{6,38},{7,39},{8,44},{9,... | collective-permute-start | bytes 983048 | tf_op jit(solution)/shard_map/ppermute | solution.py:348
  45.8 3.9 %collective-permute-start.5 = (f32[520,256]{1,0:T(8,128)S(1)}, f32[520,256]{1,0:T(8,128)S(1)}, u32[]{:S(2)}, u32[]{:S(2)}) collective-permute-start(f32[520,256]{1,0:T(8,128)S(1)} %shard_map.97.mine), channel_id=1, source_target_pairs={{0,8},{8,0},{16,24},{24,16},{32,40},{40,32},{48,56},{56,48},{64,72... | collective-permute-start | bytes 1597448 | tf_op jit(solution)/shard_map/ppermute | solution.py:384
  47.8 11.8 %collective-permute-start.7 = (bf16[8,144,256]{2,1,0:T(8,128)(2,1)S(1)}, bf16[8,144,256]{2,1,0:T(8,128)(2,1)S(1)}, u32[]{:S(2)}, u32[]{:S(2)}) collective-permute-start(bf16[8,144,256]{2,1,0:T(8,128)(2,1)S(1)} %shard_map.101), channel_id=1, source_target_pairs={{0,16},{1,17},{2,18},{3,19},{4,20},{5,21},{6,22},{7,23},{8,60},{9,... | collective-permute-start | bytes 1769480 | tf_op jit(solution)/shard_map/ppermute | solution.py:348
  49.9 8.7 %collective-permute-start.8 = (bf16[528,256]{1,0:T(8,128)(2,1)S(1)}, bf16[528,256]{1,0:T(8,128)(2,1)S(1)}, u32[]{:S(2)}, u32[]{:S(2)}) collective-permute-start(bf16[528,256]{1,0:T(8,128)(2,1)S(1)} %shard_map.98.units), channel_id=1, source_target_pairs={{0,1},{1,0},{2,3},{3,2},{4,5},{5,4},{6,7},{7,6},{8,11},{9,10},{10,... | collective-permute-start | bytes 811016 | tf_op jit(solution)/shard_map/ppermute | solution.py:386
  60.5 5.7 %collective-permute-start.9 = (f32[16,256]{1,0:T(8,128)S(1)}, f32[16,256]{1,0:T(8,128)S(1)}, u32[]{:S(2)}, u32[]{:S(2)}) collective-permute-start(f32[16,256]{1,0:T(8,128)S(1)} %shard_map.104), channel_id=1, source_target_pairs={{0,1},{1,0},{2,3},{3,2},{4,5},{5,4},{6,7},{7,6},{8,11},{9,10},{10,... | collective-permute-start | bytes 49160 | tf_op jit(solution)/shard_map/ppermute | solution.py:396
  66.2 6.4 %copy-start.1 = (bf16[128,256]{1,0:T(8,128)(2,1)S(1)}, bf16[128,256]{1,0:T(8,128)(2,1)}, u32[]{:S(2)}) copy-start(bf16[128,256]{1,0:T(8,128)(2,1)} %bank.1) | copy-start | bytes 196612
  66.3 6.4 %collective-permute-start.10 = (f32[136,256]{1,0:T(8,128)S(1)}, f32[136,256]{1,0:T(8,128)S(1)}, u32[]{:S(2)}, u32[]{:S(2)}) collective-permute-start(f32[136,256]{1,0:T(8,128)S(1)} %get-tuple-element.18), channel_id=1, source_target_pairs={{0,8},{8,0},{16,24},{24,16},{32,40},{40,32},{48,56},{56,48},{64,72... | collective-permute-start | bytes 417800 | tf_op jit(solution)/shard_map/ppermute | solution.py:405

commit v5 on v4

--- a/solution.py
+++ b/solution.py
@@ -73,7 +73,7 @@
 
 def first_kernel(
     w_input_in, w_output_in, owners_in, slots_in, fresh_in, bank_in,
-    half, out, w_input, w_output, owners, slots, fresh, bank, rows, sems,
+    half, out, w_input, w_output, owners, slots, fresh, bank, sems,
 ):
     part = bank.shape[0]
     ring = out.shape[0]
@@ -91,11 +91,7 @@
             )
         )
     ]
-    blocks = [pltpu.make_async_copy(bank, out.at[z, pl.ds(0, part)], sems.at[7 + z]) for z in range(ring)]
     for copy in loads:
-        copy.start()
-    loads[0].wait()
-    for copy in blocks:
         copy.start()
     for copy in loads[1:4]:
         copy.wait()
@@ -113,9 +109,10 @@
     slot = jnp.sum(jnp.where(chosen, slots[...].astype(F32) + 1.0, 0.0), axis=1, keepdims=True) - 1.0
     kind = lax.broadcasted_iota(I32, data.shape, 0) % 8
     both = jnp.where(kind < 4, data, slot).astype(BF16)
-    rows[...] = both.reshape(rows.shape)
-    store = pltpu.make_async_copy(rows, out.at[:, pl.ds(part, rows.shape[1])], sems.at[6])
-    store.start()
+    out[:, part:, :] = both.reshape(ring, Y_LO * 8, both.shape[1])
+    loads[0].wait()
+    for z in range(ring):
+        out[z, :part, :] = bank[...]
     for copy in loads[4:]:
         copy.wait()
     tall, width = w_input.shape
@@ -132,8 +129,6 @@
 
     for core in range(CORES):
         pl.when(core_index() == core)(functools.partial(write, core))
-    for copy in (*blocks, store):
-        copy.wait()
 
 
 def join_kernel(own, other, out):
@@ -358,11 +353,9 @@
             VMEM((1, slots.shape[0]), I32),
             VMEM(fresh_rows.shape, BF16),
             VMEM((part, width), BF16),
-            VMEM((ring, Y_LO * 8, width), BF16),
-            pltpu.SemaphoreType.DMA((7 + ring,)),
+            pltpu.SemaphoreType.DMA((6,)),
         ],
         ins=pl.ANY,
-        space=(VMEM, pl.ANY),
         limit=MOST,
     )
     b0 = lax.all_to_all(box_send, "bank", 0, 0, axis_index_groups=columns, tiled=True)

time: 74.2 us -> 73.7 us (level)
  no operation moved by 1% of the time
where the time goes in v5:
time: 73.7 us; the launch traced here: 73.2 us
  starting transfers between devices  47.9 us (65%)
  waiting for transfers between devices  15.9 us (22%)
  Pallas kernels  8.45 us (11%)
  between operations  0.85 us (1%)
    ppermute x3, starting transfers between devices, move_y(): return lax.ppermute(a, ('bank', 'dp'), along_y(devices, members, to))  11.4 us
    all_to_all x1, starting transfers between devices, body(): lax.all_to_all(box_send, 'bank', 0, 0, axis_index_groups=columns, tiled=T...  10.2 us
    ppermute x3, starting transfers between devices, around(): return lax.ppermute(a, ('bank', 'dp'), pairs)  9.33 us
    pallas_call x13, Pallas kernels, call(): pl.pallas_call(kernel, out_shape=outs, in_specs=[pl.BlockSpec(memory_spac...  8.45 us
    ppermute x3, waiting for transfers between devices, around(): return lax.ppermute(a, ('bank', 'dp'), pairs)  8.34 us
    ppermute x1, waiting for transfers between devices, body(): partners = lax.ppermute(units, ('bank', 'dp'), to_partner(devices, members))  5.39 us
    ppermute x1, starting transfers between devices, body(): got = lax.ppermute(send, 'bank', swap)  5.38 us
    ppermute x1, starting transfers between devices, body(): back = lax.ppermute(theirs, ('bank', 'dp'), to_partner(devices, members))  3.32 us
  transfers between devices with their start and end apart: 12, of which 7 were waited for; matrix products, arithmetic and copies ran while one was open for 0% of the time, Pallas kernels for 6%

profile of v5, /device:TPU:1, one launch (start us, length us, event | category | flops | bytes accessed | tf_op | source)
XLA Modules:
  0.0 73.2 jit_solution(10273692930841904048)
XLA Ops:
  0.6 2.2 %shard_map.95 = (bf16[160,512]{1,0:T(8,128)(2,1)}, bf16[8,96,256]{2,1,0:T(8,128)(2,1)}) custom-call(bf16[128,1024]{1,0:T(8,128)(2,1)} %w_input_in.1, bf16[128,256]{1,0:T(8,128)(2,1)} %w_output_in.1, s32[1,64]{1,0:T(1,128)} %bitcast.5, s32[1,64]{1,0:T(1,128)} %bitcast.6, bf16[64,256]{1,0:T(8,128)(2,1)} %fresh_in.1, bf16[128,256]{1,0:T(8,128)(2,1)} %bank.1), custom_call_target="tpu_custom_call" | custom-call | flops 1024 | bytes 1024 | tf_op jit(solution)/shard_map/pallas_call | solution.py:63
  2.8 6.7 %collective-permute-start.1 = (bf16[160,512]{1,0:T(8,128)(2,1)}, bf16[160,512]{1,0:T(8,128)(2,1)S(1)}, u32[]{:S(2)}, u32[]{:S(2)}) collective-permute-start(bf16[160,512]{1,0:T(8,128)(2,1)} %get-tuple-element.14.own), channel_id=1, source_target_pairs={{0,36},{1,37},{2,38},{3,39},{4,32},{5,33},{6,34},{7,35},{8,44},{9,... | collective-permute-start | bytes 491528 | tf_op jit(solution)/shard_map/ppermute | solution.py:343
  9.5 10.2 %all-to-all-start = ((bf16[8,96,256]{2,1,0:T(8,128)(2,1)}), bf16[8,96,256]{2,1,0:T(8,128)(2,1)S(1)}, u32[]{:S(2)}, u32[]{:S(2)}) async-start(bf16[8,96,256]{2,1,0:T(8,128)(2,1)} %get-tuple-element.12), calls=%async_computation | async-start | bytes 786432 | tf_op jit(solution)/shard_map/all_to_all | solution.py:361
  19.7 3.1 %collective-permute-start = (bf16[256,1024]{1,0:T(8,128)(2,1)S(1)}, bf16[256,1024]{1,0:T(8,128)(2,1)S(1)}, u32[]{:S(2)}, u32[]{:S(2)}) collective-permute-start(bf16[256,1024]{1,0:T(8,128)(2,1)S(1)} %copy-done), channel_id=1, source_target_pairs={{0,8},{8,0},{16,24},{24,16},{32,40},{40,32},{48,56},{56,48},{64,72... | collective-permute-start | bytes 1572872 | tf_op jit(solution)/shard_map/ppermute | solution.py:363
  22.9 4.4 %collective-permute-start.2 = (bf16[320,512]{1,0:T(8,128)(2,1)S(1)}, bf16[320,512]{1,0:T(8,128)(2,1)S(1)}, u32[]{:S(2)}, u32[]{:S(2)}) collective-permute-start(bf16[320,512]{1,0:T(8,128)(2,1)S(1)} %shard_map.96.w0), channel_id=1, source_target_pairs={{0,1},{1,2},{2,3},{3,0},{4,5},{5,6},{6,7},{7,4},{8,11},{9,8},{10,9... | collective-permute-start | bytes 983048 | tf_op jit(solution)/shard_map/ppermute | solution.py:340
  27.3 2.4 %collective-permute-start.3 = (bf16[320,512]{1,0:T(8,128)(2,1)S(1)}, bf16[320,512]{1,0:T(8,128)(2,1)S(1)}, u32[]{:S(2)}, u32[]{:S(2)}) collective-permute-start(bf16[320,512]{1,0:T(8,128)(2,1)S(1)} %shard_map.96.w0), channel_id=1, source_target_pairs={{0,2},{1,3},{2,0},{3,1},{4,6},{5,7},{6,4},{7,5},{8,10},{9,11},{10,... | collective-permute-start | bytes 983048 | tf_op jit(solution)/shard_map/ppermute | solution.py:340
  29.8 2.5 %collective-permute-start.4 = (bf16[320,512]{1,0:T(8,128)(2,1)S(1)}, bf16[320,512]{1,0:T(8,128)(2,1)S(1)}, u32[]{:S(2)}, u32[]{:S(2)}) collective-permute-start(bf16[320,512]{1,0:T(8,128)(2,1)S(1)} %shard_map.96.w0), channel_id=1, source_target_pairs={{0,3},{1,0},{2,1},{3,2},{4,7},{5,4},{6,5},{7,6},{8,9},{9,10},{10,1... | collective-permute-start | bytes 983048 | tf_op jit(solution)/shard_map/ppermute | solution.py:340
  33.1 2.7 %collective-permute-start.6 = (bf16[8,80,256]{2,1,0:T(8,128)(2,1)S(1)}, bf16[8,80,256]{2,1,0:T(8,128)(2,1)S(1)}, u32[]{:S(2)}, u32[]{:S(2)}) collective-permute-start(bf16[8,80,256]{2,1,0:T(8,128)(2,1)S(1)} %shard_map.99), channel_id=1, source_target_pairs={{0,32},{1,33},{2,34},{3,35},{4,36},{5,37},{6,38},{7,39},{8,44},{9,... | collective-permute-start | bytes 983048 | tf_op jit(solution)/shard_map/ppermute | solution.py:343
  35.9 2.9 %collective-permute-done.2.w1 = bf16[320,512]{1,0:T(8,128)(2,1)S(1)} collective-permute-done((bf16[320,512]{1,0:T(8,128)(2,1)S(1)}, bf16[320,512]{1,0:T(8,128)(2,1)S(1)}, u32[]{:S(2)}, u32[]{:S(2)}) %collective-permute-start.2) | collective-permute-done | bytes 327712 | tf_op jit(solution)/shard_map/ppermute | solution.py:340
  38.8 1.8 %collective-permute-done.3.w2 = bf16[320,512]{1,0:T(8,128)(2,1)S(1)} collective-permute-done((bf16[320,512]{1,0:T(8,128)(2,1)S(1)}, bf16[320,512]{1,0:T(8,128)(2,1)S(1)}, u32[]{:S(2)}, u32[]{:S(2)}) %collective-permute-start.3) | collective-permute-done | bytes 327712 | tf_op jit(solution)/shard_map/ppermute | solution.py:340
  40.6 3.7 %collective-permute-done.4.w3 = bf16[320,512]{1,0:T(8,128)(2,1)S(1)} collective-permute-done((bf16[320,512]{1,0:T(8,128)(2,1)S(1)}, bf16[320,512]{1,0:T(8,128)(2,1)S(1)}, u32[]{:S(2)}, u32[]{:S(2)}) %collective-permute-start.4) | collective-permute-done | bytes 327712 | tf_op jit(solution)/shard_map/ppermute | solution.py:340
  44.2 1.1 %shard_map.97.mine = f32[520,256]{1,0:T(8,128)S(1)} custom-call(bf16[256,1024]{1,0:T(8,128)(2,1)S(1)} %copy-done, bf16[256,1024]{1,0:T(8,128)(2,1)S(1)} %collective-permute-done.q_other, bf16[320,512]{1,0:T(8,128)(2,1)S(1)} %shard_map.96.w0, bf16[320,512]{1,0:T(8,128)(2,1)S(1)} %collective-permute-done.2.w1, bf16[320,512]{1,0:T(8,128)(2,1)S(1)} %collective-permute-done.3.w2, ...), custom_call_target="tpu_custom_call" | custom-call | flops 1024 | bytes 1024 | tf_op jit(solution)/shard_map/pallas_call | solution.py:63
  45.4 1.9 %collective-permute-start.5 = (f32[520,256]{1,0:T(8,128)S(1)}, f32[520,256]{1,0:T(8,128)S(1)}, u32[]{:S(2)}, u32[]{:S(2)}) collective-permute-start(f32[520,256]{1,0:T(8,128)S(1)} %shard_map.97.mine), channel_id=1, source_target_pairs={{0,8},{8,0},{16,24},{24,16},{32,40},{40,32},{48,56},{56,48},{64,72... | collective-permute-start | bytes 1597448 | tf_op jit(solution)/shard_map/ppermute | solution.py:377
  47.4 1.9 %collective-permute-start.7 = (bf16[8,144,256]{2,1,0:T(8,128)(2,1)S(1)}, bf16[8,144,256]{2,1,0:T(8,128)(2,1)S(1)}, u32[]{:S(2)}, u32[]{:S(2)}) collective-permute-start(bf16[8,144,256]{2,1,0:T(8,128)(2,1)S(1)} %shard_map.101), channel_id=1, source_target_pairs={{0,16},{1,17},{2,18},{3,19},{4,20},{5,21},{6,22},{7,23},{8,60},{9,... | collective-permute-start | bytes 1769480 | tf_op jit(solution)/shard_map/ppermute | solution.py:343
  49.5 3.3 %collective-permute-start.8 = (bf16[528,256]{1,0:T(8,128)(2,1)S(1)}, bf16[528,256]{1,0:T(8,128)(2,1)S(1)}, u32[]{:S(2)}, u32[]{:S(2)}) collective-permute-start(bf16[528,256]{1,0:T(8,128)(2,1)S(1)} %shard_map.98.units), channel_id=1, source_target_pairs={{0,1},{1,0},{2,3},{3,2},{4,5},{5,4},{6,7},{7,6},{8,11},{9,10},{10,... | collective-permute-start | bytes 811016 | tf_op jit(solution)/shard_map/ppermute | solution.py:379
  52.8 5.4 %collective-permute-done.8.units = bf16[528,256]{1,0:T(8,128)(2,1)S(1)} collective-permute-done((bf16[528,256]{1,0:T(8,128)(2,1)S(1)}, bf16[528,256]{1,0:T(8,128)(2,1)S(1)}, u32[]{:S(2)}, u32[]{:S(2)}) %collective-permute-start.8) | collective-permute-done | bytes 270368 | tf_op jit(solution)/shard_map/ppermute | solution.py:379
  58.2 0.9 %shard_map.103.refs_0_ = f32[16,256]{1,0:T(8,128)S(1)} custom-call(bf16[528,256]{1,0:T(8,128)(2,1)S(1)} %collective-permute-done.8.units, bf16[8,96,256]{2,1,0:T(8,128)(2,1)S(1)} %all-to-all-done.box.refs_0_.b0, bf16[8,80,256]{2,1,0:T(8,128)(2,1)S(1)} %collective-permute-done.6.refs_1_.two.b2), custom_call_target="tpu_custom_call" | custom-call | flops 1024 | bytes 1024 | tf_op jit(solution)/shard_map/pallas_call | solution.py:63
  59.2 0.9 %shard_map.104 = f32[16,256]{1,0:T(8,128)S(1)} custom-call(bf16[528,256]{1,0:T(8,128)(2,1)S(1)} %collective-permute-done.8.units, f32[16,256]{1,0:T(8,128)S(1)} %shard_map.103.refs_0_, bf16[8,144,256]{2,1,0:T(8,128)(2,1)S(1)} %collective-permute-done.7.refs_1_.b1), custom_call_target="tpu_custom_call" | custom-call | flops 1024 | bytes 1024 | tf_op jit(solution)/shard_map/pallas_call | solution.py:63
  60.1 3.3 %collective-permute-start.9 = (f32[16,256]{1,0:T(8,128)S(1)}, f32[16,256]{1,0:T(8,128)S(1)}, u32[]{:S(2)}, u32[]{:S(2)}) collective-permute-start(f32[16,256]{1,0:T(8,128)S(1)} %shard_map.104), channel_id=1, source_target_pairs={{0,1},{1,0},{2,3},{3,2},{4,5},{5,4},{6,7},{7,6},{8,11},{9,10},{10,... | collective-permute-start | bytes 49160 | tf_op jit(solution)/shard_map/ppermute | solution.py:389
  63.4 0.9 %shard_map.100.refs_0_ = f32[16,256]{1,0:T(8,128)S(1)} custom-call(bf16[528,256]{1,0:T(8,128)(2,1)S(1)} %shard_map.98.units, bf16[8,96,256]{2,1,0:T(8,128)(2,1)S(1)} %all-to-all-done.box.refs_0_.b0, bf16[8,80,256]{2,1,0:T(8,128)(2,1)S(1)} %collective-permute-done.6.refs_1_.two.b2), custom_call_target="tpu_custom_call" | custom-call | flops 1024 | bytes 1024 | tf_op jit(solution)/shard_map/pallas_call | solution.py:63
  64.5 0.9 %shard_map.102.state = f32[16,256]{1,0:T(8,128)S(1)} custom-call(bf16[528,256]{1,0:T(8,128)(2,1)S(1)} %shard_map.98.units, f32[16,256]{1,0:T(8,128)S(1)} %shard_map.100.refs_0_, bf16[8,144,256]{2,1,0:T(8,128)(2,1)S(1)} %collective-permute-done.7.refs_1_.b1), custom_call_target="tpu_custom_call" | custom-call | flops 1024 | bytes 1024 | tf_op jit(solution)/shard_map/pallas_call | solution.py:63
  65.8 5.4 %collective-permute-start.10 = (f32[136,256]{1,0:T(8,128)S(1)}, f32[136,256]{1,0:T(8,128)S(1)}, u32[]{:S(2)}, u32[]{:S(2)}) collective-permute-start(f32[136,256]{1,0:T(8,128)S(1)} %get-tuple-element.18), channel_id=1, source_target_pairs={{0,8},{8,0},{16,24},{24,16},{32,40},{40,32},{48,56},{56,48},{64,72... | collective-permute-start | bytes 417800 | tf_op jit(solution)/shard_map/ppermute | solution.py:398
  71.2 1.0 %collective-permute-done.10.got = f32[136,256]{1,0:T(8,128)S(1)} collective-permute-done((f32[136,256]{1,0:T(8,128)S(1)}, f32[136,256]{1,0:T(8,128)S(1)}, u32[]{:S(2)}, u32[]{:S(2)}) %collective-permute-start.10) | collective-permute-done | bytes 139296 | tf_op jit(solution)/shard_map/ppermute | solution.py:398
  72.2 1.0 %shard_map.107 = (f32[1,256]{1,0:T(1,128)}, bf16[128,256]{1,0:T(8,128)(2,1)}) custom-call(f32[8,256]{1,0:T(8,128)S(1)} %get-tuple-element.17.keep, f32[136,256]{1,0:T(8,128)S(1)} %collective-permute-done.10.got, f32[128,256]{1,0:T(8,128)S(1)} %get-tuple-element.19.mine, bf16[128,256]{1,0:T(8,128)(2,1)S(1)} %copy-done.1), custom_call_target="tpu_custom_call" | custom-call | flops 1024 | bytes 1024 | tf_op jit(solution)/shard_map/pallas_call | solution.py:63
  (21 shorter events, 1.7 us)
Async XLA Ops:
  0.6 19.1 %copy-start = (bf16[256,1024]{1,0:T(8,128)(2,1)S(1)}, bf16[256,1024]{1,0:T(8,128)(2,1)}, u32[]{:S(2)}) copy-start(bf16[256,1024]{1,0:T(8,128)(2,1)} %q_own.1) | copy-start | bytes 1572868
  2.8 20.1 %collective-permute-start.1 = (bf16[160,512]{1,0:T(8,128)(2,1)}, bf16[160,512]{1,0:T(8,128)(2,1)S(1)}, u32[]{:S(2)}, u32[]{:S(2)}) collective-permute-start(bf16[160,512]{1,0:T(8,128)(2,1)} %get-tuple-element.14.own), channel_id=1, source_target_pairs={{0,36},{1,37},{2,38},{3,39},{4,32},{5,33},{6,34},{7,35},{8,44},{9,... | collective-permute-start | bytes 491528 | tf_op jit(solution)/shard_map/ppermute | solution.py:343
  9.5 13.4 %copy-start.3 = (bf16[160,512]{1,0:T(8,128)(2,1)S(1)}, bf16[160,512]{1,0:T(8,128)(2,1)}, u32[]{:S(2)}) copy-start(bf16[160,512]{1,0:T(8,128)(2,1)} %get-tuple-element.14.own) | copy-start | bytes 491524
  9.5 23.6 %all-to-all-start = ((bf16[8,96,256]{2,1,0:T(8,128)(2,1)}), bf16[8,96,256]{2,1,0:T(8,128)(2,1)S(1)}, u32[]{:S(2)}, u32[]{:S(2)}) async-start(bf16[8,96,256]{2,1,0:T(8,128)(2,1)} %get-tuple-element.12), calls=%async_computation | async-start | bytes 786432 | tf_op jit(solution)/shard_map/all_to_all | solution.py:361
  19.7 16.2 %collective-permute-start = (bf16[256,1024]{1,0:T(8,128)(2,1)S(1)}, bf16[256,1024]{1,0:T(8,128)(2,1)S(1)}, u32[]{:S(2)}, u32[]{:S(2)}) collective-permute-start(bf16[256,1024]{1,0:T(8,128)(2,1)S(1)} %copy-done), channel_id=1, source_target_pairs={{0,8},{8,0},{16,24},{24,16},{32,40},{40,32},{48,56},{56,48},{64,72... | collective-permute-start | bytes 1572872 | tf_op jit(solution)/shard_map/ppermute | solution.py:363
  22.9 15.9 %collective-permute-start.2 = (bf16[320,512]{1,0:T(8,128)(2,1)S(1)}, bf16[320,512]{1,0:T(8,128)(2,1)S(1)}, u32[]{:S(2)}, u32[]{:S(2)}) collective-permute-start(bf16[320,512]{1,0:T(8,128)(2,1)S(1)} %shard_map.96.w0), channel_id=1, source_target_pairs={{0,1},{1,2},{2,3},{3,0},{4,5},{5,6},{6,7},{7,4},{8,11},{9,8},{10,9... | collective-permute-start | bytes 983048 | tf_op jit(solution)/shard_map/ppermute | solution.py:340
  27.3 13.2 %collective-permute-start.3 = (bf16[320,512]{1,0:T(8,128)(2,1)S(1)}, bf16[320,512]{1,0:T(8,128)(2,1)S(1)}, u32[]{:S(2)}, u32[]{:S(2)}) collective-permute-start(bf16[320,512]{1,0:T(8,128)(2,1)S(1)} %shard_map.96.w0), channel_id=1, source_target_pairs={{0,2},{1,3},{2,0},{3,1},{4,6},{5,7},{6,4},{7,5},{8,10},{9,11},{10,... | collective-permute-start | bytes 983048 | tf_op jit(solution)/shard_map/ppermute | solution.py:340
  29.8 14.5 %collective-permute-start.4 = (bf16[320,512]{1,0:T(8,128)(2,1)S(1)}, bf16[320,512]{1,0:T(8,128)(2,1)S(1)}, u32[]{:S(2)}, u32[]{:S(2)}) collective-permute-start(bf16[320,512]{1,0:T(8,128)(2,1)S(1)} %shard_map.96.w0), channel_id=1, source_target_pairs={{0,3},{1,0},{2,1},{3,2},{4,7},{5,4},{6,5},{7,6},{8,9},{9,10},{10,1... | collective-permute-start | bytes 983048 | tf_op jit(solution)/shard_map/ppermute | solution.py:340
  33.1 11.1 %copy-start.2 = (s32[256]{0:T(256)S(1)}, s32[256]{0:T(256)}, u32[]{:S(2)}) copy-start(s32[256]{0:T(256)} %param.12) | copy-start | bytes 3076
  33.1 14.2 %collective-permute-start.6 = (bf16[8,80,256]{2,1,0:T(8,128)(2,1)S(1)}, bf16[8,80,256]{2,1,0:T(8,128)(2,1)S(1)}, u32[]{:S(2)}, u32[]{:S(2)}) collective-permute-start(bf16[8,80,256]{2,1,0:T(8,128)(2,1)S(1)} %shard_map.99), channel_id=1, source_target_pairs={{0,32},{1,33},{2,34},{3,35},{4,36},{5,37},{6,38},{7,39},{8,44},{9,... | collective-permute-start | bytes 983048 | tf_op jit(solution)/shard_map/ppermute | solution.py:343
  45.4 3.9 %collective-permute-start.5 = (f32[520,256]{1,0:T(8,128)S(1)}, f32[520,256]{1,0:T(8,128)S(1)}, u32[]{:S(2)}, u32[]{:S(2)}) collective-permute-start(f32[520,256]{1,0:T(8,128)S(1)} %shard_map.97.mine), channel_id=1, source_target_pairs={{0,8},{8,0},{16,24},{24,16},{32,40},{40,32},{48,56},{56,48},{64,72... | collective-permute-start | bytes 1597448 | tf_op jit(solution)/shard_map/ppermute | solution.py:377
  47.4 11.8 %collective-permute-start.7 = (bf16[8,144,256]{2,1,0:T(8,128)(2,1)S(1)}, bf16[8,144,256]{2,1,0:T(8,128)(2,1)S(1)}, u32[]{:S(2)}, u32[]{:S(2)}) collective-permute-start(bf16[8,144,256]{2,1,0:T(8,128)(2,1)S(1)} %shard_map.101), channel_id=1, source_target_pairs={{0,16},{1,17},{2,18},{3,19},{4,20},{5,21},{6,22},{7,23},{8,60},{9,... | collective-permute-start | bytes 1769480 | tf_op jit(solution)/shard_map/ppermute | solution.py:343
  49.5 8.7 %collective-permute-start.8 = (bf16[528,256]{1,0:T(8,128)(2,1)S(1)}, bf16[528,256]{1,0:T(8,128)(2,1)S(1)}, u32[]{:S(2)}, u32[]{:S(2)}) collective-permute-start(bf16[528,256]{1,0:T(8,128)(2,1)S(1)} %shard_map.98.units), channel_id=1, source_target_pairs={{0,1},{1,0},{2,3},{3,2},{4,5},{5,4},{6,7},{7,6},{8,11},{9,10},{10,... | collective-permute-start | bytes 811016 | tf_op jit(solution)/shard_map/ppermute | solution.py:379
  60.1 5.7 %collective-permute-start.9 = (f32[16,256]{1,0:T(8,128)S(1)}, f32[16,256]{1,0:T(8,128)S(1)}, u32[]{:S(2)}, u32[]{:S(2)}) collective-permute-start(f32[16,256]{1,0:T(8,128)S(1)} %shard_map.104), channel_id=1, source_target_pairs={{0,1},{1,0},{2,3},{3,2},{4,5},{5,4},{6,7},{7,6},{8,11},{9,10},{10,... | collective-permute-start | bytes 49160 | tf_op jit(solution)/shard_map/ppermute | solution.py:389
  65.8 6.4 %copy-start.1 = (bf16[128,256]{1,0:T(8,128)(2,1)S(1)}, bf16[128,256]{1,0:T(8,128)(2,1)}, u32[]{:S(2)}) copy-start(bf16[128,256]{1,0:T(8,128)(2,1)} %bank.1) | copy-start | bytes 196612
  65.8 6.4 %collective-permute-start.10 = (f32[136,256]{1,0:T(8,128)S(1)}, f32[136,256]{1,0:T(8,128)S(1)}, u32[]{:S(2)}, u32[]{:S(2)}) collective-permute-start(f32[136,256]{1,0:T(8,128)S(1)} %get-tuple-element.18), channel_id=1, source_target_pairs={{0,8},{8,0},{16,24},{24,16},{32,40},{40,32},{48,56},{56,48},{64,72... | collective-permute-start | bytes 417800 | tf_op jit(solution)/shard_map/ppermute | solution.py:398

commit v6 on v5

--- a/solution.py
+++ b/solution.py
@@ -16,6 +16,8 @@
 X = 4
 Y_LO = 4
 Y = 8
+
+TILE = 8
 
 VMEM = pltpu.VMEM
 LIMIT = 48 * 1024 * 1024
@@ -82,10 +84,10 @@
         pltpu.make_async_copy(a, b, sems.at[i])
         for i, (a, b) in enumerate(
             (
-                (bank_in.at[pl.ds(at, part)], bank),
                 (owners_in, owners),
                 (slots_in, slots),
                 (fresh_in, fresh),
+                (bank_in.at[pl.ds(at, part)], bank),
                 (w_input_in, w_input),
                 (w_output_in, w_output),
             )
@@ -93,7 +95,7 @@
     ]
     for copy in loads:
         copy.start()
-    for copy in loads[1:4]:
+    for copy in loads[:3]:
         copy.wait()
     count = fresh.shape[0]
     owner = owners[...].astype(F32)
@@ -102,15 +104,24 @@
     same = across == across.T
     placed = jnp.sum(jnp.where(same & earlier, 1.0, 0.0), axis=0, keepdims=True)
     key = (owner * 2.0 + placed).astype(I32)
-    row = lax.broadcasted_iota(I32, (ring * Y_LO * 8, count), 0)
-    wanted = (row // 8) * 4 + (row % 4)
-    chosen = wanted == key
+    rows = out.shape[1] - part
+    line = lax.broadcasted_iota(I32, (ring * rows, count), 0)
+    inner = line % rows
+    base = (line // rows) * (Y_LO * 4)
+    left = base + jnp.where(inner < 16, inner, 2 * (inner - 16))
+    chosen = left == key
     data = jnp.dot(chosen.astype(BF16), fresh[...], preferred_element_type=F32)
-    slot = jnp.sum(jnp.where(chosen, slots[...].astype(F32) + 1.0, 0.0), axis=1, keepdims=True) - 1.0
-    kind = lax.broadcasted_iota(I32, data.shape, 0) % 8
-    both = jnp.where(kind < 4, data, slot).astype(BF16)
-    out[:, part:, :] = both.reshape(ring, Y_LO * 8, both.shape[1])
-    loads[0].wait()
+    after = slots[...].astype(F32) + 1.0
+    pair = [
+        jnp.sum(jnp.where(hit, after, 0.0), axis=1, keepdims=True) - 1.0
+        for hit in (chosen, left + 1 == key)
+    ]
+    kind = lax.broadcasted_iota(I32, data.shape, 0) % rows
+    lane = lax.broadcasted_iota(I32, data.shape, 1)
+    slot = jnp.where(lane < data.shape[1] // 2, pair[0], pair[1])
+    both = jnp.where(kind < 16, data, slot).astype(BF16)
+    out[:, part:, :] = both.reshape(ring, rows, both.shape[1])
+    loads[3].wait()
     for z in range(ring):
         out[z, :part, :] = bank[...]
     for copy in loads[4:]:
@@ -170,11 +181,19 @@
 
 
 def pick(box, part, which):
-    rows = [box[:, part + 8 * j : part + 8 * (j + 1), :] for j in range(Y_LO)]
-    out = rows[0]
+    half = box.shape[2] // 2
+    rows = [box[:, part + 4 * j : part + 4 * (j + 1), :].astype(F32) for j in range(Y_LO)]
+    slots = [box[:, part + 16 + 2 * j : part + 18 + 2 * j, :].astype(F32) for j in range(Y_LO)]
+    row, slot = rows[0], slots[0]
     for j in range(1, Y_LO):
-        out = jnp.where(which == j, rows[j], out)
-    return out
+        row = jnp.where(which == j, rows[j], row)
+        slot = jnp.where(which == j, slots[j], slot)
+    wide = [
+        jnp.concatenate([slot[:, m : m + 1, side * half : (side + 1) * half]] * 2, axis=2)
+        for m in range(2)
+        for side in range(2)
+    ]
+    return jnp.concatenate([row, *wide], axis=1).astype(BF16)
 
 
 def two_kernel(box, out):
@@ -221,8 +240,8 @@
         boxes += [(1, refs[-2], 0), (3, refs[-2], part)]
     scale = 16.0 * math.log2(math.e)
     local = ring * part
-    number = lax.broadcasted_iota(I32, (local, count), 0)
-    line = lax.broadcasted_iota(I32, (8, count), 0)
+    lane = 8
+    line = lax.broadcasted_iota(I32, (lane, count), 0)
     tail = units[CORES * count :, :].astype(F32)
     for i in range(CORES):
         unit = units[i * count : (i + 1) * count, :]
@@ -231,24 +250,33 @@
         chip = block // CORES
         away = (y_lo - chip % Y_LO + Y_LO) % Y_LO
         at = (chip // Y_LO) * part + row % part
-        at = jnp.where((block % CORES == core) & (row // part == half), at, -1)
-        top = total = picked = None
-        if old is not None:
-            top, total, picked = (old[8 * i + k : 8 * i + k + 1, :] for k in range(3))
+        at = jnp.where((block % CORES == core) & (row // part == half), at, -local)
+        high = total = None
+        picked = jnp.zeros((lane, count), F32)
         for delta, box, base in boxes:
             bank = box[:, base : base + part, :].reshape(local, box.shape[2])
             d = lax.dot_general(bank, unit, (((1,), (1,)), ((), ())), preferred_element_type=F32)
-            high = jnp.max(d, axis=0, keepdims=True)
-            hit = number == jnp.where(away == away_of(delta), at, -1)
-            here = jnp.sum(jnp.where(hit, d, 0.0), axis=0, keepdims=True)
-            if top is None:
-                top, picked = high, here
-                total = jnp.sum(jnp.exp2((d - top) * scale), axis=0, keepdims=True)
-            else:
-                before, top = top, jnp.maximum(top, high)
-                total = total * jnp.exp2((before - top) * scale)
-                total += jnp.sum(jnp.exp2((d - top) * scale), axis=0, keepdims=True)
-                picked += here
+            d = d.reshape(local // lane, lane, count)
+            apart = jnp.where(away == away_of(delta), at, -local) - line
+            for first in range(0, local // lane, TILE):
+                tile = [d[j] for j in range(first, first + TILE)]
+                top = functools.reduce(jnp.maximum, tile)
+                if high is not None:
+                    top = jnp.maximum(top, high)
+                here = sum(jnp.exp2((t - top) * scale) for t in tile)
+                total = here if high is None else total * jnp.exp2((high - top) * scale) + here
+                high = top
+                for j, t in enumerate(tile, first):
+                    picked += jnp.where(apart == j * lane, t, 0.0)
+        top = jnp.max(high, axis=0, keepdims=True)
+        if old is not None:
+            top = jnp.maximum(top, old[8 * i : 8 * i + 1, :])
+        total = jnp.sum(total * jnp.exp2((high - top) * scale), axis=0, keepdims=True)
+        picked = jnp.sum(picked, axis=0, keepdims=True)
+        if old is not None:
+            before, so_far, found = (old[8 * i + k : 8 * i + k + 1, :] for k in range(3))
+            total += so_far * jnp.exp2((before - top) * scale)
+            picked += found
         out[8 * i : 8 * i + 8, :] = jnp.where(
             line == 0, top, jnp.where(line == 1, total, jnp.where(line == 2, picked, 0.0))
         )
@@ -344,7 +372,7 @@
 
     w_mine, box_send = call(
         first_kernel,
-        (sds((tall, half), BF16), sds((ring, part + Y_LO * 8, width), BF16)),
+        (sds((tall, half), BF16), sds((ring, part + Y_LO * 6, width), BF16)),
         (w_input, w_output, owners.reshape(1, -1), slots.reshape(1, -1), fresh_rows, item_bank),
         [
             VMEM(w_input.shape, BF16),

time: 73.7 us -> 73.1 us (level)
  starting transfers between devices: 47.9 us -> 46.9 us
    ppermute x3, waiting for transfers between devices: 8.34 us -> 9.54 us  [around(): return lax.ppermute(a, ('bank', 'dp'), pairs)]
    all_to_all x1, waiting for transfers between devices: 0.81 us -> 0.01 us  [body(): lax.all_to_all(box_send, 'bank', 0, 0, axis_index_groups=columns, tiled=T...]
  transfers between devices with their start and end apart: 12 -> 12, of which waited for: 7 -> 6; matrix products, arithmetic and copies ran while one was open for 0% -> 0% of each run, Pallas kernels for 6% -> 6%
where the time goes in v6:
time: 73.1 us; the launch traced here: 72.5 us
  starting transfers between devices  46.9 us (64%)
  waiting for transfers between devices  16.5 us (23%)
  Pallas kernels  8.23 us (11%)
  between operations  0.87 us (1%)
    ppermute x3, starting transfers between devices, move_y(): return lax.ppermute(a, ('bank', 'dp'), along_y(devices, members, to))  10.9 us
    all_to_all x1, starting transfers between devices, body(): lax.all_to_all(box_send, 'bank', 0, 0, axis_index_groups=columns, tiled=T...  10.2 us
    ppermute x3, waiting for transfers between devices, around(): return lax.ppermute(a, ('bank', 'dp'), pairs)  9.54 us
    ppermute x3, starting transfers between devices, around(): return lax.ppermute(a, ('bank', 'dp'), pairs)  9.33 us
    pallas_call x13, Pallas kernels, call(): pl.pallas_call(kernel, out_shape=outs, in_specs=[pl.BlockSpec(memory_spac...  8.23 us
    ppermute x1, waiting for transfers between devices, body(): partners = lax.ppermute(units, ('bank', 'dp'), to_partner(devices, members))  5.39 us
    ppermute x1, starting transfers between devices, body(): got = lax.ppermute(send, 'bank', swap)  4.87 us
    ppermute x1, starting transfers between devices, body(): partners = lax.ppermute(units, ('bank', 'dp'), to_partner(devices, members))  3.31 us
  transfers between devices with their start and end apart: 12, of which 6 were waited for; matrix products, arithmetic and copies ran while one was open for 0% of the time, Pallas kernels for 6%

profile of v6, /device:TPU:1, one launch (start us, length us, event | category | flops | bytes accessed | tf_op | source)
XLA Modules:
  0.0 72.5 jit_solution(12073645513797501246)
XLA Ops:
  0.6 2.1 %shard_map.95 = (bf16[160,512]{1,0:T(8,128)(2,1)}, bf16[8,88,256]{2,1,0:T(8,128)(2,1)}) custom-call(bf16[128,1024]{1,0:T(8,128)(2,1)} %w_input_in.1, bf16[128,256]{1,0:T(8,128)(2,1)} %w_output_in.1, s32[1,64]{1,0:T(1,128)} %bitcast.5, s32[1,64]{1,0:T(1,128)} %bitcast.6, bf16[64,256]{1,0:T(8,128)(2,1)} %fresh_in.1, bf16[128,256]{1,0:T(8,128)(2,1)} %bank.1), custom_call_target="tpu_custom_call" | custom-call | flops 1024 | bytes 1024 | tf_op jit(solution)/shard_map/pallas_call | solution.py:65
  2.8 6.7 %collective-permute-start.1 = (bf16[160,512]{1,0:T(8,128)(2,1)}, bf16[160,512]{1,0:T(8,128)(2,1)S(1)}, u32[]{:S(2)}, u32[]{:S(2)}) collective-permute-start(bf16[160,512]{1,0:T(8,128)(2,1)} %get-tuple-element.14.own), channel_id=1, source_target_pairs={{0,36},{1,37},{2,38},{3,39},{4,32},{5,33},{6,34},{7,35},{8,44},{9,... | collective-permute-start | bytes 491528 | tf_op jit(solution)/shard_map/ppermute | solution.py:371
  9.5 10.2 %all-to-all-start = ((bf16[8,88,256]{2,1,0:T(8,128)(2,1)}), bf16[8,88,256]{2,1,0:T(8,128)(2,1)S(1)}, u32[]{:S(2)}, u32[]{:S(2)}) async-start(bf16[8,88,256]{2,1,0:T(8,128)(2,1)} %get-tuple-element.12), calls=%async_computation | async-start | bytes 720896 | tf_op jit(solution)/shard_map/all_to_all | solution.py:389
  19.7 3.1 %collective-permute-start = (bf16[256,1024]{1,0:T(8,128)(2,1)S(1)}, bf16[256,1024]{1,0:T(8,128)(2,1)S(1)}, u32[]{:S(2)}, u32[]{:S(2)}) collective-permute-start(bf16[256,1024]{1,0:T(8,128)(2,1)S(1)} %copy-done), channel_id=1, source_target_pairs={{0,8},{8,0},{16,24},{24,16},{32,40},{40,32},{48,56},{56,48},{64,72... | collective-permute-start | bytes 1572872 | tf_op jit(solution)/shard_map/ppermute | solution.py:391
  22.9 4.4 %collective-permute-start.2 = (bf16[320,512]{1,0:T(8,128)(2,1)S(1)}, bf16[320,512]{1,0:T(8,128)(2,1)S(1)}, u32[]{:S(2)}, u32[]{:S(2)}) collective-permute-start(bf16[320,512]{1,0:T(8,128)(2,1)S(1)} %shard_map.96.w0), channel_id=1, source_target_pairs={{0,1},{1,2},{2,3},{3,0},{4,5},{5,6},{6,7},{7,4},{8,11},{9,8},{10,9... | collective-permute-start | bytes 983048 | tf_op jit(solution)/shard_map/ppermute | solution.py:368
  27.3 2.4 %collective-permute-start.3 = (bf16[320,512]{1,0:T(8,128)(2,1)S(1)}, bf16[320,512]{1,0:T(8,128)(2,1)S(1)}, u32[]{:S(2)}, u32[]{:S(2)}) collective-permute-start(bf16[320,512]{1,0:T(8,128)(2,1)S(1)} %shard_map.96.w0), channel_id=1, source_target_pairs={{0,2},{1,3},{2,0},{3,1},{4,6},{5,7},{6,4},{7,5},{8,10},{9,11},{10,... | collective-permute-start | bytes 983048 | tf_op jit(solution)/shard_map/ppermute | solution.py:368
  29.7 2.5 %collective-permute-start.4 = (bf16[320,512]{1,0:T(8,128)(2,1)S(1)}, bf16[320,512]{1,0:T(8,128)(2,1)S(1)}, u32[]{:S(2)}, u32[]{:S(2)}) collective-permute-start(bf16[320,512]{1,0:T(8,128)(2,1)S(1)} %shard_map.96.w0), channel_id=1, source_target_pairs={{0,3},{1,0},{2,1},{3,2},{4,7},{5,4},{6,5},{7,6},{8,9},{9,10},{10,1... | collective-permute-start | bytes 983048 | tf_op jit(solution)/shard_map/ppermute | solution.py:368
  32.4 2.2 %collective-permute-start.6 = (bf16[8,80,256]{2,1,0:T(8,128)(2,1)S(1)}, bf16[8,80,256]{2,1,0:T(8,128)(2,1)S(1)}, u32[]{:S(2)}, u32[]{:S(2)}) collective-permute-start(bf16[8,80,256]{2,1,0:T(8,128)(2,1)S(1)} %shard_map.99), channel_id=1, source_target_pairs={{0,32},{1,33},{2,34},{3,35},{4,36},{5,37},{6,38},{7,39},{8,44},{9,... | collective-permute-start | bytes 983048 | tf_op jit(solution)/shard_map/ppermute | solution.py:371
  34.6 4.1 %collective-permute-done.2.w1 = bf16[320,512]{1,0:T(8,128)(2,1)S(1)} collective-permute-done((bf16[320,512]{1,0:T(8,128)(2,1)S(1)}, bf16[320,512]{1,0:T(8,128)(2,1)S(1)}, u32[]{:S(2)}, u32[]{:S(2)}) %collective-permute-start.2) | collective-permute-done | bytes 327712 | tf_op jit(solution)/shard_map/ppermute | solution.py:368
  38.7 1.8 %collective-permute-done.3.w2 = bf16[320,512]{1,0:T(8,128)(2,1)S(1)} collective-permute-done((bf16[320,512]{1,0:T(8,128)(2,1)S(1)}, bf16[320,512]{1,0:T(8,128)(2,1)S(1)}, u32[]{:S(2)}, u32[]{:S(2)}) %collective-permute-start.3) | collective-permute-done | bytes 327712 | tf_op jit(solution)/shard_map/ppermute | solution.py:368
  40.5 3.7 %collective-permute-done.4.w3 = bf16[320,512]{1,0:T(8,128)(2,1)S(1)} collective-permute-done((bf16[320,512]{1,0:T(8,128)(2,1)S(1)}, bf16[320,512]{1,0:T(8,128)(2,1)S(1)}, u32[]{:S(2)}, u32[]{:S(2)}) %collective-permute-start.4) | collective-permute-done | bytes 327712 | tf_op jit(solution)/shard_map/ppermute | solution.py:368
  44.2 1.1 %shard_map.97.mine = f32[520,256]{1,0:T(8,128)S(1)} custom-call(bf16[256,1024]{1,0:T(8,128)(2,1)S(1)} %copy-done, bf16[256,1024]{1,0:T(8,128)(2,1)S(1)} %collective-permute-done.q_other, bf16[320,512]{1,0:T(8,128)(2,1)S(1)} %shard_map.96.w0, bf16[320,512]{1,0:T(8,128)(2,1)S(1)} %collective-permute-done.2.w1, bf16[320,512]{1,0:T(8,128)(2,1)S(1)} %collective-permute-done.3.w2, ...), custom_call_target="tpu_custom_call" | custom-call | flops 1024 | bytes 1024 | tf_op jit(solution)/shard_map/pallas_call | solution.py:65
  45.3 1.9 %collective-permute-start.5 = (f32[520,256]{1,0:T(8,128)S(1)}, f32[520,256]{1,0:T(8,128)S(1)}, u32[]{:S(2)}, u32[]{:S(2)}) collective-permute-start(f32[520,256]{1,0:T(8,128)S(1)} %shard_map.97.mine), channel_id=1, source_target_pairs={{0,8},{8,0},{16,24},{24,16},{32,40},{40,32},{48,56},{56,48},{64,72... | collective-permute-start | bytes 1597448 | tf_op jit(solution)/shard_map/ppermute | solution.py:405
  47.4 1.9 %collective-permute-start.7 = (bf16[8,144,256]{2,1,0:T(8,128)(2,1)S(1)}, bf16[8,144,256]{2,1,0:T(8,128)(2,1)S(1)}, u32[]{:S(2)}, u32[]{:S(2)}) collective-permute-start(bf16[8,144,256]{2,1,0:T(8,128)(2,1)S(1)} %shard_map.101), channel_id=1, source_target_pairs={{0,16},{1,17},{2,18},{3,19},{4,20},{5,21},{6,22},{7,23},{8,60},{9,... | collective-permute-start | bytes 1769480 | tf_op jit(solution)/shard_map/ppermute | solution.py:371
  49.5 3.3 %collective-permute-start.8 = (bf16[528,256]{1,0:T(8,128)(2,1)S(1)}, bf16[528,256]{1,0:T(8,128)(2,1)S(1)}, u32[]{:S(2)}, u32[]{:S(2)}) collective-permute-start(bf16[528,256]{1,0:T(8,128)(2,1)S(1)} %shard_map.98.units), channel_id=1, source_target_pairs={{0,1},{1,0},{2,3},{3,2},{4,5},{5,4},{6,7},{7,6},{8,11},{9,10},{10,... | collective-permute-start | bytes 811016 | tf_op jit(solution)/shard_map/ppermute | solution.py:407
  52.8 5.4 %collective-permute-done.8.units = bf16[528,256]{1,0:T(8,128)(2,1)S(1)} collective-permute-done((bf16[528,256]{1,0:T(8,128)(2,1)S(1)}, bf16[528,256]{1,0:T(8,128)(2,1)S(1)}, u32[]{:S(2)}, u32[]{:S(2)}) %collective-permute-start.8) | collective-permute-done | bytes 270368 | tf_op jit(solution)/shard_map/ppermute | solution.py:407
  58.2 0.8 %shard_map.103.refs_0_ = f32[16,256]{1,0:T(8,128)S(1)} custom-call(bf16[528,256]{1,0:T(8,128)(2,1)S(1)} %collective-permute-done.8.units, bf16[8,88,256]{2,1,0:T(8,128)(2,1)S(1)} %all-to-all-done.box.refs_0_.b0, bf16[8,80,256]{2,1,0:T(8,128)(2,1)S(1)} %collective-permute-done.6.refs_1_.two.b2), custom_call_target="tpu_custom_call" | custom-call | flops 1024 | bytes 1024 | tf_op jit(solution)/shard_map/pallas_call | solution.py:65
  59.1 0.8 %shard_map.104 = f32[16,256]{1,0:T(8,128)S(1)} custom-call(bf16[528,256]{1,0:T(8,128)(2,1)S(1)} %collective-permute-done.8.units, f32[16,256]{1,0:T(8,128)S(1)} %shard_map.103.refs_0_, bf16[8,144,256]{2,1,0:T(8,128)(2,1)S(1)} %collective-permute-done.7.refs_1_.b1), custom_call_target="tpu_custom_call" | custom-call | flops 1024 | bytes 1024 | tf_op jit(solution)/shard_map/pallas_call | solution.py:65
  59.9 3.3 %collective-permute-start.9 = (f32[16,256]{1,0:T(8,128)S(1)}, f32[16,256]{1,0:T(8,128)S(1)}, u32[]{:S(2)}, u32[]{:S(2)}) collective-permute-start(f32[16,256]{1,0:T(8,128)S(1)} %shard_map.104), channel_id=1, source_target_pairs={{0,1},{1,0},{2,3},{3,2},{4,5},{5,4},{6,7},{7,6},{8,11},{9,10},{10,... | collective-permute-start | bytes 49160 | tf_op jit(solution)/shard_map/ppermute | solution.py:417
  63.2 0.8 %shard_map.100.refs_0_ = f32[16,256]{1,0:T(8,128)S(1)} custom-call(bf16[528,256]{1,0:T(8,128)(2,1)S(1)} %shard_map.98.units, bf16[8,88,256]{2,1,0:T(8,128)(2,1)S(1)} %all-to-all-done.box.refs_0_.b0, bf16[8,80,256]{2,1,0:T(8,128)(2,1)S(1)} %collective-permute-done.6.refs_1_.two.b2), custom_call_target="tpu_custom_call" | custom-call | flops 1024 | bytes 1024 | tf_op jit(solution)/shard_map/pallas_call | solution.py:65
  64.2 0.8 %shard_map.102.state = f32[16,256]{1,0:T(8,128)S(1)} custom-call(bf16[528,256]{1,0:T(8,128)(2,1)S(1)} %shard_map.98.units, f32[16,256]{1,0:T(8,128)S(1)} %shard_map.100.refs_0_, bf16[8,144,256]{2,1,0:T(8,128)(2,1)S(1)} %collective-permute-done.7.refs_1_.b1), custom_call_target="tpu_custom_call" | custom-call | flops 1024 | bytes 1024 | tf_op jit(solution)/shard_map/pallas_call | solution.py:65
  65.6 4.9 %collective-permute-start.10 = (f32[136,256]{1,0:T(8,128)S(1)}, f32[136,256]{1,0:T(8,128)S(1)}, u32[]{:S(2)}, u32[]{:S(2)}) collective-permute-start(f32[136,256]{1,0:T(8,128)S(1)} %get-tuple-element.18), channel_id=1, source_target_pairs={{0,8},{8,0},{16,24},{24,16},{32,40},{40,32},{48,56},{56,48},{64,72... | collective-permute-start | bytes 417800 | tf_op jit(solution)/shard_map/ppermute | solution.py:426
  70.5 1.0 %collective-permute-done.10.got = f32[136,256]{1,0:T(8,128)S(1)} collective-permute-done((f32[136,256]{1,0:T(8,128)S(1)}, f32[136,256]{1,0:T(8,128)S(1)}, u32[]{:S(2)}, u32[]{:S(2)}) %collective-permute-start.10) | collective-permute-done | bytes 139296 | tf_op jit(solution)/shard_map/ppermute | solution.py:426
  71.5 1.0 %shard_map.107 = (f32[1,256]{1,0:T(1,128)}, bf16[128,256]{1,0:T(8,128)(2,1)}) custom-call(f32[8,256]{1,0:T(8,128)S(1)} %get-tuple-element.17.keep, f32[136,256]{1,0:T(8,128)S(1)} %collective-permute-done.10.got, f32[128,256]{1,0:T(8,128)S(1)} %get-tuple-element.19.mine, bf16[128,256]{1,0:T(8,128)(2,1)S(1)} %copy-done.1), custom_call_target="tpu_custom_call" | custom-call | flops 1024 | bytes 1024 | tf_op jit(solution)/shard_map/pallas_call | solution.py:65
  (21 shorter events, 1.2 us)
Async XLA Ops:
  0.6 19.0 %copy-start = (bf16[256,1024]{1,0:T(8,128)(2,1)S(1)}, bf16[256,1024]{1,0:T(8,128)(2,1)}, u32[]{:S(2)}) copy-start(bf16[256,1024]{1,0:T(8,128)(2,1)} %q_own.1) | copy-start | bytes 1572868
  2.8 20.1 %collective-permute-start.1 = (bf16[160,512]{1,0:T(8,128)(2,1)}, bf16[160,512]{1,0:T(8,128)(2,1)S(1)}, u32[]{:S(2)}, u32[]{:S(2)}) collective-permute-start(bf16[160,512]{1,0:T(8,128)(2,1)} %get-tuple-element.14.own), channel_id=1, source_target_pairs={{0,36},{1,37},{2,38},{3,39},{4,32},{5,33},{6,34},{7,35},{8,44},{9,... | collective-permute-start | bytes 491528 | tf_op jit(solution)/shard_map/ppermute | solution.py:371
  9.5 13.4 %copy-start.3 = (bf16[160,512]{1,0:T(8,128)(2,1)S(1)}, bf16[160,512]{1,0:T(8,128)(2,1)}, u32[]{:S(2)}) copy-start(bf16[160,512]{1,0:T(8,128)(2,1)} %get-tuple-element.14.own) | copy-start | bytes 491524
  9.5 22.7 %all-to-all-start = ((bf16[8,88,256]{2,1,0:T(8,128)(2,1)}), bf16[8,88,256]{2,1,0:T(8,128)(2,1)S(1)}, u32[]{:S(2)}, u32[]{:S(2)}) async-start(bf16[8,88,256]{2,1,0:T(8,128)(2,1)} %get-tuple-element.12), calls=%async_computation | async-start | bytes 720896 | tf_op jit(solution)/shard_map/all_to_all | solution.py:389
  19.7 15.0 %collective-permute-start = (bf16[256,1024]{1,0:T(8,128)(2,1)S(1)}, bf16[256,1024]{1,0:T(8,128)(2,1)S(1)}, u32[]{:S(2)}, u32[]{:S(2)}) collective-permute-start(bf16[256,1024]{1,0:T(8,128)(2,1)S(1)} %copy-done), channel_id=1, source_target_pairs={{0,8},{8,0},{16,24},{24,16},{32,40},{40,32},{48,56},{56,48},{64,72... | collective-permute-start | bytes 1572872 | tf_op jit(solution)/shard_map/ppermute | solution.py:391
  22.9 15.9 %collective-permute-start.2 = (bf16[320,512]{1,0:T(8,128)(2,1)S(1)}, bf16[320,512]{1,0:T(8,128)(2,1)S(1)}, u32[]{:S(2)}, u32[]{:S(2)}) collective-permute-start(bf16[320,512]{1,0:T(8,128)(2,1)S(1)} %shard_map.96.w0), channel_id=1, source_target_pairs={{0,1},{1,2},{2,3},{3,0},{4,5},{5,6},{6,7},{7,4},{8,11},{9,8},{10,9... | collective-permute-start | bytes 983048 | tf_op jit(solution)/shard_map/ppermute | solution.py:368
  27.3 13.2 %collective-permute-start.3 = (bf16[320,512]{1,0:T(8,128)(2,1)S(1)}, bf16[320,512]{1,0:T(8,128)(2,1)S(1)}, u32[]{:S(2)}, u32[]{:S(2)}) collective-permute-start(bf16[320,512]{1,0:T(8,128)(2,1)S(1)} %shard_map.96.w0), channel_id=1, source_target_pairs={{0,2},{1,3},{2,0},{3,1},{4,6},{5,7},{6,4},{7,5},{8,10},{9,11},{10,... | collective-permute-start | bytes 983048 | tf_op jit(solution)/shard_map/ppermute | solution.py:368
  29.7 14.5 %collective-permute-start.4 = (bf16[320,512]{1,0:T(8,128)(2,1)S(1)}, bf16[320,512]{1,0:T(8,128)(2,1)S(1)}, u32[]{:S(2)}, u32[]{:S(2)}) collective-permute-start(bf16[320,512]{1,0:T(8,128)(2,1)S(1)} %shard_map.96.w0), channel_id=1, source_target_pairs={{0,3},{1,0},{2,1},{3,2},{4,7},{5,4},{6,5},{7,6},{8,9},{9,10},{10,1... | collective-permute-start | bytes 983048 | tf_op jit(solution)/shard_map/ppermute | solution.py:368
  32.4 11.8 %copy-start.2 = (s32[256]{0:T(256)S(1)}, s32[256]{0:T(256)}, u32[]{:S(2)}) copy-start(s32[256]{0:T(256)} %param.12) | copy-start | bytes 3076
  32.4 14.9 %collective-permute-start.6 = (bf16[8,80,256]{2,1,0:T(8,128)(2,1)S(1)}, bf16[8,80,256]{2,1,0:T(8,128)(2,1)S(1)}, u32[]{:S(2)}, u32[]{:S(2)}) collective-permute-start(bf16[8,80,256]{2,1,0:T(8,128)(2,1)S(1)} %shard_map.99), channel_id=1, source_target_pairs={{0,32},{1,33},{2,34},{3,35},{4,36},{5,37},{6,38},{7,39},{8,44},{9,... | collective-permute-start | bytes 983048 | tf_op jit(solution)/shard_map/ppermute | solution.py:371
  45.3 4.0 %collective-permute-start.5 = (f32[520,256]{1,0:T(8,128)S(1)}, f32[520,256]{1,0:T(8,128)S(1)}, u32[]{:S(2)}, u32[]{:S(2)}) collective-permute-start(f32[520,256]{1,0:T(8,128)S(1)} %shard_map.97.mine), channel_id=1, source_target_pairs={{0,8},{8,0},{16,24},{24,16},{32,40},{40,32},{48,56},{56,48},{64,72... | collective-permute-start | bytes 1597448 | tf_op jit(solution)/shard_map/ppermute | solution.py:405
  47.4 11.7 %collective-permute-start.7 = (bf16[8,144,256]{2,1,0:T(8,128)(2,1)S(1)}, bf16[8,144,256]{2,1,0:T(8,128)(2,1)S(1)}, u32[]{:S(2)}, u32[]{:S(2)}) collective-permute-start(bf16[8,144,256]{2,1,0:T(8,128)(2,1)S(1)} %shard_map.101), channel_id=1, source_target_pairs={{0,16},{1,17},{2,18},{3,19},{4,20},{5,21},{6,22},{7,23},{8,60},{9,... | collective-permute-start | bytes 1769480 | tf_op jit(solution)/shard_map/ppermute | solution.py:371
  49.5 8.7 %collective-permute-start.8 = (bf16[528,256]{1,0:T(8,128)(2,1)S(1)}, bf16[528,256]{1,0:T(8,128)(2,1)S(1)}, u32[]{:S(2)}, u32[]{:S(2)}) collective-permute-start(bf16[528,256]{1,0:T(8,128)(2,1)S(1)} %shard_map.98.units), channel_id=1, source_target_pairs={{0,1},{1,0},{2,3},{3,2},{4,5},{5,4},{6,7},{7,6},{8,11},{9,10},{10,... | collective-permute-start | bytes 811016 | tf_op jit(solution)/shard_map/ppermute | solution.py:407
  59.9 5.7 %collective-permute-start.9 = (f32[16,256]{1,0:T(8,128)S(1)}, f32[16,256]{1,0:T(8,128)S(1)}, u32[]{:S(2)}, u32[]{:S(2)}) collective-permute-start(f32[16,256]{1,0:T(8,128)S(1)} %shard_map.104), channel_id=1, source_target_pairs={{0,1},{1,0},{2,3},{3,2},{4,5},{5,4},{6,7},{7,6},{8,11},{9,10},{10,... | collective-permute-start | bytes 49160 | tf_op jit(solution)/shard_map/ppermute | solution.py:417
  65.6 5.9 %copy-start.1 = (bf16[128,256]{1,0:T(8,128)(2,1)S(1)}, bf16[128,256]{1,0:T(8,128)(2,1)}, u32[]{:S(2)}) copy-start(bf16[128,256]{1,0:T(8,128)(2,1)} %bank.1) | copy-start | bytes 196612
  65.6 5.9 %collective-permute-start.10 = (f32[136,256]{1,0:T(8,128)S(1)}, f32[136,256]{1,0:T(8,128)S(1)}, u32[]{:S(2)}, u32[]{:S(2)}) collective-permute-start(f32[136,256]{1,0:T(8,128)S(1)} %get-tuple-element.18), channel_id=1, source_target_pairs={{0,8},{8,0},{16,24},{24,16},{32,40},{40,32},{48,56},{56,48},{64,72... | collective-permute-start | bytes 417800 | tf_op jit(solution)/shard_map/ppermute | solution.py:426
